TPU v7x, 256 devices: a whole 4x4x8 slice. The times are simulated.
256 devices in a mesh: ctx: 32 (over x_lo, z, core), tp: 8 (over x_hi, y).
Axes of the slice: x: 4 (x_hi: 2, x_lo: 2; x = x_hi * 2 + x_lo), y: 4, z: 8, core: 2. Of those that a mesh axis runs over, the one named last changes fastest.
Arguments:
- hidden_in: bfloat16 [16384, 5376], P('ctx', 'tp'), may hold values from -30 to 30
- w_query: bfloat16 [5376, 2048], P(None, 'tp'), may hold values from -0.078125 to 0.078125
- w_key: bfloat16 [5376, 1024], P(None, 'tp'), may hold values from -0.078125 to 0.078125
- w_value: bfloat16 [5376, 1024], P(None, 'tp'), may hold values from -0.078125 to 0.078125
- q_gain: float32 [128], replicated, may hold values from 0.5 to 1.5
- k_gain: float32 [128], replicated, may hold values from 0.5 to 1.5
- grad_out: bfloat16 [16384, 2048], P('ctx', 'tp'), may hold values from -24 to 24
Outputs:
- grad_input: bfloat16 [16384, 5376], P('ctx', 'tp')
- grad_wq: float32 [5376, 2048], P('ctx', 'tp')
- grad_wk: float32 [5376, 1024], P('ctx', 'tp')
- grad_wv: float32 [5376, 1024], P('ctx', 'tp')
All inputs are finite; a program needn't handle non-finite values.
Results may differ from a plain program's by a relative error of at most 0.034.
Values may be sent and summed in bfloat16 or wider, within the bound.
No kernel may reach another device: no remote copies, remote signals or barrier semaphores. Data moves between devices by JAX's collectives and lax.ppermute only.
A program may use at most 128 MiB of HBM per device.

v0:
```python
import functools
import math

import jax
import jax.numpy as jnp
from jax import lax
from jax.experimental import pallas as pl
from jax.experimental.pallas import tpu as pltpu
from jax.sharding import PartitionSpec as P

WINDOW = 1024
HD = 128
HALF = 64
NY, NXH = 4, 2
NXL, NZ, NC = 2, 8, 2

query_scale = 1.0 / math.sqrt(168.0)
rope_base = 10000.0
norm_eps = 1e-06
f32 = jnp.float32
bf16 = jnp.bfloat16
VMEM = pl.BlockSpec(memory_space=pltpu.VMEM)


def tp_perm(dx, dy):
    return [
        (x * NY + y, ((x + dx) % NXH) * NY + (y + dy) % NY)
        for x in range(NXH)
        for y in range(NY)
    ]


def y_step(v, d):
    return lax.ppermute(v, "tp", tp_perm(0, d))


def x_swap(v):
    return lax.ppermute(v, "tp", tp_perm(1, 0))


def core_swap(v):
    return lax.ppermute(v, "ctx", [(i, i ^ 1) for i in range(NXL * NZ * NC)])


def xlo_swap(v):
    n = NXL * NZ * NC
    return lax.ppermute(v, "ctx", [(i, (i + n // 2) % n) for i in range(n)])


def from_behind(block, distance):
    n = NXL * NZ * NC
    route = [(i - distance, i) for i in range(n) if 0 <= i - distance < n]
    return lax.ppermute(block, "ctx", route)


def tie(values, *after):
    return lax.optimization_barrier((*values, *after))[: len(values)]


RELS = [(0, 0), (0, 3), (0, 1), (1, 0), (0, 2), (1, 3), (1, 1), (1, 2)]
SENT = [(1, 2), (0, 2), (1, 3), (1, 1), (1, 0), (0, 3), (0, 1), (0, 0)]


def gather_tp(own, beside_second):
    half = own.shape[0] // 2
    below = y_step(own, 1)
    above = y_step(own, -1)
    across = x_swap(own)
    second = (
        jnp.concatenate([below[:half], across[half:]]),
        jnp.concatenate([across[:half], above[half:]]),
        jnp.concatenate([below[:half], above[half:]]),
    )
    up = y_step(second[0], 1)
    down = y_step(second[1], -1)
    side = x_swap(second[2])
    far = jnp.concatenate([up[:half], down[half:]])
    x_below = jnp.concatenate([side[:half], up[half:]])
    x_above = jnp.concatenate([down[:half], side[half:]])
    third = tie((side[:half], side[half:]), *beside_second([own, below, above, across]))
    far_up = y_step(third[0], 1)
    far_down = y_step(third[1], -1)
    x_far = jnp.concatenate([far_up, far_down])
    return [own, below, above, across, far, x_below, x_above, x_far]


def cost(us):
    return pl.CostEstimate(flops=0, bytes_accessed=int(us * 3.4e6), transcendentals=0)


def call(kernel, outs, us, scratch=(), smem_first=False, mib=40):
    def run(*args):
        in_specs = [VMEM] * len(args)
        if smem_first:
            in_specs[0] = pl.BlockSpec(memory_space=pltpu.SMEM)
        return pl.pallas_call(
            kernel,
            out_shape=outs,
            in_specs=in_specs,
            out_specs=jax.tree.map(lambda _: VMEM, outs),
            scratch_shapes=list(scratch),
            compiler_params=pltpu.CompilerParams(vmem_limit_bytes=mib * 2**20),
            cost_estimate=cost(us),
        )(*args)

    return run


def halves(ref):
    half = ref.shape[-2] // 2
    return slice(0, half), slice(half, 2 * half)


def add_pair(keep_ref, got_ref, q_ref, k_ref, v_ref):
    total = keep_ref[...].astype(f32) + got_ref[...].astype(f32)
    q_ref[...] = total[:, : 2 * HD]
    k_ref[...] = total[:, 2 * HD : 3 * HD]
    v_ref[...] = total[:, 3 * HD :]


def head_terms(w_ref, dq_ref, dkv_ref):
    width = dq_ref.shape[0]
    t = jnp.dot(w_ref[0, :, :width], dq_ref[...], preferred_element_type=f32)
    return t + jnp.dot(w_ref[0, :, width:], dkv_ref[...], preferred_element_type=f32)


def first_terms(own_ref, w_ref, dq_ref, dkv_ref, top_ref, bottom_ref):
    t = head_terms(w_ref, dq_ref, dkv_ref).astype(bf16)
    lo, hi = halves(w_ref)
    top_ref[...] = t[lo]
    bottom_ref[...] = t[hi]


def second_terms(own_ref, w_ref, dq_ref, dkv_ref, side_ref, down_ref, up_ref):
    lo, hi = halves(w_ref)
    i = pl.program_id(0)
    t = head_terms(w_ref, dq_ref, dkv_ref).astype(bf16)

    @pl.when(i == 0)
    def _():
        down_ref[lo, :] = t[lo]
        up_ref[hi, :] = t[hi]

    @pl.when(i == 1)
    def _():
        side_ref[lo, :] = t[lo]
        down_ref[hi, :] = t[hi]

    @pl.when(i == 2)
    def _():
        up_ref[lo, :] = t[lo]
        side_ref[hi, :] = t[hi]


def third_terms(own_ref, w_ref, dq_ref, dkv_ref, across_ref, below_ref, above_ref, mine_ref):
    i = pl.program_id(0)
    t = head_terms(w_ref, dq_ref, dkv_ref)
    for n, ref in enumerate((across_ref, below_ref, above_ref, mine_ref)):

        @pl.when(i == n)
        def _(ref=ref):
            ref[...] = t.astype(ref.dtype)


def add_side(side_ref, top_ref, bottom_ref, out_ref):
    lo, hi = halves(side_ref)
    out_ref[lo, :] = (side_ref[lo, :].astype(f32) + top_ref[...].astype(f32)).astype(bf16)
    out_ref[hi, :] = (side_ref[hi, :].astype(f32) + bottom_ref[...].astype(f32)).astype(bf16)


def add_across(term_ref, down_ref, up_ref, out_ref):
    lo, hi = halves(term_ref)
    out_ref[lo, :] = (term_ref[lo, :].astype(f32) + up_ref[lo, :].astype(f32)).astype(bf16)
    out_ref[hi, :] = (term_ref[hi, :].astype(f32) + down_ref[hi, :].astype(f32)).astype(bf16)


def add_near(below_ref, above_ref, side_ref, down_ref, up_ref, out_b_ref, out_a_ref):
    lo, hi = halves(below_ref)
    more_b = side_ref[lo, :].astype(f32) + down_ref[lo, :].astype(f32)
    more_a = side_ref[hi, :].astype(f32) + up_ref[hi, :].astype(f32)
    out_b_ref[lo, :] = (below_ref[lo, :].astype(f32) + more_b).astype(bf16)
    out_b_ref[hi, :] = below_ref[hi, :]
    out_a_ref[lo, :] = above_ref[lo, :]
    out_a_ref[hi, :] = (above_ref[hi, :].astype(f32) + more_a).astype(bf16)


def add_last(mine_ref, a_ref, b_ref, c_ref, out_ref):
    got = a_ref[...].astype(f32) + b_ref[...].astype(f32) + c_ref[...].astype(f32)
    out_ref[...] = (mine_ref[...] + got).astype(bf16)


def with_table(kernel, us, grid, table, specs, args, outs, out_specs, scratch=()):
    return pl.pallas_call(
        kernel,
        out_shape=outs,
        grid_spec=pltpu.PrefetchScalarGridSpec(
            num_scalar_prefetch=1,
            grid=grid,
            in_specs=specs,
            out_specs=out_specs,
            scratch_shapes=list(scratch),
        ),
        compiler_params=pltpu.CompilerParams(vmem_limit_bytes=56 * 2**20),
        cost_estimate=cost(us),
    )(table, *args)


def scatter_tp(w_own, dq, dkv, table, beside):
    _, feats, cols = w_own.shape
    toks = dq.shape[1]
    sds = jax.ShapeDtypeStruct
    full, part = sds((feats, toks), bf16), sds((feats // 2, toks), bf16)

    def terms(kernel, us, first, count, outs, after=None):
        whole = lambda v: pl.BlockSpec(v.shape, lambda i, t: (0,) * len(v.shape))
        at = 1 + len(RELS) + first
        return with_table(
            kernel,
            us,
            (count,),
            table if after is None else tie((table,), after)[0],
            [
                pl.BlockSpec((1, feats, cols), lambda i, t: (t[at + i], 0, 0)),
                whole(dq),
                whole(dkv),
            ],
            (w_own, dq, dkv),
            outs,
            [whole(o) for o in outs],
        )

    top, bottom = terms(first_terms, 2.0, 0, 1, [part, part])
    extra = beside(top)
    top, bottom = y_step(top, -1), y_step(bottom, 1)
    side, down, up = terms(second_terms, 4.5, 1, 3, [full] * 3, extra)
    down, up = y_step(down, -1), y_step(up, 1)
    side = x_swap(call(add_side, full, 0.8)(side, top, bottom))
    mine = sds((feats, toks), f32)
    across, below, above, mine = terms(third_terms, 6.0, 4, 4, [full, full, full, mine])
    down, up, across, below, above = lax.optimization_barrier((down, up, across, below, above))
    across = x_swap(call(add_across, full, 0.8)(across, down, up))
    below, above = call(add_near, (full, full), 1.2)(below, above, side, down, up)
    below, above = y_step(below, -1), y_step(above, 1)
    return call(add_last, full, 1.5)(mine, across, below, above), extra


def join_kernel(place_ref, xa_ref, oa_ref, xb_ref, ob_ref, xc_ref, oc_ref, out_ref):
    step = pl.program_id(0)
    toks = oa_ref.shape[3]

    def put(x_ref, o_ref):
        for i in range(2):
            out_ref[0, i, 0, :, :toks] = x_ref[0, i, 0]
            out_ref[0, i, 0, :, toks:] = o_ref[0, i]

    pl.when(step < 4)(lambda: put(xa_ref, oa_ref))
    pl.when((step >= 4) & (step < 7))(lambda: put(xb_ref, ob_ref))
    pl.when(step == 7)(lambda: put(xc_ref, oc_ref))


def unrotate_norm(grad, raw, gain, cos, sin):
    top, bottom = grad[:HALF], grad[HALF:]
    d_normed = jnp.concatenate([top * cos + bottom * sin, bottom * cos - top * sin], axis=0)
    inv = lax.rsqrt(jnp.mean(raw * raw, axis=0, keepdims=True) + norm_eps)
    scaled = d_normed * gain
    along = jnp.mean(raw * scaled, axis=0, keepdims=True)
    return inv * scaled - raw * (inv * inv * inv * along)


def rotate_norm(raw, gain, cos, sin):
    inv = lax.rsqrt(jnp.mean(raw * raw, axis=0, keepdims=True) + norm_eps)
    normed = raw * inv * gain
    top, bottom = normed[:HALF], normed[HALF:]
    return jnp.concatenate([top * cos - bottom * sin, bottom * cos + top * sin], axis=0)


def heads_kernel(raw_ref, qg_ref, kg_ref, cos_ref, sin_ref, q_ref, kv_ref):
    cos, sin = cos_ref[...], sin_ref[...]
    for h in range(2):
        rows = slice(h * HD, (h + 1) * HD)
        q_ref[rows, :] = rotate_norm(raw_ref[rows, :], qg_ref[...], cos, sin).astype(bf16)
    kv_ref[0:HD, :] = rotate_norm(raw_ref[2 * HD : 3 * HD, :], kg_ref[...], cos, sin).astype(bf16)
    kv_ref[HD : 2 * HD, :] = raw_ref[3 * HD : 4 * HD, :].astype(bf16)


def attend_kernel(
    ctx_ref, q_ref, raw_ref, own_ref, m1_ref, m2_ref, go_ref, qg_ref, cos_ref, sin_ref,
    dq_ref, d_own_ref, d_m1_ref, d_m2_ref, e_s, dp_s, dk_s, dv_s,
):
    ctx = ctx_ref[0]
    toks = q_ref.shape[1]
    sub = 256
    cos, sin = cos_ref[...], sin_ref[...]
    blocks = (m2_ref, m1_ref, own_ref)
    for h in range(2):
        rows = slice(h * HD, (h + 1) * HD)
        q_t = q_ref[rows, :]
        q = q_t.T
        go = go_ref[:, rows]
        go_t = go.T
        total = jnp.zeros((1, toks), f32)
        weighted = jnp.zeros((1, toks), f32)
        for b in range(3):
            k = blocks[b][0:HD, :].T
            v = blocks[b][HD : 2 * HD, :].T
            for s0 in range(0, toks, sub):
                at = slice(b * toks + s0, b * toks + s0 + sub)
                s = jnp.dot(k[s0 : s0 + sub], q_t, preferred_element_type=f32) * query_scale
                dp = jnp.dot(v[s0 : s0 + sub], go_t, preferred_element_type=f32).astype(bf16)
                key = lax.broadcasted_iota(jnp.int32, (sub, toks), 0) + s0
                query = lax.broadcasted_iota(jnp.int32, (sub, toks), 1)
                if b == 0:
                    inside = (key > query) & (ctx >= 2)
                elif b == 1:
                    inside = (key >= 0) & (ctx >= 1)
                else:
                    inside = key <= query
                e = jnp.where(inside, jnp.exp(s), 0.0)
                e_s[at, :] = e
                dp_s[at, :] = dp
                total = total + jnp.sum(e, axis=0, keepdims=True)
                weighted = weighted + jnp.sum(e * dp.astype(f32), axis=0, keepdims=True)
        inv = 1.0 / total
        weighted = weighted * inv
        dq_t = jnp.zeros((HD, toks), f32)
        for b in range(3):
            for s0 in range(0, toks, sub):
                at = slice(b * toks + s0, b * toks + s0 + sub)
                p = e_s[at, :] * inv
                ds = (p * (dp_s[at, :].astype(f32) - weighted) * query_scale).astype(bf16)
                dv = jnp.dot(p.astype(bf16), go, preferred_element_type=f32)
                dk = jnp.dot(ds, q, preferred_element_type=f32)
                dq_t = dq_t + jnp.dot(
                    blocks[b][0:HD, s0 : s0 + sub], ds, preferred_element_type=f32
                )
                if h == 0:
                    dk_s[at, :] = dk
                    dv_s[at, :] = dv
                else:
                    out = (d_m2_ref, d_m1_ref, d_own_ref)[b]
                    out[0, s0 : s0 + sub, :] = (dk_s[at, :] + dk).astype(out.dtype)
                    out[1, s0 : s0 + sub, :] = (dv_s[at, :] + dv).astype(out.dtype)
        dq_low = dq_t.astype(bf16).astype(f32)
        dq_ref[rows, :] = unrotate_norm(dq_low, raw_ref[rows, :], qg_ref[...], cos, sin).astype(bf16)


def finish_kernel(own_ref, r1_ref, r2_ref, raw_ref, kg_ref, cos_ref, sin_ref, out_ref):
    def total(i):
        t = own_ref[i] + r1_ref[i].astype(f32) + r2_ref[i].astype(f32)
        return t.T.astype(bf16).astype(f32)

    out_ref[0:HD, :] = unrotate_norm(
        total(0), raw_ref[2 * HD : 3 * HD, :], kg_ref[...], cos_ref[...], sin_ref[...]
    ).astype(bf16)
    out_ref[HD : 2 * HD, :] = total(1).astype(bf16)


def shards(hidden_in, w_query, w_key, w_value, q_gain, k_gain, grad_out):
    toks, feats = hidden_in.shape
    sds = jax.ShapeDtypeStruct
    ctx = lax.axis_index("ctx")
    tp = lax.axis_index("tp")
    core, j = ctx % NC, ctx // NC
    xh, y = tp // NY, tp % NY
    n_tp = NXH * NY
    blk = feats // 4

    def owner(rel):
        return ((xh + rel[0]) % NXH) * NY + (y + rel[1]) % NY

    positions = ctx * toks + lax.iota(jnp.int32, toks)
    freqs = jnp.exp(-math.log(rope_base) * (2.0 * jnp.arange(HALF, dtype=f32) / HD))
    angles = freqs[:, None] * positions.astype(f32)[None, :]
    cos, sin = jnp.cos(angles), jnp.sin(angles)
    qg, kg = q_gain[:, None], k_gain[:, None]

    w_cat = jnp.concatenate([w_query, w_key, w_value], axis=1)
    w_own = w_cat.reshape(n_tp, feats, w_cat.shape[1])

    def project(total, parts, rels):
        for xs, rel in zip(parts, rels):
            ws = lax.dynamic_index_in_dim(w_own, owner(rel), 0, keepdims=False)
            term = lax.dot_general(ws, xs, (((0,), (0,)), ((), ())), preferred_element_type=f32)
            total = term if total is None else total + term
        return total

    begun = []

    def for_both(parts):
        x = jnp.stack(parts).reshape(len(parts), 2, NC, blk, toks)
        return x, lax.dynamic_index_in_dim(x, 1 - core, 2, keepdims=False)

    def beside(parts):
        begun.append(project(None, parts, RELS[:4]))
        begun.append(for_both(parts))
        return begun[0], *begun[1], cos, sin

    x_parts = gather_tp(hidden_in.T, beside)
    most = project(begun[0], x_parts[4:7], RELS[4:7])
    xb, ob = for_both(x_parts[4:7])
    last, most, xb, ob = lax.optimization_barrier((x_parts[7], most, xb, ob))
    raw = project(most, [last], RELS[7:])

    q_t, kv_t = call(heads_kernel, (sds((2 * HD, toks), bf16), sds((2 * HD, toks), bf16)), 1.5)(
        raw, qg, kg, cos, sin
    )
    rings = [[(a * NZ + z) * NC + c for z in range(NZ)] for a in range(NXL) for c in range(NC)]
    xl = j // NZ
    table = jnp.stack([core, *[owner(rel) for rel in RELS + SENT]]).astype(jnp.int32)

    def join(pairs, table):
        specs, first = [], 0
        for x, _ in pairs:
            at = lambda i, first=first, n=x.shape[0]: jnp.clip(i - first, 0, n - 1)
            first += x.shape[0]
            specs.append(
                pl.BlockSpec(
                    (1, 2, 1, blk, toks), lambda i, t, at=at: (at(i), 0, t[0], 0, 0)
                )
            )
            specs.append(pl.BlockSpec((1, 2, blk, toks), lambda i, t, at=at: (at(i), 0, 0, 0)))
        return with_table(
            join_kernel,
            6.0,
            (n_tp,),
            table,
            specs,
            [v for pair in pairs for v in pair],
            jax.ShapeDtypeStruct((NY, 2, NXH, blk, 2 * toks), bf16),
            pl.BlockSpec(
                (1, 2, 1, blk, 2 * toks), lambda i, t: (t[i + 1] % NY, 0, t[i + 1] // NY, 0, 0)
            ),
        ).reshape(NZ, NXL * blk, 2 * toks)

    def along_z(g):
        return lax.psum_scatter(
            g, "ctx", scatter_dimension=0, tiled=True, axis_index_groups=rings
        )[0]

    def across_x(g):
        g = g.reshape(NXL, blk, -1)
        keep = lax.dynamic_index_in_dim(g, xl, 0, keepdims=False)
        send = lax.dynamic_index_in_dim(g, 1 - xl, 0, keepdims=False)
        outs = [sds((blk, w), f32) for w in (2 * HD, HD, HD)]
        return call(add_pair, outs, 0.7)(keep, xlo_swap(send))

    kv1 = from_behind(kv_t, 1)
    kv2 = from_behind(kv_t, 2)
    xa, oa = begun[1]
    xc, oc = for_both([last])
    pairs = [(xa, core_swap(oa)), (xb, core_swap(ob)), (xc, core_swap(oc))]
    pair = sds((2, toks, HD), bf16)
    dq_raw, d_own, d1, d2 = call(
        attend_kernel,
        (sds((2 * HD, toks), bf16), sds((2, toks, HD), f32), pair, pair),
        5.5,
        (
            pltpu.VMEM((3 * toks, toks), f32),
            pltpu.VMEM((3 * toks, toks), bf16),
            pltpu.VMEM((3 * toks, HD), f32),
            pltpu.VMEM((3 * toks, HD), f32),
        ),
        smem_first=True,
    )(ctx[None], q_t, raw, kv_t, kv1, kv2, grad_out, qg, cos, sin)
    r1 = from_behind(d1, -1)
    r2 = from_behind(d2, -2)
    x_pair = join(pairs, tie((table,), dq_raw)[0])
    dq_other = core_swap(dq_raw)
    r1, r2, x_pair, dq_other = lax.optimization_barrier((r1, r2, x_pair, dq_other))
    dkv_raw = call(finish_kernel, sds((2 * HD, toks), bf16), 1.3)(
        d_own, r1, r2, raw, kg, cos, sin
    )
    dkv_other = core_swap(dkv_raw)

    def beside_tail(after):
        here, there, _ = lax.optimization_barrier((dkv_raw, dkv_other, after))
        d_pair = jnp.concatenate(
            [
                jnp.concatenate([dq_raw, dq_other], axis=1),
                jnp.concatenate([here, there], axis=1),
            ]
        )
        g = lax.dot_general(x_pair, d_pair, (((2,), (1,)), ((), ())), preferred_element_type=f32)
        return g.astype(bf16)

    grad_input, g = scatter_tp(w_own, dq_raw, dkv_raw, table, beside_tail)
    grad_input = grad_input.T
    grad_w = across_x(along_z(g))
    return (grad_input, *grad_w)


def solution(mesh):
    placed = (P("ctx", "tp"), P(None, "tp"), P(None, "tp"), P(None, "tp"), P(), P(), P("ctx", "tp"))
    return jax.shard_map(
        shards,
        mesh=mesh,
        in_specs=placed,
        out_specs=(P("ctx", "tp"), P("ctx", "tp"), P("ctx", "tp"), P("ctx", "tp")),
        check_vma=False,
    )
```

profile of v0, /device:TPU:2, one launch (start us, length us, event | category | flops | bytes accessed | tf_op | source)
XLA Modules:
  0.0 175.2 jit_solution(6219237429846423146)
XLA Ops:
  7.2 2.2 %collective-permute-start.3 = (bf16[672,512]{1,0:T(8,128)(2,1)}, bf16[672,512]{1,0:T(8,128)(2,1)S(1)}, u32[]{:S(2)}, u32[]{:S(2)}) collective-permute-start(bf16[672,512]{1,0:T(8,128)(2,1)} %bitcast.89), channel_id=1, source_target_pairs={{0,4},{1,5},{2,6},{3,7},{4,0},{5,1},{6,2},{7,3},{8,12},{9,13},{10,... | collective-permute-start | bytes 2064392 | tf_op jit(solution)/shard_map/ppermute | solution.py:38
  9.4 3.0 %collective-permute-start.1 = (bf16[672,512]{1,0:T(8,128)(2,1)}, bf16[672,512]{1,0:T(8,128)(2,1)S(1)}, u32[]{:S(2)}, u32[]{:S(2)}) collective-permute-start(bf16[672,512]{1,0:T(8,128)(2,1)} %bitcast.90), channel_id=1, source_target_pairs={{0,3},{1,0},{2,1},{3,2},{4,7},{5,4},{6,5},{7,6},{8,11},{9,8},{10,9... | collective-permute-start | bytes 2064392 | tf_op jit(solution)/shard_map/ppermute | solution.py:34
  12.4 3.4 %pad_maximum_fusion = bf16[5376,512]{1,0:T(8,128)(2,1)S(1)} fusion(bf16[5376,128]{1,0:T(8,128)(2,1)} %param.10, bf16[5376,128]{1,0:T(8,128)(2,1)} %param.9, bf16[5376,256]{1,0:T(8,128)(2,1)} %param.8), kind=kLoop, calls=%fused_computation | loop fusion | flops 16515072 | bytes 11010048 | tf_op jit(solution)/shard_map/concatenate | solution.py:377
  17.1 10.1 %collective-permute-done.1 = bf16[672,512]{1,0:T(8,128)(2,1)S(1)} collective-permute-done((bf16[672,512]{1,0:T(8,128)(2,1)}, bf16[672,512]{1,0:T(8,128)(2,1)S(1)}, u32[]{:S(2)}, u32[]{:S(2)}) %collective-permute-start.1) | collective-permute-done | bytes 688160 | tf_op jit(solution)/shard_map/ppermute | solution.py:34
  27.3 3.2 %collective-permute-done = bf16[672,512]{1,0:T(8,128)(2,1)S(1)} collective-permute-done((bf16[672,512]{1,0:T(8,128)(2,1)}, bf16[672,512]{1,0:T(8,128)(2,1)S(1)}, u32[]{:S(2)}, u32[]{:S(2)}) %collective-permute-start) | collective-permute-done | bytes 688160 | tf_op jit(solution)/shard_map/ppermute | solution.py:34
  30.8 1.5 collective-permute-start.2
  32.3 3.1 %collective-permute-start.7 = (bf16[672,512]{1,0:T(8,128)(2,1)S(1)}, bf16[672,512]{1,0:T(8,128)(2,1)S(1)}, u32[]{:S(2)}, u32[]{:S(2)}) collective-permute-start(bf16[672,512]{1,0:T(8,128)(2,1)S(1)} %get-tuple-element.94), channel_id=1, source_target_pairs={{0,3},{1,0},{2,1},{3,2},{4,7},{5,4},{6,5},{7,6},{8,11},{9,8},{10,9... | collective-permute-start | bytes 2064392 | tf_op jit(solution)/shard_map/ppermute | solution.py:34
  35.8 1.4 dynamic-slice_bitcast_fusion
  39.0 9.0 %collective-permute-done.2 = bf16[672,512]{1,0:T(8,128)(2,1)S(1)} collective-permute-done((bf16[672,512]{1,0:T(8,128)(2,1)S(1)}, bf16[672,512]{1,0:T(8,128)(2,1)S(1)}, u32[]{:S(2)}, u32[]{:S(2)}) %collective-permute-start.2) | collective-permute-done | bytes 688160 | tf_op jit(solution)/shard_map/ppermute | solution.py:38
  49.6 3.7 %collective-permute-start.5 = (bf16[336,512]{1,0:T(8,128)(2,1)S(1)}, bf16[336,512]{1,0:T(8,128)(2,1)S(1)}, u32[]{:S(2)}, u32[]{:S(2)}) collective-permute-start(bf16[336,512]{1,0:T(8,128)(2,1)S(1)} %get-tuple-element.44), channel_id=1, source_target_pairs={{0,3},{1,0},{2,1},{3,2},{4,7},{5,4},{6,5},{7,6},{8,11},{9,8},{10,9... | collective-permute-start | bytes 1032200 | tf_op jit(solution)/shard_map/ppermute | solution.py:34
  53.4 1.8 %fusion.2 = f32[512,512]{1,0:T(8,128)} fusion(f32[512,512]{1,0:T(8,128)S(1)} %fusion.11, f32[512,512]{1,0:T(8,128)S(1)} %fusion.13, f32[512,512]{1,0:T(8,128)S(1)} %fusion, bf16[8,672,512]{2,1,0:T(8,128)(2,1)S(1)} %bitcast.75, s32[]{:T(128)S(6)} %select_n.183, bf16[336,512]{1,0:T(8,128)(2,1)S(1)} %get-tuple-element.84, ...), kind=kOutput, calls=%fused_computation.10 | convolution fusion | flops 354484224 | bytes 5570564 | tf_op jit(solution)/shard_map/dot_general | solution.py:383
  55.4 1.3 copy-done.11
  56.7 1.1 dynamic-slice_bitcast_fusion.1
  58.9 0.7 collective-permute-start.14
  59.7 1.7 fusion.9
  61.4 1.5 add.260.raw_ref
  63.2 3.8 %collective-permute-start.9 = (bf16[256,512]{1,0:T(8,128)(2,1)S(1)}, bf16[256,512]{1,0:T(8,128)(2,1)S(1)}, u32[]{:S(2)}, u32[]{:S(2)}) collective-permute-start(bf16[256,512]{1,0:T(8,128)(2,1)S(1)} %get-tuple-element.48.own_ref), channel_id=1, source_target_pairs={{0,16},{8,24},{16,32},{24,40},{32,48},{40,56},{48,64},{56,72},{64,... | collective-permute-start | bytes 786440 | tf_op jit(solution)/shard_map/ppermute | solution.py:53
  67.0 1.9 %collective-permute-start.8 = (bf16[256,512]{1,0:T(8,128)(2,1)S(1)}, bf16[256,512]{1,0:T(8,128)(2,1)S(1)}, u32[]{:S(2)}, u32[]{:S(2)}) collective-permute-start(bf16[256,512]{1,0:T(8,128)(2,1)S(1)} %get-tuple-element.48.own_ref), channel_id=1, source_target_pairs={{0,8},{8,16},{16,24},{24,32},{32,40},{40,48},{48,56},{56,64},{64,7... | collective-permute-start | bytes 786440 | tf_op jit(solution)/shard_map/ppermute | solution.py:53
  68.9 9.7 %collective-permute-done.9.m2_ref = bf16[256,512]{1,0:T(8,128)(2,1)S(1)} collective-permute-done((bf16[256,512]{1,0:T(8,128)(2,1)S(1)}, bf16[256,512]{1,0:T(8,128)(2,1)S(1)}, u32[]{:S(2)}, u32[]{:S(2)}) %collective-permute-start.9) | collective-permute-done | bytes 262176 | tf_op jit(solution)/shard_map/ppermute | solution.py:53
  78.7 2.2 %collective-permute-done.8.m1_ref = bf16[256,512]{1,0:T(8,128)(2,1)S(1)} collective-permute-done((bf16[256,512]{1,0:T(8,128)(2,1)S(1)}, bf16[256,512]{1,0:T(8,128)(2,1)S(1)}, u32[]{:S(2)}, u32[]{:S(2)}) %collective-permute-start.8) | collective-permute-done | bytes 262176 | tf_op jit(solution)/shard_map/ppermute | solution.py:53
  80.9 5.4 %shard_map.103 = (bf16[256,512]{1,0:T(8,128)(2,1)S(1)}, f32[2,512,128]{2,1,0:T(8,128)S(1)}, bf16[2,512,128]{2,1,0:T(8,128)(2,1)S(1)}, bf16[2,512,128]{2,1,0:T(8,128)(2,1)S(1)}) custom-call(s32[1]{0:T(128)} %bitcast.10.ctx_ref, bf16[256,512]{1,0:T(8,128)(2,1)S(1)} %get-tuple-element.47.q_ref, f32[512,512]{1,0:T(8,128)S(1)} %add.260.raw_ref, ...), custom_call_target="tpu_custom_call" | custom-call | bytes 18700000 | tf_op jit(solution)/shard_map/pallas_call | solution.py:96
  86.3 1.9 %collective-permute-start.10 = (bf16[2,512,128]{2,1,0:T(8,128)(2,1)S(1)}, bf16[2,512,128]{2,1,0:T(8,128)(2,1)S(1)}, u32[]{:S(2)}, u32[]{:S(2)}) collective-permute-start(bf16[2,512,128]{2,1,0:T(8,128)(2,1)S(1)} %get-tuple-element.51), channel_id=1, source_target_pairs={{8,0},{16,8},{24,16},{32,24},{40,32},{48,40},{56,48},{64,56},{72,6... | collective-permute-start | bytes 786440 | tf_op jit(solution)/shard_map/ppermute | solution.py:53
  88.2 3.6 %collective-permute-start.11 = (bf16[2,512,128]{2,1,0:T(8,128)(2,1)S(1)}, bf16[2,512,128]{2,1,0:T(8,128)(2,1)S(1)}, u32[]{:S(2)}, u32[]{:S(2)}) collective-permute-start(bf16[2,512,128]{2,1,0:T(8,128)(2,1)S(1)} %get-tuple-element.52), channel_id=1, source_target_pairs={{16,0},{24,8},{32,16},{40,24},{48,32},{56,40},{64,48},{72,56},{80,... | collective-permute-start | bytes 786440 | tf_op jit(solution)/shard_map/ppermute | solution.py:53
  93.5 8.1 %shard_map.104 = bf16[4,2,2,168,1024]{4,3,2,1,0:T(8,128)(2,1)} custom-call(s32[17]{0:T(128)} %stack.74.place_ref.own_ref, bf16[4,2,2,168,512]{4,3,2,1,0:T(8,128)(2,1)} %copy-done.10, bf16[4,2,168,512]{3,2,1,0:T(8,128)(2,1)} %collective-permute-done.12.oa_ref, bf16[3,2,2,168,512]{4,3,2,1,0:T(8,128)(2,1)} %copy-done.11, ...), custom_call_target="tpu_custom_call" | custom-call | bytes 20400000 | tf_op jit(solution)/shard_map/pallas_call | solution.py:193
  102.5 3.6 %shard_map.107 = (bf16[336,512]{1,0:T(8,128)(2,1)}, bf16[336,512]{1,0:T(8,128)(2,1)}) custom-call(s32[17]{0:T(128)} %stack.74.place_ref.own_ref, bf16[8,672,512]{2,1,0:T(8,128)(2,1)} %bitcast.77, bf16[256,512]{1,0:T(8,128)(2,1)} %copy-done.1, bf16[256,512]{1,0:T(8,128)(2,1)} %copy-done), custom_call_target="tpu_custom_call" | custom-call | bytes 6800000 | tf_op jit(solution)/shard_map/pallas_call | solution.py:193
  106.1 5.5 %convolution_convert_fusion = bf16[8,336,512]{2,1,0:T(8,128)(2,1)} fusion(bf16[8,336,1024]{2,1,0:T(8,128)(2,1)S(1)} %bitcast.80, bf16[256,512]{1,0:T(8,128)(2,1)S(1)} %collective-permute-done.16, bf16[256,512]{1,0:T(8,128)(2,1)} %copy-done, bf16[256,512]{1,0:T(8,128)(2,1)} %collective-permute-done.15, bf16[256,512]{1,0:T(8,128)(2,1)S(1)} %copy-done.2), kind=kOutput, calls=%fused_computation.2 | convolution fusion | flops 2824142848 | bytes 9306112 | tf_op jit(solution)/shard_map/dot_general | solution.py:483
  111.7 0.9 copy-done.19
  112.6 0.9 collective-permute-start.21
  113.5 2.4 %collective-permute-start.20 = (bf16[336,512]{1,0:T(8,128)(2,1)S(1)}, bf16[336,512]{1,0:T(8,128)(2,1)S(1)}, u32[]{:S(2)}, u32[]{:S(2)}) collective-permute-start(bf16[336,512]{1,0:T(8,128)(2,1)S(1)} %copy-done.18), channel_id=1, source_target_pairs={{0,3},{1,0},{2,1},{3,2},{4,7},{5,4},{6,5},{7,6},{8,11},{9,8},{10,9... | collective-permute-start | bytes 1032200 | tf_op jit(solution)/shard_map/ppermute | solution.py:34
  115.9 5.6 %shard_map.108 = (bf16[672,512]{1,0:T(8,128)(2,1)}, bf16[672,512]{1,0:T(8,128)(2,1)}, bf16[672,512]{1,0:T(8,128)(2,1)}) custom-call(s32[17]{0:T(128)} %stack.74.place_ref.own_ref, bf16[8,672,512]{2,1,0:T(8,128)(2,1)} %bitcast.78, bf16[256,512]{1,0:T(8,128)(2,1)} %copy-done.1, bf16[256,512]{1,0:T(8,128)(2,1)} %copy-done), custom_call_target="tpu_custom_call" | custom-call | bytes 15300000 | tf_op jit(solution)/shard_map/pallas_call | solution.py:193
  121.4 1.9 %collective-permute-start.17 = (bf16[672,512]{1,0:T(8,128)(2,1)}, bf16[672,512]{1,0:T(8,128)(2,1)S(1)}, u32[]{:S(2)}, u32[]{:S(2)}) collective-permute-start(bf16[672,512]{1,0:T(8,128)(2,1)} %get-tuple-element.65), channel_id=1, source_target_pairs={{0,3},{1,0},{2,1},{3,2},{4,7},{5,4},{6,5},{7,6},{8,11},{9,8},{10,9... | collective-permute-start | bytes 2064392 | tf_op jit(solution)/shard_map/ppermute | solution.py:34
  123.5 0.8 collective-permute-done.21.bottom_ref
  124.3 1.1 copy-done.6
  125.5 2.0 %collective-permute-start.22 = (bf16[672,512]{1,0:T(8,128)(2,1)S(1)}, bf16[672,512]{1,0:T(8,128)(2,1)S(1)}, u32[]{:S(2)}, u32[]{:S(2)}) collective-permute-start(bf16[672,512]{1,0:T(8,128)(2,1)S(1)} %shard_map.110), channel_id=1, source_target_pairs={{0,4},{1,5},{2,6},{3,7},{4,0},{5,1},{6,2},{7,3},{8,12},{9,13},{10,... | collective-permute-start | bytes 2064392 | tf_op jit(solution)/shard_map/ppermute | solution.py:38
  127.6 6.7 %shard_map.106 = (bf16[672,512]{1,0:T(8,128)(2,1)}, bf16[672,512]{1,0:T(8,128)(2,1)}, bf16[672,512]{1,0:T(8,128)(2,1)}, f32[672,512]{1,0:T(8,128)}) custom-call(s32[17]{0:T(128)} %stack.74.place_ref.own_ref, bf16[8,672,512]{2,1,0:T(8,128)(2,1)} %bitcast.79, bf16[256,512]{1,0:T(8,128)(2,1)} %copy-done.1, bf16[256,512]{1,0:T(8,128)(2,1)} %copy-done), custom_call_target="tpu_custom_call" | custom-call | bytes 20400000 | tf_op jit(solution)/shard_map/pallas_call | solution.py:193
  134.3 4.7 %collective-permute-done.17.down_ref = bf16[672,512]{1,0:T(8,128)(2,1)S(1)} collective-permute-done((bf16[672,512]{1,0:T(8,128)(2,1)}, bf16[672,512]{1,0:T(8,128)(2,1)S(1)}, u32[]{:S(2)}, u32[]{:S(2)}) %collective-permute-start.17) | collective-permute-done | bytes 688160 | tf_op jit(solution)/shard_map/ppermute | solution.py:34
  139.0 2.6 %collective-permute-done.18.up_ref = bf16[672,512]{1,0:T(8,128)(2,1)S(1)} collective-permute-done((bf16[672,512]{1,0:T(8,128)(2,1)}, bf16[672,512]{1,0:T(8,128)(2,1)S(1)}, u32[]{:S(2)}, u32[]{:S(2)}) %collective-permute-start.18) | collective-permute-done | bytes 688160 | tf_op jit(solution)/shard_map/ppermute | solution.py:34
  141.6 1.1 copy-done.7
  142.8 2.0 %collective-permute-start.19 = (bf16[672,512]{1,0:T(8,128)(2,1)S(1)}, bf16[672,512]{1,0:T(8,128)(2,1)S(1)}, u32[]{:S(2)}, u32[]{:S(2)}) collective-permute-start(bf16[672,512]{1,0:T(8,128)(2,1)S(1)} %shard_map.109), channel_id=1, source_target_pairs={{0,4},{1,5},{2,6},{3,7},{4,0},{5,1},{6,2},{7,3},{8,12},{9,13},{10,... | collective-permute-start | bytes 2064392 | tf_op jit(solution)/shard_map/ppermute | solution.py:38
  144.9 1.2 shard_map.111
  146.1 2.3 %collective-permute-start.23 = (bf16[672,512]{1,0:T(8,128)(2,1)}, bf16[672,512]{1,0:T(8,128)(2,1)S(1)}, u32[]{:S(2)}, u32[]{:S(2)}) collective-permute-start(bf16[672,512]{1,0:T(8,128)(2,1)} %get-tuple-element.77), channel_id=1, source_target_pairs={{0,3},{1,0},{2,1},{3,2},{4,7},{5,4},{6,5},{7,6},{8,11},{9,8},{10,9... | collective-permute-start | bytes 2064392 | tf_op jit(solution)/shard_map/ppermute | solution.py:34
  148.5 6.3 %reduce-scatter.2.cloned.1.call-done = bf16[1,336,512]{2,1,0:T(8,128)(2,1)} async-done(((bf16[8,336,512]{2,1,0:T(8,128)(2,1)}), bf16[1,336,512]{2,1,0:T(8,128)(2,1)}) %reduce-scatter.2.cloned.1.call-update) | async-done | bytes 344080 | tf_op jit(solution)/shard_map/reduce_scatter | solution.py:436
  154.8 1.0 dynamic-slice_bitcast_fusion.3
  155.8 0.8 collective-permute-start.25
  156.6 5.7 %collective-permute-done.19.a_ref = bf16[672,512]{1,0:T(8,128)(2,1)S(1)} collective-permute-done((bf16[672,512]{1,0:T(8,128)(2,1)S(1)}, bf16[672,512]{1,0:T(8,128)(2,1)S(1)}, u32[]{:S(2)}, u32[]{:S(2)}) %collective-permute-start.19) | collective-permute-done | bytes 688160 | tf_op jit(solution)/shard_map/ppermute | solution.py:38
  162.3 3.1 %collective-permute-done.24.c_ref = bf16[672,512]{1,0:T(8,128)(2,1)} collective-permute-done((bf16[672,512]{1,0:T(8,128)(2,1)}, bf16[672,512]{1,0:T(8,128)(2,1)}, u32[]{:S(2)}, u32[]{:S(2)}) %collective-permute-start.24) | collective-permute-done | bytes 688160 | tf_op jit(solution)/shard_map/ppermute | solution.py:34
  165.3 2.2 %shard_map.112 = bf16[672,512]{1,0:T(8,128)(2,1)} custom-call(f32[672,512]{1,0:T(8,128)S(1)} %copy-done.3, bf16[672,512]{1,0:T(8,128)(2,1)S(1)} %collective-permute-done.19.a_ref, bf16[672,512]{1,0:T(8,128)(2,1)S(1)} %collective-permute-done.23.b_ref, bf16[672,512]{1,0:T(8,128)(2,1)} %collective-permute-done.24.c_ref), custom_call_target="tpu_custom_call" | custom-call | bytes 5100000 | tf_op jit(solution)/shard_map/pallas_call | solution.py:96
  167.6 0.7 shard_map.113
  (92 shorter events, 9.9 us)
Async XLA Ops:
  7.2 147.6 %reduce-scatter.2.cloned.1.call-start = ((), (), s32[]{:S(2)}) async-start(), calls=%async_computation.1 | async-start | bytes 3096576 | tf_op jit(solution)/shard_map/reduce_scatter | solution.py:436
  7.2 20.0 %collective-permute-start.3 = (bf16[672,512]{1,0:T(8,128)(2,1)}, bf16[672,512]{1,0:T(8,128)(2,1)S(1)}, u32[]{:S(2)}, u32[]{:S(2)}) collective-permute-start(bf16[672,512]{1,0:T(8,128)(2,1)} %bitcast.89), channel_id=1, source_target_pairs={{0,4},{1,5},{2,6},{3,7},{4,0},{5,1},{6,2},{7,3},{8,12},{9,13},{10,... | collective-permute-start | bytes 2064392 | tf_op jit(solution)/shard_map/ppermute | solution.py:38
  9.4 17.7 %collective-permute-start.1 = (bf16[672,512]{1,0:T(8,128)(2,1)}, bf16[672,512]{1,0:T(8,128)(2,1)S(1)}, u32[]{:S(2)}, u32[]{:S(2)}) collective-permute-start(bf16[672,512]{1,0:T(8,128)(2,1)} %bitcast.90), channel_id=1, source_target_pairs={{0,3},{1,0},{2,1},{3,2},{4,7},{5,4},{6,5},{7,6},{8,11},{9,8},{10,9... | collective-permute-start | bytes 2064392 | tf_op jit(solution)/shard_map/ppermute | solution.py:34
  12.4 18.0 %collective-permute-start = (bf16[672,512]{1,0:T(8,128)(2,1)}, bf16[672,512]{1,0:T(8,128)(2,1)S(1)}, u32[]{:S(2)}, u32[]{:S(2)}) collective-permute-start(bf16[672,512]{1,0:T(8,128)(2,1)} %bitcast.91), channel_id=1, source_target_pairs={{0,1},{1,2},{2,3},{3,0},{4,5},{5,6},{6,7},{7,4},{8,9},{9,10},{10,1... | collective-permute-start | bytes 2064392 | tf_op jit(solution)/shard_map/ppermute | solution.py:34
  12.4 4.0 %copy-start.14 = (bf16[512,672]{0,1:T(8,128)(2,1)S(1)}, bf16[512,672]{0,1:T(8,128)(2,1)}, u32[]{:S(2)}) copy-start(bf16[512,672]{0,1:T(8,128)(2,1)} %param.7) | copy-start | bytes 2064388
  15.9 37.5 %copy-start.9 = (bf16[5376,512]{1,0:T(8,128)(2,1)}, bf16[5376,512]{1,0:T(8,128)(2,1)S(1)}, u32[]{:S(2)}) copy-start(bf16[5376,512]{1,0:T(8,128)(2,1)S(1)} %pad_maximum_fusion) | copy-start | bytes 16515076
  30.7 18.1 %collective-permute-start.6 = (bf16[672,512]{1,0:T(8,128)(2,1)S(1)}, bf16[672,512]{1,0:T(8,128)(2,1)S(1)}, u32[]{:S(2)}, u32[]{:S(2)}) collective-permute-start(bf16[672,512]{1,0:T(8,128)(2,1)S(1)} %get-tuple-element.92), channel_id=1, source_target_pairs={{0,1},{1,2},{2,3},{3,0},{4,5},{5,6},{6,7},{7,4},{8,9},{9,10},{10,1... | collective-permute-start | bytes 2064392 | tf_op jit(solution)/shard_map/ppermute | solution.py:34
  30.8 17.3 %collective-permute-start.2 = (bf16[672,512]{1,0:T(8,128)(2,1)S(1)}, bf16[672,512]{1,0:T(8,128)(2,1)S(1)}, u32[]{:S(2)}, u32[]{:S(2)}) collective-permute-start(bf16[672,512]{1,0:T(8,128)(2,1)S(1)} %get-tuple-element.93), channel_id=1, source_target_pairs={{0,4},{1,5},{2,6},{3,7},{4,0},{5,1},{6,2},{7,3},{8,12},{9,13},{10,... | collective-permute-start | bytes 2064392 | tf_op jit(solution)/shard_map/ppermute | solution.py:38
  32.3 15.8 %collective-permute-start.7 = (bf16[672,512]{1,0:T(8,128)(2,1)S(1)}, bf16[672,512]{1,0:T(8,128)(2,1)S(1)}, u32[]{:S(2)}, u32[]{:S(2)}) collective-permute-start(bf16[672,512]{1,0:T(8,128)(2,1)S(1)} %get-tuple-element.94), channel_id=1, source_target_pairs={{0,3},{1,0},{2,1},{3,2},{4,7},{5,4},{6,5},{7,6},{8,11},{9,8},{10,9... | collective-permute-start | bytes 2064392 | tf_op jit(solution)/shard_map/ppermute | solution.py:34
  35.8 2.0 %copy-start.10 = (bf16[4,2,2,168,512]{4,3,2,1,0:T(8,128)(2,1)}, bf16[4,2,2,168,512]{4,3,2,1,0:T(8,128)(2,1)S(1)}, u32[]{:S(2)}) copy-start(bf16[4,2,2,168,512]{4,3,2,1,0:T(8,128)(2,1)S(1)} %pad_maximum_fusion.1.xa_ref) | copy-start | bytes 8257540
  37.1 56.3 %collective-permute-start.12 = (bf16[4,2,168,512]{3,2,1,0:T(8,128)(2,1)}, bf16[4,2,168,512]{3,2,1,0:T(8,128)(2,1)}, u32[]{:S(2)}, u32[]{:S(2)}) collective-permute-start(bf16[4,2,168,512]{3,2,1,0:T(8,128)(2,1)} %dynamic-slice_bitcast_fusion), channel_id=1, source_target_pairs={{0,8},{8,0},{16,24},{24,16},{32,40},{40,32},{48,56},{56,48},{64,72... | collective-permute-start | bytes 4128776 | tf_op jit(solution)/shard_map/ppermute | solution.py:42
  49.6 8.9 %collective-permute-start.4 = (bf16[336,512]{1,0:T(8,128)(2,1)S(1)}, bf16[336,512]{1,0:T(8,128)(2,1)S(1)}, u32[]{:S(2)}, u32[]{:S(2)}) collective-permute-start(bf16[336,512]{1,0:T(8,128)(2,1)S(1)} %get-tuple-element.43), channel_id=1, source_target_pairs={{0,1},{1,2},{2,3},{3,0},{4,5},{5,6},{6,7},{7,4},{8,9},{9,10},{10,1... | collective-permute-start | bytes 1032200 | tf_op jit(solution)/shard_map/ppermute | solution.py:34
  49.6 8.8 %collective-permute-start.5 = (bf16[336,512]{1,0:T(8,128)(2,1)S(1)}, bf16[336,512]{1,0:T(8,128)(2,1)S(1)}, u32[]{:S(2)}, u32[]{:S(2)}) collective-permute-start(bf16[336,512]{1,0:T(8,128)(2,1)S(1)} %get-tuple-element.44), channel_id=1, source_target_pairs={{0,3},{1,0},{2,1},{3,2},{4,7},{5,4},{6,5},{7,6},{8,11},{9,8},{10,9... | collective-permute-start | bytes 1032200 | tf_op jit(solution)/shard_map/ppermute | solution.py:34
  55.4 1.3 copy-start.11
  56.7 1.9 %copy-start.16 = (f32[128]{0:T(128)S(1)}, f32[128]{0:T(128)}, u32[]{:S(2)}) copy-start(f32[128]{0:T(128)} %param.11) | copy-start | bytes 1540
  56.7 2.1 %copy-start.17 = (f32[128]{0:T(128)S(1)}, f32[128]{0:T(128)}, u32[]{:S(2)}) copy-start(f32[128]{0:T(128)} %param.12) | copy-start | bytes 1540
  58.5 1.2 copy-start.13
  58.6 34.9 %collective-permute-start.13 = (bf16[3,2,168,512]{3,2,1,0:T(8,128)(2,1)}, bf16[3,2,168,512]{3,2,1,0:T(8,128)(2,1)}, u32[]{:S(2)}, u32[]{:S(2)}) collective-permute-start(bf16[3,2,168,512]{3,2,1,0:T(8,128)(2,1)} %dynamic-slice_bitcast_fusion.1), channel_id=1, source_target_pairs={{0,8},{8,0},{16,24},{24,16},{32,40},{40,32},{48,56},{56,48},{64,72... | collective-permute-start | bytes 3096584 | tf_op jit(solution)/shard_map/ppermute | solution.py:42
  58.9 32.9 %collective-permute-start.14 = (bf16[1,2,168,512]{3,2,1,0:T(8,128)(2,1)S(1)}, bf16[1,2,168,512]{3,2,1,0:T(8,128)(2,1)S(1)}, u32[]{:S(2)}, u32[]{:S(2)}) collective-permute-start(bf16[1,2,168,512]{3,2,1,0:T(8,128)(2,1)S(1)} %dynamic-slice_bitcast_fusion.2), channel_id=1, source_target_pairs={{0,8},{8,0},{16,24},{24,16},{32,40},{40,32},{48,56},{56,48},{64,72... | collective-permute-start | bytes 1032200 | tf_op jit(solution)/shard_map/ppermute | solution.py:42
  61.4 19.5 %copy-start.8 = (bf16[512,256]{1,0:T(8,128)(2,1)S(1)}, bf16[512,256]{1,0:T(8,128)(2,1)}, u32[]{:S(2)}) copy-start(bf16[512,256]{1,0:T(8,128)(2,1)} %go_ref.1) | copy-start | bytes 786436
  63.2 15.5 %collective-permute-start.9 = (bf16[256,512]{1,0:T(8,128)(2,1)S(1)}, bf16[256,512]{1,0:T(8,128)(2,1)S(1)}, u32[]{:S(2)}, u32[]{:S(2)}) collective-permute-start(bf16[256,512]{1,0:T(8,128)(2,1)S(1)} %get-tuple-element.48.own_ref), channel_id=1, source_target_pairs={{0,16},{8,24},{16,32},{24,40},{32,48},{40,56},{48,64},{56,72},{64,... | collective-permute-start | bytes 786440 | tf_op jit(solution)/shard_map/ppermute | solution.py:53
  67.0 13.8 %collective-permute-start.8 = (bf16[256,512]{1,0:T(8,128)(2,1)S(1)}, bf16[256,512]{1,0:T(8,128)(2,1)S(1)}, u32[]{:S(2)}, u32[]{:S(2)}) collective-permute-start(bf16[256,512]{1,0:T(8,128)(2,1)S(1)} %get-tuple-element.48.own_ref), channel_id=1, source_target_pairs={{0,8},{8,16},{16,24},{24,32},{32,40},{40,48},{48,56},{56,64},{64,7... | collective-permute-start | bytes 786440 | tf_op jit(solution)/shard_map/ppermute | solution.py:53
  86.3 15.3 %copy-start.1 = (bf16[256,512]{1,0:T(8,128)(2,1)}, bf16[256,512]{1,0:T(8,128)(2,1)S(1)}, u32[]{:S(2)}) copy-start(bf16[256,512]{1,0:T(8,128)(2,1)S(1)} %get-tuple-element.49.dq_ref) | copy-start | bytes 786436
  86.3 15.2 %collective-permute-start.10 = (bf16[2,512,128]{2,1,0:T(8,128)(2,1)S(1)}, bf16[2,512,128]{2,1,0:T(8,128)(2,1)S(1)}, u32[]{:S(2)}, u32[]{:S(2)}) collective-permute-start(bf16[2,512,128]{2,1,0:T(8,128)(2,1)S(1)} %get-tuple-element.51), channel_id=1, source_target_pairs={{8,0},{16,8},{24,16},{32,24},{40,32},{48,40},{56,48},{64,56},{72,6... | collective-permute-start | bytes 786440 | tf_op jit(solution)/shard_map/ppermute | solution.py:53
  88.2 13.3 %collective-permute-start.11 = (bf16[2,512,128]{2,1,0:T(8,128)(2,1)S(1)}, bf16[2,512,128]{2,1,0:T(8,128)(2,1)S(1)}, u32[]{:S(2)}, u32[]{:S(2)}) collective-permute-start(bf16[2,512,128]{2,1,0:T(8,128)(2,1)S(1)} %get-tuple-element.52), channel_id=1, source_target_pairs={{16,0},{24,8},{32,16},{40,24},{48,32},{56,40},{64,48},{72,56},{80,... | collective-permute-start | bytes 786440 | tf_op jit(solution)/shard_map/ppermute | solution.py:53
  91.9 0.7 copy-start.15
  92.6 8.9 %collective-permute-start.15 = (bf16[256,512]{1,0:T(8,128)(2,1)S(1)}, bf16[256,512]{1,0:T(8,128)(2,1)}, u32[]{:S(2)}, u32[]{:S(2)}) collective-permute-start(bf16[256,512]{1,0:T(8,128)(2,1)S(1)} %get-tuple-element.49.dq_ref), channel_id=1, source_target_pairs={{0,8},{8,0},{16,24},{24,16},{32,40},{40,32},{48,56},{56,48},{64,72... | collective-permute-start | bytes 786440 | tf_op jit(solution)/shard_map/ppermute | solution.py:42
  101.8 0.7 copy-start
  101.8 4.3 %copy-start.2 = (bf16[256,512]{1,0:T(8,128)(2,1)S(1)}, bf16[256,512]{1,0:T(8,128)(2,1)}, u32[]{:S(2)}) copy-start(bf16[256,512]{1,0:T(8,128)(2,1)} %copy-done.1) | copy-start | bytes 786436
  101.8 4.3 %copy-start.12 = (bf16[4,2,2,168,1024]{4,3,2,1,0:T(8,128)(2,1)S(1)}, bf16[4,2,2,168,1024]{4,3,2,1,0:T(8,128)(2,1)}, u32[]{:S(2)}) copy-start(bf16[4,2,2,168,1024]{4,3,2,1,0:T(8,128)(2,1)} %shard_map.104) | copy-start | bytes 16515076
  101.8 4.3 %collective-permute-start.16 = (bf16[256,512]{1,0:T(8,128)(2,1)S(1)}, bf16[256,512]{1,0:T(8,128)(2,1)S(1)}, u32[]{:S(2)}, u32[]{:S(2)}) collective-permute-start(bf16[256,512]{1,0:T(8,128)(2,1)S(1)} %shard_map.105.dkv_ref), channel_id=1, source_target_pairs={{0,8},{8,0},{16,24},{24,16},{32,40},{40,32},{48,56},{56,48},{64,72... | collective-permute-start | bytes 786440 | tf_op jit(solution)/shard_map/ppermute | solution.py:42
  111.6 1.0 copy-start.19
  111.6 1.8 %copy-start.18 = (bf16[336,512]{1,0:T(8,128)(2,1)S(1)}, bf16[336,512]{1,0:T(8,128)(2,1)}, u32[]{:S(2)}) copy-start(bf16[336,512]{1,0:T(8,128)(2,1)} %get-tuple-element.61) | copy-start | bytes 1032196
  112.6 11.7 %collective-permute-start.21 = (bf16[336,512]{1,0:T(8,128)(2,1)S(1)}, bf16[336,512]{1,0:T(8,128)(2,1)S(1)}, u32[]{:S(2)}, u32[]{:S(2)}) collective-permute-start(bf16[336,512]{1,0:T(8,128)(2,1)S(1)} %copy-done.19), channel_id=1, source_target_pairs={{0,1},{1,2},{2,3},{3,0},{4,5},{5,6},{6,7},{7,4},{8,9},{9,10},{10,1... | collective-permute-start | bytes 1032200 | tf_op jit(solution)/shard_map/ppermute | solution.py:34
  113.5 10.8 %collective-permute-start.20 = (bf16[336,512]{1,0:T(8,128)(2,1)S(1)}, bf16[336,512]{1,0:T(8,128)(2,1)S(1)}, u32[]{:S(2)}, u32[]{:S(2)}) collective-permute-start(bf16[336,512]{1,0:T(8,128)(2,1)S(1)} %copy-done.18), channel_id=1, source_target_pairs={{0,3},{1,0},{2,1},{3,2},{4,7},{5,4},{6,5},{7,6},{8,11},{9,8},{10,9... | collective-permute-start | bytes 1032200 | tf_op jit(solution)/shard_map/ppermute | solution.py:34
  121.4 17.6 %collective-permute-start.17 = (bf16[672,512]{1,0:T(8,128)(2,1)}, bf16[672,512]{1,0:T(8,128)(2,1)S(1)}, u32[]{:S(2)}, u32[]{:S(2)}) collective-permute-start(bf16[672,512]{1,0:T(8,128)(2,1)} %get-tuple-element.65), channel_id=1, source_target_pairs={{0,3},{1,0},{2,1},{3,2},{4,7},{5,4},{6,5},{7,6},{8,11},{9,8},{10,9... | collective-permute-start | bytes 2064392 | tf_op jit(solution)/shard_map/ppermute | solution.py:34
  123.4 18.2 %collective-permute-start.18 = (bf16[672,512]{1,0:T(8,128)(2,1)}, bf16[672,512]{1,0:T(8,128)(2,1)S(1)}, u32[]{:S(2)}, u32[]{:S(2)}) collective-permute-start(bf16[672,512]{1,0:T(8,128)(2,1)} %get-tuple-element.66), channel_id=1, source_target_pairs={{0,1},{1,2},{2,3},{3,0},{4,5},{5,6},{6,7},{7,4},{8,9},{9,10},{10,1... | collective-permute-start | bytes 2064392 | tf_op jit(solution)/shard_map/ppermute | solution.py:34
  124.3 1.1 copy-start.6
  125.5 19.3 %collective-permute-start.22 = (bf16[672,512]{1,0:T(8,128)(2,1)S(1)}, bf16[672,512]{1,0:T(8,128)(2,1)S(1)}, u32[]{:S(2)}, u32[]{:S(2)}) collective-permute-start(bf16[672,512]{1,0:T(8,128)(2,1)S(1)} %shard_map.110), channel_id=1, source_target_pairs={{0,4},{1,5},{2,6},{3,7},{4,0},{5,1},{6,2},{7,3},{8,12},{9,13},{10,... | collective-permute-start | bytes 2064392 | tf_op jit(solution)/shard_map/ppermute | solution.py:38
  134.3 10.6 %copy-start.4 = (bf16[672,512]{1,0:T(8,128)(2,1)S(1)}, bf16[672,512]{1,0:T(8,128)(2,1)}, u32[]{:S(2)}) copy-start(bf16[672,512]{1,0:T(8,128)(2,1)} %get-tuple-element.73.below_ref) | copy-start | bytes 2064388
  134.3 10.6 %copy-start.5 = (bf16[672,512]{1,0:T(8,128)(2,1)S(1)}, bf16[672,512]{1,0:T(8,128)(2,1)}, u32[]{:S(2)}) copy-start(bf16[672,512]{1,0:T(8,128)(2,1)} %get-tuple-element.74.above_ref) | copy-start | bytes 2064388
  141.6 1.1 copy-start.7
  142.8 22.5 %copy-start.3 = (f32[672,512]{1,0:T(8,128)S(1)}, f32[672,512]{1,0:T(8,128)}, u32[]{:S(2)}) copy-start(f32[672,512]{1,0:T(8,128)} %get-tuple-element.58.mine_ref) | copy-start | bytes 4128772
  142.8 19.4 %collective-permute-start.19 = (bf16[672,512]{1,0:T(8,128)(2,1)S(1)}, bf16[672,512]{1,0:T(8,128)(2,1)S(1)}, u32[]{:S(2)}, u32[]{:S(2)}) collective-permute-start(bf16[672,512]{1,0:T(8,128)(2,1)S(1)} %shard_map.109), channel_id=1, source_target_pairs={{0,4},{1,5},{2,6},{3,7},{4,0},{5,1},{6,2},{7,3},{8,12},{9,13},{10,... | collective-permute-start | bytes 2064392 | tf_op jit(solution)/shard_map/ppermute | solution.py:38
  146.1 16.1 %collective-permute-start.23 = (bf16[672,512]{1,0:T(8,128)(2,1)}, bf16[672,512]{1,0:T(8,128)(2,1)S(1)}, u32[]{:S(2)}, u32[]{:S(2)}) collective-permute-start(bf16[672,512]{1,0:T(8,128)(2,1)} %get-tuple-element.77), channel_id=1, source_target_pairs={{0,3},{1,0},{2,1},{3,2},{4,7},{5,4},{6,5},{7,6},{8,11},{9,8},{10,9... | collective-permute-start | bytes 2064392 | tf_op jit(solution)/shard_map/ppermute | solution.py:34
  148.5 16.9 %collective-permute-start.24 = (bf16[672,512]{1,0:T(8,128)(2,1)}, bf16[672,512]{1,0:T(8,128)(2,1)}, u32[]{:S(2)}, u32[]{:S(2)}) collective-permute-start(bf16[672,512]{1,0:T(8,128)(2,1)} %get-tuple-element.78), channel_id=1, source_target_pairs={{0,1},{1,2},{2,3},{3,0},{4,5},{5,6},{6,7},{7,4},{8,9},{9,10},{10,1... | collective-permute-start | bytes 2064392 | tf_op jit(solution)/shard_map/ppermute | solution.py:34
  155.8 11.8 %collective-permute-start.25 = (bf16[168,512]{1,0:T(8,128)(2,1)S(1)}, bf16[168,512]{1,0:T(8,128)(2,1)S(1)}, u32[]{:S(2)}, u32[]{:S(2)}) collective-permute-start(bf16[168,512]{1,0:T(8,128)(2,1)S(1)} %get-tuple-element.90), channel_id=1, source_target_pairs={{0,128},{8,136},{16,144},{24,152},{32,160},{40,168},{48,176},{56,1... | collective-permute-start | bytes 516104 | tf_op jit(solution)/shard_map/ppermute | solution.py:47
Sparse Core Ops, SparseCore 0:
  111.8 42.9 reduce-scatter.1
where the time goes:
time: 176 us; the launch traced here: 175 us
  waiting for transfers between devices  58.1 us (33%)
  starting transfers between devices  39 us (22%)
  Pallas kernels  34.4 us (20%)
  between operations  14.5 us (8%)
  matrix products  12.6 us (7%)
  local copies, waits for them, and re-layouts  10.2 us (6%)
  other arithmetic  6.39 us (4%)
    ppermute x12, waiting for transfers between devices, y_step(): return lax.ppermute(v, 'tp', tp_perm(0, d))  25.2 us
    pallas_call x4, Pallas kernels, with_table(): pl.pallas_call(kernel, out_shape=outs, grid_spec=pltpu.PrefetchScalarGrid...  23.9 us
    ppermute x12, starting transfers between devices, y_step(): return lax.ppermute(v, 'tp', tp_perm(0, d))  17.6 us
    ppermute x4, waiting for transfers between devices, x_swap(): return lax.ppermute(v, 'tp', tp_perm(1, 0))  14.7 us
    ppermute x4, waiting for transfers between devices, from_behind(): return lax.ppermute(block, 'ctx', route)  11.9 us
    ppermute x4, starting transfers between devices, from_behind(): return lax.ppermute(block, 'ctx', route)  11.3 us
    pallas_call x8, Pallas kernels, run(): pl.pallas_call(kernel, out_shape=outs, in_specs=in_specs, out_specs=jax.t...  10.5 us
    ppermute x4, starting transfers between devices, x_swap(): return lax.ppermute(v, 'tp', tp_perm(1, 0))  7.78 us
  transfers between devices with their start and end apart: 27, of which 12 were waited for; matrix products, arithmetic and copies ran while one was open for 10% of the time, Pallas kernels for 19%

commit v1 on v0

--- a/solution.py
+++ b/solution.py
@@ -189,7 +189,7 @@
     out_ref[...] = (mine_ref[...] + got).astype(bf16)
 
 
-def with_table(kernel, us, grid, table, specs, args, outs, out_specs, scratch=()):
+def with_table(kernel, us, grid, table, specs, args, outs, out_specs, scratch=(), alias={}):
     return pl.pallas_call(
         kernel,
         out_shape=outs,
@@ -202,6 +202,7 @@
         ),
         compiler_params=pltpu.CompilerParams(vmem_limit_bytes=56 * 2**20),
         cost_estimate=cost(us),
+        input_output_aliases=alias,
     )(table, *args)
 
 
@@ -244,18 +245,17 @@
     return call(add_last, full, 1.5)(mine, across, below, above), extra
 
 
-def join_kernel(place_ref, xa_ref, oa_ref, xb_ref, ob_ref, xc_ref, oc_ref, out_ref):
+def join_first(table_ref, x_ref, o_ref, out_ref):
+    toks = o_ref.shape[3]
+    for i in range(2):
+        out_ref[0, i, 0, :, :toks] = x_ref[0, i, 0]
+        out_ref[0, i, 0, :, toks:] = o_ref[0, i]
+
+
+def join_rest(table_ref, xb_ref, ob_ref, xc_ref, oc_ref, begun_ref, out_ref):
     step = pl.program_id(0)
-    toks = oa_ref.shape[3]
-
-    def put(x_ref, o_ref):
-        for i in range(2):
-            out_ref[0, i, 0, :, :toks] = x_ref[0, i, 0]
-            out_ref[0, i, 0, :, toks:] = o_ref[0, i]
-
-    pl.when(step < 4)(lambda: put(xa_ref, oa_ref))
-    pl.when((step >= 4) & (step < 7))(lambda: put(xb_ref, ob_ref))
-    pl.when(step == 7)(lambda: put(xc_ref, oc_ref))
+    pl.when(step < 3)(lambda: join_first(table_ref, xb_ref, ob_ref, out_ref))
+    pl.when(step == 3)(lambda: join_first(table_ref, xc_ref, oc_ref, out_ref))
 
 
 def unrotate_norm(grad, raw, gain, cos, sin):
@@ -274,8 +274,13 @@
     return jnp.concatenate([top * cos - bottom * sin, bottom * cos + top * sin], axis=0)
 
 
-def heads_kernel(raw_ref, qg_ref, kg_ref, cos_ref, sin_ref, q_ref, kv_ref):
+def heads_kernel(
+    most_ref, w_ref, last_ref, qg_ref, kg_ref, cos_ref, sin_ref, q_ref, kv_ref, raw_ref
+):
     cos, sin = cos_ref[...], sin_ref[...]
+    raw_ref[...] = most_ref[...] + jnp.dot(
+        w_ref[...], last_ref[...], preferred_element_type=f32
+    )
     for h in range(2):
         rows = slice(h * HD, (h + 1) * HD)
         q_ref[rows, :] = rotate_norm(raw_ref[rows, :], qg_ref[...], cos, sin).astype(bf16)
@@ -377,6 +382,9 @@
     w_cat = jnp.concatenate([w_query, w_key, w_value], axis=1)
     w_own = w_cat.reshape(n_tp, feats, w_cat.shape[1])
 
+    table = jnp.stack([core, *[owner(rel) for rel in RELS + SENT]]).astype(jnp.int32)
+    w_last = lax.dynamic_index_in_dim(w_own, owner(RELS[7]), 0, keepdims=False).T
+
     def project(total, parts, rels):
         for xs, rel in zip(parts, rels):
             ws = lax.dynamic_index_in_dim(w_own, owner(rel), 0, keepdims=False)
@@ -393,44 +401,33 @@
     def beside(parts):
         begun.append(project(None, parts, RELS[:4]))
         begun.append(for_both(parts))
-        return begun[0], *begun[1], cos, sin
+        return begun[0], *begun[1], cos, sin, w_last, table
 
     x_parts = gather_tp(hidden_in.T, beside)
     most = project(begun[0], x_parts[4:7], RELS[4:7])
     xb, ob = for_both(x_parts[4:7])
     last, most, xb, ob = lax.optimization_barrier((x_parts[7], most, xb, ob))
-    raw = project(most, [last], RELS[7:])
-
-    q_t, kv_t = call(heads_kernel, (sds((2 * HD, toks), bf16), sds((2 * HD, toks), bf16)), 1.5)(
-        raw, qg, kg, cos, sin
+
+    low = sds((2 * HD, toks), bf16)
+    q_t, kv_t, raw = call(heads_kernel, (low, low, sds(most.shape, f32)), 2.5)(
+        most, w_last, last, qg, kg, cos, sin
     )
     rings = [[(a * NZ + z) * NC + c for z in range(NZ)] for a in range(NXL) for c in range(NC)]
     xl = j // NZ
-    table = jnp.stack([core, *[owner(rel) for rel in RELS + SENT]]).astype(jnp.int32)
-
-    def join(pairs, table):
-        specs, first = [], 0
-        for x, _ in pairs:
-            at = lambda i, first=first, n=x.shape[0]: jnp.clip(i - first, 0, n - 1)
-            first += x.shape[0]
-            specs.append(
-                pl.BlockSpec(
-                    (1, 2, 1, blk, toks), lambda i, t, at=at: (at(i), 0, t[0], 0, 0)
-                )
-            )
-            specs.append(pl.BlockSpec((1, 2, blk, toks), lambda i, t, at=at: (at(i), 0, 0, 0)))
-        return with_table(
-            join_kernel,
-            6.0,
-            (n_tp,),
-            table,
-            specs,
-            [v for pair in pairs for v in pair],
-            jax.ShapeDtypeStruct((NY, 2, NXH, blk, 2 * toks), bf16),
-            pl.BlockSpec(
-                (1, 2, 1, blk, 2 * toks), lambda i, t: (t[i + 1] % NY, 0, t[i + 1] // NY, 0, 0)
-            ),
-        ).reshape(NZ, NXL * blk, 2 * toks)
+
+    def x_specs(at):
+        return [
+            pl.BlockSpec((1, 2, 1, blk, toks), lambda i, t: (at(i), 0, t[0], 0, 0)),
+            pl.BlockSpec((1, 2, blk, toks), lambda i, t: (at(i), 0, 0, 0)),
+        ]
+
+    def pair_spec(first):
+        return pl.BlockSpec(
+            (1, 2, 1, blk, 2 * toks),
+            lambda i, t: (t[first + i] % NY, 0, t[first + i] // NY, 0, 0),
+        )
+
+    pair_shape = sds((NY, 2, NXH, blk, 2 * toks), bf16)
 
     def along_z(g):
         return lax.psum_scatter(
@@ -447,8 +444,18 @@
     kv1 = from_behind(kv_t, 1)
     kv2 = from_behind(kv_t, 2)
     xa, oa = begun[1]
-    xc, oc = for_both([last])
-    pairs = [(xa, core_swap(oa)), (xb, core_swap(ob)), (xc, core_swap(oc))]
+    joined = with_table(
+        join_first,
+        4.0,
+        (4,),
+        tie((table,), kv_t)[0],
+        x_specs(lambda i: i),
+        (xa, core_swap(oa)),
+        pair_shape,
+        pair_spec(1),
+    )
+    kv2, joined = lax.optimization_barrier((kv2, joined))
+    xc, oc = for_both(tie((last,), kv_t))
     pair = sds((2, toks, HD), bf16)
     dq_raw, d_own, d1, d2 = call(
         attend_kernel,
@@ -464,9 +471,24 @@
     )(ctx[None], q_t, raw, kv_t, kv1, kv2, grad_out, qg, cos, sin)
     r1 = from_behind(d1, -1)
     r2 = from_behind(d2, -2)
-    x_pair = join(pairs, tie((table,), dq_raw)[0])
+    x_pair = with_table(
+        join_rest,
+        4.0,
+        (4,),
+        tie((table,), dq_raw)[0],
+        [
+            *x_specs(lambda i: jnp.minimum(i, 2)),
+            *x_specs(lambda i: 0),
+            pl.BlockSpec(memory_space=pl.ANY),
+        ],
+        (xb, core_swap(ob), xc, core_swap(oc), joined),
+        pair_shape,
+        pair_spec(5),
+        alias={5: 0},
+    ).reshape(NZ, NXL * blk, 2 * toks)
     dq_other = core_swap(dq_raw)
-    r1, r2, x_pair, dq_other = lax.optimization_barrier((r1, r2, x_pair, dq_other))
+    dq_pair = jnp.concatenate([dq_raw, dq_other], axis=1)
+    r1, r2, x_pair, dq_pair = lax.optimization_barrier((r1, r2, x_pair, dq_pair))
     dkv_raw = call(finish_kernel, sds((2 * HD, toks), bf16), 1.3)(
         d_own, r1, r2, raw, kg, cos, sin
     )
@@ -474,12 +496,7 @@
 
     def beside_tail(after):
         here, there, _ = lax.optimization_barrier((dkv_raw, dkv_other, after))
-        d_pair = jnp.concatenate(
-            [
-                jnp.concatenate([dq_raw, dq_other], axis=1),
-                jnp.concatenate([here, there], axis=1),
-            ]
-        )
+        d_pair = jnp.concatenate([dq_pair, jnp.concatenate([here, there], axis=1)])
         g = lax.dot_general(x_pair, d_pair, (((2,), (1,)), ((), ())), preferred_element_type=f32)
         return g.astype(bf16)
 

time: 176 us -> 170 us (0.966)
  waiting for transfers between devices: 58.1 us -> 48 us
  local copies, waits for them, and re-layouts: 10.2 us -> 13.1 us
  Pallas kernels: 34.4 us -> 36.4 us
    ppermute x12, waiting for transfers between devices: 25.2 us -> 20.3 us  [y_step(): return lax.ppermute(v, 'tp', tp_perm(0, d))]
    ppermute x4, waiting for transfers between devices: 14.7 us -> 10.2 us  [x_swap(): return lax.ppermute(v, 'tp', tp_perm(1, 0))]
    ppermute x4, waiting for transfers between devices: 11.9 us -> 8.97 us  [from_behind(): return lax.ppermute(block, 'ctx', route)]
    reduce_scatter x1, waiting for transfers between devices: 6.31 us -> 8.41 us  [along_z(): lax.psum_scatter(g, 'ctx', scatter_dimension=0, tiled=True, axis_index_gr...]
    pallas_call x4 -> x5, Pallas kernels: 23.9 us -> 25.5 us  [with_table(): pl.pallas_call(kernel, out_shape=outs, grid_spec=pltpu.PrefetchScalarGrid...]
    unnamed x40 -> x42, local copies, waits for them, and re-layouts: 5.56 us -> 7.05 us
    dot_general x8 -> x7, matrix products: 7.13 us -> 6.69 us  [project(): lax.dot_general(ws, xs, (((0,), (0,)), ((), ())), preferred_element_type=...]
  transfers between devices with their start and end apart: 27 -> 27, of which waited for: 12 -> 13; matrix products, arithmetic and copies ran while one was open for 10% -> 11% of each run, Pallas kernels for 19% -> 21%
where the time goes in v1:
time: 170 us; the launch traced here: 169 us
  waiting for transfers between devices  48 us (28%)
  starting transfers between devices  39.1 us (23%)
  Pallas kernels  36.4 us (21%)
  between operations  14.5 us (9%)
  local copies, waits for them, and re-layouts  13.1 us (8%)
  matrix products  12.1 us (7%)
  other arithmetic  6.02 us (4%)
    pallas_call x5, Pallas kernels, with_table(): pl.pallas_call(kernel, out_shape=outs, grid_spec=pltpu.PrefetchScalarGrid...  25.5 us
    ppermute x12, waiting for transfers between devices, y_step(): return lax.ppermute(v, 'tp', tp_perm(0, d))  20.3 us
    ppermute x12, starting transfers between devices, y_step(): return lax.ppermute(v, 'tp', tp_perm(0, d))  17.3 us
    ppermute x4, starting transfers between devices, from_behind(): return lax.ppermute(block, 'ctx', route)  12.3 us
    pallas_call x8, Pallas kernels, run(): pl.pallas_call(kernel, out_shape=outs, in_specs=in_specs, out_specs=jax.t...  11 us
    ppermute x4, waiting for transfers between devices, x_swap(): return lax.ppermute(v, 'tp', tp_perm(1, 0))  10.2 us
    ppermute x4, waiting for transfers between devices, from_behind(): return lax.ppermute(block, 'ctx', route)  8.97 us
    reduce_scatter x1, waiting for transfers between devices, along_z(): lax.psum_scatter(g, 'ctx', scatter_dimension=0, tiled=True, axis_index_gr...  8.41 us
  transfers between devices with their start and end apart: 27, of which 13 were waited for; matrix products, arithmetic and copies ran while one was open for 11% of the time, Pallas kernels for 21%

profile of v1, /device:TPU:2, one launch (start us, length us, event | category | flops | bytes accessed | tf_op | source)
XLA Modules:
  0.0 169.2 jit_solution(17761040964733980722)
XLA Ops:
  7.2 2.2 %collective-permute-start.3 = (bf16[672,512]{1,0:T(8,128)(2,1)}, bf16[672,512]{1,0:T(8,128)(2,1)}, u32[]{:S(2)}, u32[]{:S(2)}) collective-permute-start(bf16[672,512]{1,0:T(8,128)(2,1)} %bitcast.90), channel_id=1, source_target_pairs={{0,4},{1,5},{2,6},{3,7},{4,0},{5,1},{6,2},{7,3},{8,12},{9,13},{10,... | collective-permute-start | bytes 2064392 | tf_op jit(solution)/shard_map/ppermute | solution.py:38
  9.4 3.0 %collective-permute-start.1 = (bf16[672,512]{1,0:T(8,128)(2,1)}, bf16[672,512]{1,0:T(8,128)(2,1)S(1)}, u32[]{:S(2)}, u32[]{:S(2)}) collective-permute-start(bf16[672,512]{1,0:T(8,128)(2,1)} %bitcast.91), channel_id=1, source_target_pairs={{0,3},{1,0},{2,1},{3,2},{4,7},{5,4},{6,5},{7,6},{8,11},{9,8},{10,9... | collective-permute-start | bytes 2064392 | tf_op jit(solution)/shard_map/ppermute | solution.py:34
  12.4 3.4 %pad_maximum_fusion = bf16[5376,512]{1,0:T(8,128)(2,1)S(1)} fusion(bf16[5376,128]{1,0:T(8,128)(2,1)} %param.10, bf16[5376,128]{1,0:T(8,128)(2,1)} %param.9, bf16[5376,256]{1,0:T(8,128)(2,1)} %param.8), kind=kLoop, calls=%fused_computation | loop fusion | flops 16515072 | bytes 11010048 | tf_op jit(solution)/shard_map/concatenate | solution.py:382
  15.8 2.4 %copy-done.9 = bf16[5376,512]{1,0:T(8,128)(2,1)} copy-done((bf16[5376,512]{1,0:T(8,128)(2,1)}, bf16[5376,512]{1,0:T(8,128)(2,1)S(1)}, u32[]{:S(2)}) %copy-start.9) | copy-done | bytes 5505048
  19.8 1.9 %fusion.16 = f32[512,512]{1,0:T(8,128)S(1)} fusion(bf16[512,672]{0,1:T(8,128)(2,1)} %param.7, bf16[8,672,512]{2,1,0:T(8,128)(2,1)} %bitcast.72, s32[]{:T(128)S(6)} %select_n.178), kind=kOutput, calls=%fused_computation.33 | convolution fusion | flops 352321536 | bytes 2424836 | tf_op jit(solution)/shard_map/dot_general | solution.py:391
  21.7 5.5 %collective-permute-done.1 = bf16[672,512]{1,0:T(8,128)(2,1)S(1)} collective-permute-done((bf16[672,512]{1,0:T(8,128)(2,1)}, bf16[672,512]{1,0:T(8,128)(2,1)S(1)}, u32[]{:S(2)}, u32[]{:S(2)}) %collective-permute-start.1) | collective-permute-done | bytes 688160 | tf_op jit(solution)/shard_map/ppermute | solution.py:34
  27.2 1.1 fusion.35
  28.3 2.1 %collective-permute-done = bf16[672,512]{1,0:T(8,128)(2,1)S(1)} collective-permute-done((bf16[672,512]{1,0:T(8,128)(2,1)}, bf16[672,512]{1,0:T(8,128)(2,1)S(1)}, u32[]{:S(2)}, u32[]{:S(2)}) %collective-permute-start) | collective-permute-done | bytes 688160 | tf_op jit(solution)/shard_map/ppermute | solution.py:34
  30.8 1.5 collective-permute-start.2
  32.3 3.1 %collective-permute-start.7 = (bf16[672,512]{1,0:T(8,128)(2,1)S(1)}, bf16[672,512]{1,0:T(8,128)(2,1)S(1)}, u32[]{:S(2)}, u32[]{:S(2)}) collective-permute-start(bf16[672,512]{1,0:T(8,128)(2,1)S(1)} %get-tuple-element.104), channel_id=1, source_target_pairs={{0,3},{1,0},{2,1},{3,2},{4,7},{5,4},{6,5},{7,6},{8,11},{9,8},{10,9... | collective-permute-start | bytes 2064392 | tf_op jit(solution)/shard_map/ppermute | solution.py:34
  35.4 1.5 pad_maximum_fusion.1.x_ref
  36.9 1.3 dynamic-slice_bitcast_fusion
  38.9 1.7 %fusion.12 = f32[512,512]{1,0:T(8,128)S(1)} fusion(bf16[672,512]{1,0:T(8,128)(2,1)} %collective-permute-done.3, bf16[8,672,512]{2,1,0:T(8,128)(2,1)S(1)} %bitcast.79, s32[]{:T(128)S(6)} %select_n.181), kind=kOutput, calls=%fused_computation.29 | convolution fusion | flops 352321536 | bytes 2424836 | tf_op jit(solution)/shard_map/dot_general | solution.py:391
  41.2 6.8 %collective-permute-done.2 = bf16[672,512]{1,0:T(8,128)(2,1)S(1)} collective-permute-done((bf16[672,512]{1,0:T(8,128)(2,1)S(1)}, bf16[672,512]{1,0:T(8,128)(2,1)S(1)}, u32[]{:S(2)}, u32[]{:S(2)}) %collective-permute-start.2) | collective-permute-done | bytes 688160 | tf_op jit(solution)/shard_map/ppermute | solution.py:38
  50.4 3.0 %collective-permute-start.5 = (bf16[336,512]{1,0:T(8,128)(2,1)S(1)}, bf16[336,512]{1,0:T(8,128)(2,1)S(1)}, u32[]{:S(2)}, u32[]{:S(2)}) collective-permute-start(bf16[336,512]{1,0:T(8,128)(2,1)S(1)} %get-tuple-element.49), channel_id=1, source_target_pairs={{0,3},{1,0},{2,1},{3,2},{4,7},{5,4},{6,5},{7,6},{8,11},{9,8},{10,9... | collective-permute-start | bytes 1032200 | tf_op jit(solution)/shard_map/ppermute | solution.py:34
  53.7 1.2 dynamic-slice_bitcast_fusion.1
  55.5 3.0 %collective-permute-done.4 = bf16[336,512]{1,0:T(8,128)(2,1)S(1)} collective-permute-done((bf16[336,512]{1,0:T(8,128)(2,1)S(1)}, bf16[336,512]{1,0:T(8,128)(2,1)S(1)}, u32[]{:S(2)}, u32[]{:S(2)}) %collective-permute-start.4) | collective-permute-done | bytes 344096 | tf_op jit(solution)/shard_map/ppermute | solution.py:34
  59.9 4.0 %collective-permute-start.9 = (bf16[256,512]{1,0:T(8,128)(2,1)S(1)}, bf16[256,512]{1,0:T(8,128)(2,1)S(1)}, u32[]{:S(2)}, u32[]{:S(2)}) collective-permute-start(bf16[256,512]{1,0:T(8,128)(2,1)S(1)} %get-tuple-element.54.own_ref), channel_id=1, source_target_pairs={{0,16},{8,24},{16,32},{24,40},{32,48},{40,56},{48,64},{56,72},{64,... | collective-permute-start | bytes 786440 | tf_op jit(solution)/shard_map/ppermute | solution.py:53
  63.8 2.1 %collective-permute-start.8 = (bf16[256,512]{1,0:T(8,128)(2,1)S(1)}, bf16[256,512]{1,0:T(8,128)(2,1)S(1)}, u32[]{:S(2)}, u32[]{:S(2)}) collective-permute-start(bf16[256,512]{1,0:T(8,128)(2,1)S(1)} %get-tuple-element.54.own_ref), channel_id=1, source_target_pairs={{0,8},{8,16},{16,24},{24,32},{32,40},{40,48},{48,56},{56,64},{64,7... | collective-permute-start | bytes 786440 | tf_op jit(solution)/shard_map/ppermute | solution.py:53
  66.0 4.8 %shard_map.103.begun_ref = bf16[4,2,2,168,1024]{4,3,2,1,0:T(8,128)(2,1)} custom-call(s32[17]{0:T(128)} %stack.74.table_ref.own_ref, bf16[4,2,2,168,512]{4,3,2,1,0:T(8,128)(2,1)} %copy-done.11, bf16[4,2,168,512]{3,2,1,0:T(8,128)(2,1)} %collective-permute-done.10.o_ref), custom_call_target="tpu_custom_call" | custom-call | bytes 13600000 | tf_op jit(solution)/shard_map/pallas_call | solution.py:193
  70.7 4.8 %collective-permute-done.9.m2_ref = bf16[256,512]{1,0:T(8,128)(2,1)S(1)} collective-permute-done((bf16[256,512]{1,0:T(8,128)(2,1)S(1)}, bf16[256,512]{1,0:T(8,128)(2,1)S(1)}, u32[]{:S(2)}, u32[]{:S(2)}) %collective-permute-start.9) | collective-permute-done | bytes 262176 | tf_op jit(solution)/shard_map/ppermute | solution.py:53
  75.5 2.6 %collective-permute-done.8.m1_ref = bf16[256,512]{1,0:T(8,128)(2,1)S(1)} collective-permute-done((bf16[256,512]{1,0:T(8,128)(2,1)S(1)}, bf16[256,512]{1,0:T(8,128)(2,1)S(1)}, u32[]{:S(2)}, u32[]{:S(2)}) %collective-permute-start.8) | collective-permute-done | bytes 262176 | tf_op jit(solution)/shard_map/ppermute | solution.py:53
  78.2 5.4 %shard_map.104 = (bf16[256,512]{1,0:T(8,128)(2,1)S(1)}, f32[2,512,128]{2,1,0:T(8,128)S(1)}, bf16[2,512,128]{2,1,0:T(8,128)(2,1)S(1)}, bf16[2,512,128]{2,1,0:T(8,128)(2,1)S(1)}) custom-call(s32[1]{0:T(128)} %bitcast.10.ctx_ref, bf16[256,512]{1,0:T(8,128)(2,1)S(1)} %get-tuple-element.52.q_ref, f32[512,512]{1,0:T(8,128)S(1)} %get-tuple-element.53.raw_ref, ...), custom_call_target="tpu_custom_call" | custom-call | bytes 18700000 | tf_op jit(solution)/shard_map/pallas_call | solution.py:96
  84.3 3.3 %collective-permute-start.11 = (bf16[2,512,128]{2,1,0:T(8,128)(2,1)S(1)}, bf16[2,512,128]{2,1,0:T(8,128)(2,1)S(1)}, u32[]{:S(2)}, u32[]{:S(2)}) collective-permute-start(bf16[2,512,128]{2,1,0:T(8,128)(2,1)S(1)} %get-tuple-element.59), channel_id=1, source_target_pairs={{8,0},{16,8},{24,16},{32,24},{40,32},{48,40},{56,48},{64,56},{72,6... | collective-permute-start | bytes 786440 | tf_op jit(solution)/shard_map/ppermute | solution.py:53
  87.6 2.9 %collective-permute-start.12 = (bf16[2,512,128]{2,1,0:T(8,128)(2,1)S(1)}, bf16[2,512,128]{2,1,0:T(8,128)(2,1)S(1)}, u32[]{:S(2)}, u32[]{:S(2)}) collective-permute-start(bf16[2,512,128]{2,1,0:T(8,128)(2,1)S(1)} %get-tuple-element.60), channel_id=1, source_target_pairs={{16,0},{24,8},{32,16},{40,24},{48,32},{56,40},{64,48},{72,56},{80,... | collective-permute-start | bytes 786440 | tf_op jit(solution)/shard_map/ppermute | solution.py:53
  91.3 4.9 %shard_map.105 = bf16[4,2,2,168,1024]{4,3,2,1,0:T(8,128)(2,1)} custom-call(s32[17]{0:T(128)} %stack.74.table_ref.own_ref, bf16[3,2,2,168,512]{4,3,2,1,0:T(8,128)(2,1)} %copy-done.12, bf16[3,2,168,512]{3,2,1,0:T(8,128)(2,1)} %collective-permute-done.13.ob_ref, bf16[1,2,2,168,512]{4,3,2,1,0:T(8,128)(2,1)} %bitcast.69, ...), custom_call_target="tpu_custom_call", output_to_operand_aliasing={{}: (5, {})} | custom-call | bytes 13600000 | tf_op jit(solution)/shard_map/pallas_call | solution.py:193
  96.2 1.6 collective-permute-done.12.r2_ref
  98.8 3.5 %shard_map.108 = (bf16[336,512]{1,0:T(8,128)(2,1)}, bf16[336,512]{1,0:T(8,128)(2,1)}) custom-call(s32[17]{0:T(128)} %stack.74.table_ref.own_ref, bf16[8,672,512]{2,1,0:T(8,128)(2,1)} %bitcast.73, bf16[256,512]{1,0:T(8,128)(2,1)} %copy-done.1, bf16[256,512]{1,0:T(8,128)(2,1)} %copy-done.2), custom_call_target="tpu_custom_call" | custom-call | bytes 6800000 | tf_op jit(solution)/shard_map/pallas_call | solution.py:193
  102.3 5.4 %convolution_convert_fusion = bf16[8,336,512]{2,1,0:T(8,128)(2,1)} fusion(bf16[8,336,1024]{2,1,0:T(8,128)(2,1)S(1)} %bitcast.84, bf16[256,512]{1,0:T(8,128)(2,1)S(1)} %collective-permute-done.16, bf16[256,512]{1,0:T(8,128)(2,1)} %copy-done.2, bf16[256,1024]{1,0:T(8,128)(2,1)S(1)} %pad_maximum_fusion.10), kind=kOutput, calls=%fused_computation.2 | convolution fusion | flops 2823094272 | bytes 9306112 | tf_op jit(solution)/shard_map/dot_general | solution.py:500
  107.8 0.9 copy-done.18
  108.7 1.5 collective-permute-start.21
  110.2 1.8 %collective-permute-start.20 = (bf16[336,512]{1,0:T(8,128)(2,1)S(1)}, bf16[336,512]{1,0:T(8,128)(2,1)S(1)}, u32[]{:S(2)}, u32[]{:S(2)}) collective-permute-start(bf16[336,512]{1,0:T(8,128)(2,1)S(1)} %copy-done.17), channel_id=1, source_target_pairs={{0,3},{1,0},{2,1},{3,2},{4,7},{5,4},{6,5},{7,6},{8,11},{9,8},{10,9... | collective-permute-start | bytes 1032200 | tf_op jit(solution)/shard_map/ppermute | solution.py:34
  111.9 5.6 %shard_map.109 = (bf16[672,512]{1,0:T(8,128)(2,1)}, bf16[672,512]{1,0:T(8,128)(2,1)}, bf16[672,512]{1,0:T(8,128)(2,1)}) custom-call(s32[17]{0:T(128)} %stack.74.table_ref.own_ref, bf16[8,672,512]{2,1,0:T(8,128)(2,1)} %bitcast.74, bf16[256,512]{1,0:T(8,128)(2,1)} %copy-done.1, bf16[256,512]{1,0:T(8,128)(2,1)} %copy-done.2), custom_call_target="tpu_custom_call" | custom-call | bytes 15300000 | tf_op jit(solution)/shard_map/pallas_call | solution.py:193
  117.5 1.9 %collective-permute-start.17 = (bf16[672,512]{1,0:T(8,128)(2,1)}, bf16[672,512]{1,0:T(8,128)(2,1)S(1)}, u32[]{:S(2)}, u32[]{:S(2)}) collective-permute-start(bf16[672,512]{1,0:T(8,128)(2,1)} %get-tuple-element.75), channel_id=1, source_target_pairs={{0,3},{1,0},{2,1},{3,2},{4,7},{5,4},{6,5},{7,6},{8,11},{9,8},{10,9... | collective-permute-start | bytes 2064392 | tf_op jit(solution)/shard_map/ppermute | solution.py:34
  119.7 1.1 copy-done.6
  121.0 2.1 %collective-permute-start.22 = (bf16[672,512]{1,0:T(8,128)(2,1)S(1)}, bf16[672,512]{1,0:T(8,128)(2,1)S(1)}, u32[]{:S(2)}, u32[]{:S(2)}) collective-permute-start(bf16[672,512]{1,0:T(8,128)(2,1)S(1)} %shard_map.111), channel_id=1, source_target_pairs={{0,4},{1,5},{2,6},{3,7},{4,0},{5,1},{6,2},{7,3},{8,12},{9,13},{10,... | collective-permute-start | bytes 2064392 | tf_op jit(solution)/shard_map/ppermute | solution.py:38
  123.1 6.7 %shard_map.107 = (bf16[672,512]{1,0:T(8,128)(2,1)}, bf16[672,512]{1,0:T(8,128)(2,1)}, bf16[672,512]{1,0:T(8,128)(2,1)}, f32[672,512]{1,0:T(8,128)}) custom-call(s32[17]{0:T(128)} %stack.74.table_ref.own_ref, bf16[8,672,512]{2,1,0:T(8,128)(2,1)} %bitcast.75, bf16[256,512]{1,0:T(8,128)(2,1)} %copy-done.1, bf16[256,512]{1,0:T(8,128)(2,1)} %copy-done.2), custom_call_target="tpu_custom_call" | custom-call | bytes 20400000 | tf_op jit(solution)/shard_map/pallas_call | solution.py:193
  129.8 4.6 %collective-permute-done.17.down_ref = bf16[672,512]{1,0:T(8,128)(2,1)S(1)} collective-permute-done((bf16[672,512]{1,0:T(8,128)(2,1)}, bf16[672,512]{1,0:T(8,128)(2,1)S(1)}, u32[]{:S(2)}, u32[]{:S(2)}) %collective-permute-start.17) | collective-permute-done | bytes 688160 | tf_op jit(solution)/shard_map/ppermute | solution.py:34
  134.4 2.6 %collective-permute-done.18.up_ref = bf16[672,512]{1,0:T(8,128)(2,1)S(1)} collective-permute-done((bf16[672,512]{1,0:T(8,128)(2,1)}, bf16[672,512]{1,0:T(8,128)(2,1)S(1)}, u32[]{:S(2)}, u32[]{:S(2)}) %collective-permute-start.18) | collective-permute-done | bytes 688160 | tf_op jit(solution)/shard_map/ppermute | solution.py:34
  137.0 1.1 copy-done.7
  138.3 2.1 %collective-permute-start.19 = (bf16[672,512]{1,0:T(8,128)(2,1)S(1)}, bf16[672,512]{1,0:T(8,128)(2,1)S(1)}, u32[]{:S(2)}, u32[]{:S(2)}) collective-permute-start(bf16[672,512]{1,0:T(8,128)(2,1)S(1)} %shard_map.110), channel_id=1, source_target_pairs={{0,4},{1,5},{2,6},{3,7},{4,0},{5,1},{6,2},{7,3},{8,12},{9,13},{10,... | collective-permute-start | bytes 2064392 | tf_op jit(solution)/shard_map/ppermute | solution.py:38
  140.4 1.3 shard_map.112
  141.6 1.5 collective-permute-start.23
  143.6 8.4 %reduce-scatter.2.cloned.1.call-done = bf16[1,336,512]{2,1,0:T(8,128)(2,1)} async-done(((bf16[8,336,512]{2,1,0:T(8,128)(2,1)}), bf16[1,336,512]{2,1,0:T(8,128)(2,1)}) %reduce-scatter.2.cloned.1.call-update) | async-done | bytes 344080 | tf_op jit(solution)/shard_map/reduce_scatter | solution.py:433
  152.1 1.0 dynamic-slice_bitcast_fusion.4
  153.7 3.4 %collective-permute-done.19.a_ref = bf16[672,512]{1,0:T(8,128)(2,1)S(1)} collective-permute-done((bf16[672,512]{1,0:T(8,128)(2,1)S(1)}, bf16[672,512]{1,0:T(8,128)(2,1)S(1)}, u32[]{:S(2)}, u32[]{:S(2)}) %collective-permute-start.19) | collective-permute-done | bytes 688160 | tf_op jit(solution)/shard_map/ppermute | solution.py:38
  157.1 2.3 %collective-permute-done.24.c_ref = bf16[672,512]{1,0:T(8,128)(2,1)} collective-permute-done((bf16[672,512]{1,0:T(8,128)(2,1)}, bf16[672,512]{1,0:T(8,128)(2,1)}, u32[]{:S(2)}, u32[]{:S(2)}) %collective-permute-start.24) | collective-permute-done | bytes 688160 | tf_op jit(solution)/shard_map/ppermute | solution.py:34
  159.4 2.2 %shard_map.113 = bf16[672,512]{1,0:T(8,128)(2,1)} custom-call(f32[672,512]{1,0:T(8,128)S(1)} %copy-done.3, bf16[672,512]{1,0:T(8,128)(2,1)S(1)} %collective-permute-done.19.a_ref, bf16[672,512]{1,0:T(8,128)(2,1)S(1)} %collective-permute-done.23.b_ref, bf16[672,512]{1,0:T(8,128)(2,1)} %collective-permute-done.24.c_ref), custom_call_target="tpu_custom_call" | custom-call | bytes 5100000 | tf_op jit(solution)/shard_map/pallas_call | solution.py:96
  (97 shorter events, 12.6 us)
Async XLA Ops:
  7.2 144.9 %reduce-scatter.2.cloned.1.call-start = ((), (), s32[]{:S(2)}) async-start(), calls=%async_computation.1 | async-start | bytes 3096576 | tf_op jit(solution)/shard_map/reduce_scatter | solution.py:433
  7.2 20.0 %collective-permute-start.3 = (bf16[672,512]{1,0:T(8,128)(2,1)}, bf16[672,512]{1,0:T(8,128)(2,1)}, u32[]{:S(2)}, u32[]{:S(2)}) collective-permute-start(bf16[672,512]{1,0:T(8,128)(2,1)} %bitcast.90), channel_id=1, source_target_pairs={{0,4},{1,5},{2,6},{3,7},{4,0},{5,1},{6,2},{7,3},{8,12},{9,13},{10,... | collective-permute-start | bytes 2064392 | tf_op jit(solution)/shard_map/ppermute | solution.py:38
  9.4 17.7 %collective-permute-start.1 = (bf16[672,512]{1,0:T(8,128)(2,1)}, bf16[672,512]{1,0:T(8,128)(2,1)S(1)}, u32[]{:S(2)}, u32[]{:S(2)}) collective-permute-start(bf16[672,512]{1,0:T(8,128)(2,1)} %bitcast.91), channel_id=1, source_target_pairs={{0,3},{1,0},{2,1},{3,2},{4,7},{5,4},{6,5},{7,6},{8,11},{9,8},{10,9... | collective-permute-start | bytes 2064392 | tf_op jit(solution)/shard_map/ppermute | solution.py:34
  12.4 18.0 %collective-permute-start = (bf16[672,512]{1,0:T(8,128)(2,1)}, bf16[672,512]{1,0:T(8,128)(2,1)S(1)}, u32[]{:S(2)}, u32[]{:S(2)}) collective-permute-start(bf16[672,512]{1,0:T(8,128)(2,1)} %bitcast.92), channel_id=1, source_target_pairs={{0,1},{1,2},{2,3},{3,0},{4,5},{5,6},{6,7},{7,4},{8,9},{9,10},{10,1... | collective-permute-start | bytes 2064392 | tf_op jit(solution)/shard_map/ppermute | solution.py:34
  15.8 2.4 %copy-start.9 = (bf16[5376,512]{1,0:T(8,128)(2,1)}, bf16[5376,512]{1,0:T(8,128)(2,1)S(1)}, u32[]{:S(2)}) copy-start(bf16[5376,512]{1,0:T(8,128)(2,1)S(1)} %pad_maximum_fusion) | copy-start | bytes 16515076
  28.3 7.1 %copy-start.13 = (bf16[512,672]{0,1:T(8,128)(2,1)S(1)}, bf16[512,672]{0,1:T(8,128)(2,1)}, u32[]{:S(2)}) copy-start(bf16[512,672]{0,1:T(8,128)(2,1)} %param.7) | copy-start | bytes 2064388
  30.5 7.7 %slice-start = ((s8[5505024]{0:T(1024)(128)(4,1)}), s8[4194304]{0:T(1024)(128)(4,1)S(1)}, s32[]{:S(2)}) async-start(s8[5505024]{0:T(1024)(128)(4,1)} %bitcast.76), calls=%async_computation.2 | async-start | bytes 8388608
  30.7 18.1 %collective-permute-start.6 = (bf16[672,512]{1,0:T(8,128)(2,1)S(1)}, bf16[672,512]{1,0:T(8,128)(2,1)S(1)}, u32[]{:S(2)}, u32[]{:S(2)}) collective-permute-start(bf16[672,512]{1,0:T(8,128)(2,1)S(1)} %get-tuple-element.102), channel_id=1, source_target_pairs={{0,1},{1,2},{2,3},{3,0},{4,5},{5,6},{6,7},{7,4},{8,9},{9,10},{10,1... | collective-permute-start | bytes 2064392 | tf_op jit(solution)/shard_map/ppermute | solution.py:34
  30.8 17.3 %collective-permute-start.2 = (bf16[672,512]{1,0:T(8,128)(2,1)S(1)}, bf16[672,512]{1,0:T(8,128)(2,1)S(1)}, u32[]{:S(2)}, u32[]{:S(2)}) collective-permute-start(bf16[672,512]{1,0:T(8,128)(2,1)S(1)} %get-tuple-element.103), channel_id=1, source_target_pairs={{0,4},{1,5},{2,6},{3,7},{4,0},{5,1},{6,2},{7,3},{8,12},{9,13},{10,... | collective-permute-start | bytes 2064392 | tf_op jit(solution)/shard_map/ppermute | solution.py:38
  32.3 15.8 %collective-permute-start.7 = (bf16[672,512]{1,0:T(8,128)(2,1)S(1)}, bf16[672,512]{1,0:T(8,128)(2,1)S(1)}, u32[]{:S(2)}, u32[]{:S(2)}) collective-permute-start(bf16[672,512]{1,0:T(8,128)(2,1)S(1)} %get-tuple-element.104), channel_id=1, source_target_pairs={{0,3},{1,0},{2,1},{3,2},{4,7},{5,4},{6,5},{7,6},{8,11},{9,8},{10,9... | collective-permute-start | bytes 2064392 | tf_op jit(solution)/shard_map/ppermute | solution.py:34
  35.4 2.8 %slice-start.1 = ((s8[5505024]{0:T(1024)(128)(4,1)}), s8[1310720]{0:T(1024)(128)(4,1)S(1)}, s32[]{:S(2)}) async-start(s8[5505024]{0:T(1024)(128)(4,1)} %bitcast.76), calls=%async_computation.3 | async-start | bytes 2621440
  36.9 2.0 %copy-start.11 = (bf16[4,2,2,168,512]{4,3,2,1,0:T(8,128)(2,1)}, bf16[4,2,2,168,512]{4,3,2,1,0:T(8,128)(2,1)S(1)}, u32[]{:S(2)}) copy-start(bf16[4,2,2,168,512]{4,3,2,1,0:T(8,128)(2,1)S(1)} %pad_maximum_fusion.1.x_ref) | copy-start | bytes 8257540
  38.2 27.8 %collective-permute-start.10 = (bf16[4,2,168,512]{3,2,1,0:T(8,128)(2,1)}, bf16[4,2,168,512]{3,2,1,0:T(8,128)(2,1)}, u32[]{:S(2)}, u32[]{:S(2)}) collective-permute-start(bf16[4,2,168,512]{3,2,1,0:T(8,128)(2,1)} %dynamic-slice_bitcast_fusion), channel_id=1, source_target_pairs={{0,8},{8,0},{16,24},{24,16},{32,40},{40,32},{48,56},{56,48},{64,72... | collective-permute-start | bytes 4128776 | tf_op jit(solution)/shard_map/ppermute | solution.py:42
  49.6 8.9 %collective-permute-start.4 = (bf16[336,512]{1,0:T(8,128)(2,1)S(1)}, bf16[336,512]{1,0:T(8,128)(2,1)S(1)}, u32[]{:S(2)}, u32[]{:S(2)}) collective-permute-start(bf16[336,512]{1,0:T(8,128)(2,1)S(1)} %get-tuple-element.48), channel_id=1, source_target_pairs={{0,1},{1,2},{2,3},{3,0},{4,5},{5,6},{6,7},{7,4},{8,9},{9,10},{10,1... | collective-permute-start | bytes 1032200 | tf_op jit(solution)/shard_map/ppermute | solution.py:34
  50.4 8.1 %collective-permute-start.5 = (bf16[336,512]{1,0:T(8,128)(2,1)S(1)}, bf16[336,512]{1,0:T(8,128)(2,1)S(1)}, u32[]{:S(2)}, u32[]{:S(2)}) collective-permute-start(bf16[336,512]{1,0:T(8,128)(2,1)S(1)} %get-tuple-element.49), channel_id=1, source_target_pairs={{0,3},{1,0},{2,1},{3,2},{4,7},{5,4},{6,5},{7,6},{8,11},{9,8},{10,9... | collective-permute-start | bytes 1032200 | tf_op jit(solution)/shard_map/ppermute | solution.py:34
  53.6 1.9 %copy-start.12 = (bf16[3,2,2,168,512]{4,3,2,1,0:T(8,128)(2,1)}, bf16[3,2,2,168,512]{4,3,2,1,0:T(8,128)(2,1)S(1)}, u32[]{:S(2)}) copy-start(bf16[3,2,2,168,512]{4,3,2,1,0:T(8,128)(2,1)S(1)} %pad_maximum_fusion.2.xb_ref) | copy-start | bytes 6193156
  54.9 4.0 %copy-start.15 = (f32[128]{0:T(128)S(1)}, f32[128]{0:T(128)}, u32[]{:S(2)}) copy-start(f32[128]{0:T(128)} %param.11) | copy-start | bytes 1540
  54.9 4.1 %copy-start.16 = (f32[128]{0:T(128)S(1)}, f32[128]{0:T(128)}, u32[]{:S(2)}) copy-start(f32[128]{0:T(128)} %param.12) | copy-start | bytes 1540
  58.6 25.1 %copy-start = (bf16[672,512]{1,0:T(8,128)(2,1)}, bf16[672,512]{1,0:T(8,128)(2,1)S(1)}, u32[]{:S(2)}) copy-start(bf16[672,512]{1,0:T(8,128)(2,1)S(1)} %pad_maximum_fusion.6.last_ref) | copy-start | bytes 2064388
  58.6 32.0 %collective-permute-start.13 = (bf16[3,2,168,512]{3,2,1,0:T(8,128)(2,1)}, bf16[3,2,168,512]{3,2,1,0:T(8,128)(2,1)}, u32[]{:S(2)}, u32[]{:S(2)}) collective-permute-start(bf16[3,2,168,512]{3,2,1,0:T(8,128)(2,1)} %dynamic-slice_bitcast_fusion.1), channel_id=1, source_target_pairs={{0,8},{8,0},{16,24},{24,16},{32,40},{40,32},{48,56},{56,48},{64,72... | collective-permute-start | bytes 3096584 | tf_op jit(solution)/shard_map/ppermute | solution.py:42
  59.9 18.3 %copy-start.8 = (bf16[512,256]{1,0:T(8,128)(2,1)S(1)}, bf16[512,256]{1,0:T(8,128)(2,1)}, u32[]{:S(2)}) copy-start(bf16[512,256]{1,0:T(8,128)(2,1)} %go_ref.1) | copy-start | bytes 786436
  59.9 15.7 %collective-permute-start.9 = (bf16[256,512]{1,0:T(8,128)(2,1)S(1)}, bf16[256,512]{1,0:T(8,128)(2,1)S(1)}, u32[]{:S(2)}, u32[]{:S(2)}) collective-permute-start(bf16[256,512]{1,0:T(8,128)(2,1)S(1)} %get-tuple-element.54.own_ref), channel_id=1, source_target_pairs={{0,16},{8,24},{16,32},{24,40},{32,48},{40,56},{48,64},{56,72},{64,... | collective-permute-start | bytes 786440 | tf_op jit(solution)/shard_map/ppermute | solution.py:53
  63.8 14.3 %collective-permute-start.8 = (bf16[256,512]{1,0:T(8,128)(2,1)S(1)}, bf16[256,512]{1,0:T(8,128)(2,1)S(1)}, u32[]{:S(2)}, u32[]{:S(2)}) collective-permute-start(bf16[256,512]{1,0:T(8,128)(2,1)S(1)} %get-tuple-element.54.own_ref), channel_id=1, source_target_pairs={{0,8},{8,16},{16,24},{24,32},{32,40},{40,48},{48,56},{56,64},{64,7... | collective-permute-start | bytes 786440 | tf_op jit(solution)/shard_map/ppermute | solution.py:53
  83.6 12.7 %copy-start.1 = (bf16[256,512]{1,0:T(8,128)(2,1)}, bf16[256,512]{1,0:T(8,128)(2,1)S(1)}, u32[]{:S(2)}) copy-start(bf16[256,512]{1,0:T(8,128)(2,1)S(1)} %get-tuple-element.57.dq_ref) | copy-start | bytes 786436
  83.6 6.9 %collective-permute-start.15 = (bf16[256,512]{1,0:T(8,128)(2,1)S(1)}, bf16[256,512]{1,0:T(8,128)(2,1)S(1)}, u32[]{:S(2)}, u32[]{:S(2)}) collective-permute-start(bf16[256,512]{1,0:T(8,128)(2,1)S(1)} %get-tuple-element.57.dq_ref), channel_id=1, source_target_pairs={{0,8},{8,0},{16,24},{24,16},{32,40},{40,32},{48,56},{56,48},{64,72... | collective-permute-start | bytes 786440 | tf_op jit(solution)/shard_map/ppermute | solution.py:42
  83.7 6.8 %collective-permute-start.14 = (bf16[1,2,168,512]{3,2,1,0:T(8,128)(2,1)S(1)}, bf16[1,2,168,512]{3,2,1,0:T(8,128)(2,1)S(1)}, u32[]{:S(2)}, u32[]{:S(2)}) collective-permute-start(bf16[1,2,168,512]{3,2,1,0:T(8,128)(2,1)S(1)} %dynamic-slice_bitcast_fusion.3), channel_id=1, source_target_pairs={{0,8},{8,0},{16,24},{24,16},{32,40},{40,32},{48,56},{56,48},{64,72... | collective-permute-start | bytes 1032200 | tf_op jit(solution)/shard_map/ppermute | solution.py:42
  84.3 11.9 %collective-permute-start.11 = (bf16[2,512,128]{2,1,0:T(8,128)(2,1)S(1)}, bf16[2,512,128]{2,1,0:T(8,128)(2,1)S(1)}, u32[]{:S(2)}, u32[]{:S(2)}) collective-permute-start(bf16[2,512,128]{2,1,0:T(8,128)(2,1)S(1)} %get-tuple-element.59), channel_id=1, source_target_pairs={{8,0},{16,8},{24,16},{32,24},{40,32},{48,40},{56,48},{64,56},{72,6... | collective-permute-start | bytes 786440 | tf_op jit(solution)/shard_map/ppermute | solution.py:53
  87.6 10.2 %collective-permute-start.12 = (bf16[2,512,128]{2,1,0:T(8,128)(2,1)S(1)}, bf16[2,512,128]{2,1,0:T(8,128)(2,1)S(1)}, u32[]{:S(2)}, u32[]{:S(2)}) collective-permute-start(bf16[2,512,128]{2,1,0:T(8,128)(2,1)S(1)} %get-tuple-element.60), channel_id=1, source_target_pairs={{16,0},{24,8},{32,16},{40,24},{48,32},{56,40},{64,48},{72,56},{80,... | collective-permute-start | bytes 786440 | tf_op jit(solution)/shard_map/ppermute | solution.py:53
  90.6 0.7 copy-start.14
  98.1 0.7 copy-start.2
  98.1 4.2 %copy-start.10 = (bf16[4,2,2,168,1024]{4,3,2,1,0:T(8,128)(2,1)S(1)}, bf16[4,2,2,168,1024]{4,3,2,1,0:T(8,128)(2,1)}, u32[]{:S(2)}) copy-start(bf16[4,2,2,168,1024]{4,3,2,1,0:T(8,128)(2,1)} %shard_map.105) | copy-start | bytes 16515076
  98.1 4.2 %collective-permute-start.16 = (bf16[256,512]{1,0:T(8,128)(2,1)S(1)}, bf16[256,512]{1,0:T(8,128)(2,1)S(1)}, u32[]{:S(2)}, u32[]{:S(2)}) collective-permute-start(bf16[256,512]{1,0:T(8,128)(2,1)S(1)} %shard_map.106.dkv_ref), channel_id=1, source_target_pairs={{0,8},{8,0},{16,24},{24,16},{32,40},{40,32},{48,56},{56,48},{64,72... | collective-permute-start | bytes 786440 | tf_op jit(solution)/shard_map/ppermute | solution.py:42
  107.7 1.0 copy-start.18
  107.7 2.4 %copy-start.17 = (bf16[336,512]{1,0:T(8,128)(2,1)S(1)}, bf16[336,512]{1,0:T(8,128)(2,1)}, u32[]{:S(2)}) copy-start(bf16[336,512]{1,0:T(8,128)(2,1)} %get-tuple-element.71) | copy-start | bytes 1032196
  108.7 11.0 %collective-permute-start.21 = (bf16[336,512]{1,0:T(8,128)(2,1)S(1)}, bf16[336,512]{1,0:T(8,128)(2,1)S(1)}, u32[]{:S(2)}, u32[]{:S(2)}) collective-permute-start(bf16[336,512]{1,0:T(8,128)(2,1)S(1)} %copy-done.18), channel_id=1, source_target_pairs={{0,1},{1,2},{2,3},{3,0},{4,5},{5,6},{6,7},{7,4},{8,9},{9,10},{10,1... | collective-permute-start | bytes 1032200 | tf_op jit(solution)/shard_map/ppermute | solution.py:34
  110.2 9.5 %collective-permute-start.20 = (bf16[336,512]{1,0:T(8,128)(2,1)S(1)}, bf16[336,512]{1,0:T(8,128)(2,1)S(1)}, u32[]{:S(2)}, u32[]{:S(2)}) collective-permute-start(bf16[336,512]{1,0:T(8,128)(2,1)S(1)} %copy-done.17), channel_id=1, source_target_pairs={{0,3},{1,0},{2,1},{3,2},{4,7},{5,4},{6,5},{7,6},{8,11},{9,8},{10,9... | collective-permute-start | bytes 1032200 | tf_op jit(solution)/shard_map/ppermute | solution.py:34
  117.5 16.9 %collective-permute-start.17 = (bf16[672,512]{1,0:T(8,128)(2,1)}, bf16[672,512]{1,0:T(8,128)(2,1)S(1)}, u32[]{:S(2)}, u32[]{:S(2)}) collective-permute-start(bf16[672,512]{1,0:T(8,128)(2,1)} %get-tuple-element.75), channel_id=1, source_target_pairs={{0,3},{1,0},{2,1},{3,2},{4,7},{5,4},{6,5},{7,6},{8,11},{9,8},{10,9... | collective-permute-start | bytes 2064392 | tf_op jit(solution)/shard_map/ppermute | solution.py:34
  119.4 17.6 %collective-permute-start.18 = (bf16[672,512]{1,0:T(8,128)(2,1)}, bf16[672,512]{1,0:T(8,128)(2,1)S(1)}, u32[]{:S(2)}, u32[]{:S(2)}) collective-permute-start(bf16[672,512]{1,0:T(8,128)(2,1)} %get-tuple-element.76), channel_id=1, source_target_pairs={{0,1},{1,2},{2,3},{3,0},{4,5},{5,6},{6,7},{7,4},{8,9},{9,10},{10,1... | collective-permute-start | bytes 2064392 | tf_op jit(solution)/shard_map/ppermute | solution.py:34
  119.7 1.1 copy-start.6
  121.0 19.4 %collective-permute-start.22 = (bf16[672,512]{1,0:T(8,128)(2,1)S(1)}, bf16[672,512]{1,0:T(8,128)(2,1)S(1)}, u32[]{:S(2)}, u32[]{:S(2)}) collective-permute-start(bf16[672,512]{1,0:T(8,128)(2,1)S(1)} %shard_map.111), channel_id=1, source_target_pairs={{0,4},{1,5},{2,6},{3,7},{4,0},{5,1},{6,2},{7,3},{8,12},{9,13},{10,... | collective-permute-start | bytes 2064392 | tf_op jit(solution)/shard_map/ppermute | solution.py:38
  129.8 10.6 %copy-start.4 = (bf16[672,512]{1,0:T(8,128)(2,1)S(1)}, bf16[672,512]{1,0:T(8,128)(2,1)}, u32[]{:S(2)}) copy-start(bf16[672,512]{1,0:T(8,128)(2,1)} %get-tuple-element.83.below_ref) | copy-start | bytes 2064388
  129.8 10.6 %copy-start.5 = (bf16[672,512]{1,0:T(8,128)(2,1)S(1)}, bf16[672,512]{1,0:T(8,128)(2,1)}, u32[]{:S(2)}) copy-start(bf16[672,512]{1,0:T(8,128)(2,1)} %get-tuple-element.84.above_ref) | copy-start | bytes 2064388
  137.0 1.1 copy-start.7
  138.3 21.1 %copy-start.3 = (f32[672,512]{1,0:T(8,128)S(1)}, f32[672,512]{1,0:T(8,128)}, u32[]{:S(2)}) copy-start(f32[672,512]{1,0:T(8,128)} %get-tuple-element.68.mine_ref) | copy-start | bytes 4128772
  138.3 18.8 %collective-permute-start.19 = (bf16[672,512]{1,0:T(8,128)(2,1)S(1)}, bf16[672,512]{1,0:T(8,128)(2,1)S(1)}, u32[]{:S(2)}, u32[]{:S(2)}) collective-permute-start(bf16[672,512]{1,0:T(8,128)(2,1)S(1)} %shard_map.110), channel_id=1, source_target_pairs={{0,4},{1,5},{2,6},{3,7},{4,0},{5,1},{6,2},{7,3},{8,12},{9,13},{10,... | collective-permute-start | bytes 2064392 | tf_op jit(solution)/shard_map/ppermute | solution.py:38
  141.6 15.5 %collective-permute-start.23 = (bf16[672,512]{1,0:T(8,128)(2,1)}, bf16[672,512]{1,0:T(8,128)(2,1)S(1)}, u32[]{:S(2)}, u32[]{:S(2)}) collective-permute-start(bf16[672,512]{1,0:T(8,128)(2,1)} %get-tuple-element.87), channel_id=1, source_target_pairs={{0,3},{1,0},{2,1},{3,2},{4,7},{5,4},{6,5},{7,6},{8,11},{9,8},{10,9... | collective-permute-start | bytes 2064392 | tf_op jit(solution)/shard_map/ppermute | solution.py:34
  143.1 16.2 %collective-permute-start.24 = (bf16[672,512]{1,0:T(8,128)(2,1)}, bf16[672,512]{1,0:T(8,128)(2,1)}, u32[]{:S(2)}, u32[]{:S(2)}) collective-permute-start(bf16[672,512]{1,0:T(8,128)(2,1)} %get-tuple-element.88), channel_id=1, source_target_pairs={{0,1},{1,2},{2,3},{3,0},{4,5},{5,6},{6,7},{7,4},{8,9},{9,10},{10,1... | collective-permute-start | bytes 2064392 | tf_op jit(solution)/shard_map/ppermute | solution.py:34
  153.1 8.5 %collective-permute-start.25 = (bf16[168,512]{1,0:T(8,128)(2,1)S(1)}, bf16[168,512]{1,0:T(8,128)(2,1)S(1)}, u32[]{:S(2)}, u32[]{:S(2)}) collective-permute-start(bf16[168,512]{1,0:T(8,128)(2,1)S(1)} %get-tuple-element.100), channel_id=1, source_target_pairs={{0,128},{8,136},{16,144},{24,152},{32,160},{40,168},{48,176},{56,1... | collective-permute-start | bytes 516104 | tf_op jit(solution)/shard_map/ppermute | solution.py:47
Sparse Core Ops, SparseCore 0:
  107.9 44.1 reduce-scatter.1

commit v2 on v1

--- a/solution.py
+++ b/solution.py
@@ -118,23 +118,17 @@
     v_ref[...] = total[:, 3 * HD :]
 
 
-def head_terms(w_ref, dq_ref, dkv_ref):
-    width = dq_ref.shape[0]
-    t = jnp.dot(w_ref[0, :, :width], dq_ref[...], preferred_element_type=f32)
-    return t + jnp.dot(w_ref[0, :, width:], dkv_ref[...], preferred_element_type=f32)
-
-
-def first_terms(own_ref, w_ref, dq_ref, dkv_ref, top_ref, bottom_ref):
-    t = head_terms(w_ref, dq_ref, dkv_ref).astype(bf16)
+def first_terms(own_ref, w_ref, d_ref, top_ref, bottom_ref):
+    t = jnp.dot(w_ref[0], d_ref[...], preferred_element_type=f32).astype(bf16)
     lo, hi = halves(w_ref)
     top_ref[...] = t[lo]
     bottom_ref[...] = t[hi]
 
 
-def second_terms(own_ref, w_ref, dq_ref, dkv_ref, side_ref, down_ref, up_ref):
+def second_terms(own_ref, w_ref, d_ref, side_ref, down_ref, up_ref):
     lo, hi = halves(w_ref)
     i = pl.program_id(0)
-    t = head_terms(w_ref, dq_ref, dkv_ref).astype(bf16)
+    t = jnp.dot(w_ref[0], d_ref[...], preferred_element_type=f32).astype(bf16)
 
     @pl.when(i == 0)
     def _():
@@ -152,9 +146,9 @@
         side_ref[hi, :] = t[hi]
 
 
-def third_terms(own_ref, w_ref, dq_ref, dkv_ref, across_ref, below_ref, above_ref, mine_ref):
+def third_terms(own_ref, w_ref, d_ref, across_ref, below_ref, above_ref, mine_ref):
     i = pl.program_id(0)
-    t = head_terms(w_ref, dq_ref, dkv_ref)
+    t = jnp.dot(w_ref[0], d_ref[...], preferred_element_type=f32)
     for n, ref in enumerate((across_ref, below_ref, above_ref, mine_ref)):
 
         @pl.when(i == n)
@@ -206,9 +200,9 @@
     )(table, *args)
 
 
-def scatter_tp(w_own, dq, dkv, table, beside):
+def scatter_tp(w_own, d_all, table, beside):
     _, feats, cols = w_own.shape
-    toks = dq.shape[1]
+    toks = d_all.shape[1]
     sds = jax.ShapeDtypeStruct
     full, part = sds((feats, toks), bf16), sds((feats // 2, toks), bf16)
 
@@ -222,10 +216,9 @@
             table if after is None else tie((table,), after)[0],
             [
                 pl.BlockSpec((1, feats, cols), lambda i, t: (t[at + i], 0, 0)),
-                whole(dq),
-                whole(dkv),
+                whole(d_all),
             ],
-            (w_own, dq, dkv),
+            (w_own, d_all),
             outs,
             [whole(o) for o in outs],
         )
@@ -294,26 +287,35 @@
 ):
     ctx = ctx_ref[0]
     toks = q_ref.shape[1]
-    sub = 256
+    sub = toks // 2
     cos, sin = cos_ref[...], sin_ref[...]
     blocks = (m2_ref, m1_ref, own_ref)
+
+    def reach(b, i):
+        first = 1 if b == 2 and i == 1 else 0
+        last = 0 if b == 0 and i == 0 else 1
+        return slice(first * sub, (last + 1) * sub), range(first, last + 1)
+
     for h in range(2):
         rows = slice(h * HD, (h + 1) * HD)
         q_t = q_ref[rows, :]
         q = q_t.T
         go = go_ref[:, rows]
         go_t = go.T
-        total = jnp.zeros((1, toks), f32)
-        weighted = jnp.zeros((1, toks), f32)
+        totals, weights = ([jnp.zeros((1, sub), f32)] * 2 for _ in range(2))
+        dqs = [jnp.zeros((HD, sub), f32)] * 2
         for b in range(3):
             k = blocks[b][0:HD, :].T
             v = blocks[b][HD : 2 * HD, :].T
-            for s0 in range(0, toks, sub):
-                at = slice(b * toks + s0, b * toks + s0 + sub)
-                s = jnp.dot(k[s0 : s0 + sub], q_t, preferred_element_type=f32) * query_scale
-                dp = jnp.dot(v[s0 : s0 + sub], go_t, preferred_element_type=f32).astype(bf16)
-                key = lax.broadcasted_iota(jnp.int32, (sub, toks), 0) + s0
-                query = lax.broadcasted_iota(jnp.int32, (sub, toks), 1)
+            for i in range(2):
+                at = slice(b * toks + i * sub, b * toks + (i + 1) * sub)
+                own = slice(i * sub, (i + 1) * sub)
+                cols, spans = reach(b, i)
+                width = cols.stop - cols.start
+                s = jnp.dot(k[own], q_t[:, cols], preferred_element_type=f32) * query_scale
+                dp = jnp.dot(v[own], go_t[:, cols], preferred_element_type=f32).astype(bf16)
+                key = lax.broadcasted_iota(jnp.int32, (sub, width), 0) + i * sub
+                query = lax.broadcasted_iota(jnp.int32, (sub, width), 1) + cols.start
                 if b == 0:
                     inside = (key > query) & (ctx >= 2)
                 elif b == 1:
@@ -321,43 +323,51 @@
                 else:
                     inside = key <= query
                 e = jnp.where(inside, jnp.exp(s), 0.0)
-                e_s[at, :] = e
-                dp_s[at, :] = dp
-                total = total + jnp.sum(e, axis=0, keepdims=True)
-                weighted = weighted + jnp.sum(e * dp.astype(f32), axis=0, keepdims=True)
-        inv = 1.0 / total
-        weighted = weighted * inv
-        dq_t = jnp.zeros((HD, toks), f32)
+                e_s[at, cols] = e
+                dp_s[at, cols] = dp
+                part = jnp.sum(e, axis=0, keepdims=True)
+                share = jnp.sum(e * dp.astype(f32), axis=0, keepdims=True)
+                for n, j in enumerate(spans):
+                    here = slice(n * sub, (n + 1) * sub)
+                    totals[j] = totals[j] + part[:, here]
+                    weights[j] = weights[j] + share[:, here]
+        inv = 1.0 / jnp.concatenate(totals, axis=1)
+        weighted = jnp.concatenate(weights, axis=1) * inv
         for b in range(3):
-            for s0 in range(0, toks, sub):
-                at = slice(b * toks + s0, b * toks + s0 + sub)
-                p = e_s[at, :] * inv
-                ds = (p * (dp_s[at, :].astype(f32) - weighted) * query_scale).astype(bf16)
-                dv = jnp.dot(p.astype(bf16), go, preferred_element_type=f32)
-                dk = jnp.dot(ds, q, preferred_element_type=f32)
-                dq_t = dq_t + jnp.dot(
-                    blocks[b][0:HD, s0 : s0 + sub], ds, preferred_element_type=f32
-                )
+            for i in range(2):
+                at = slice(b * toks + i * sub, b * toks + (i + 1) * sub)
+                own = slice(i * sub, (i + 1) * sub)
+                cols, spans = reach(b, i)
+                p = e_s[at, cols] * inv[:, cols]
+                ds = p * (dp_s[at, cols].astype(f32) - weighted[:, cols]) * query_scale
+                ds = ds.astype(bf16)
+                dv = jnp.dot(p.astype(bf16), go[cols], preferred_element_type=f32)
+                dk = jnp.dot(ds, q[cols], preferred_element_type=f32)
+                more = jnp.dot(blocks[b][0:HD, own], ds, preferred_element_type=f32)
+                for n, j in enumerate(spans):
+                    dqs[j] = dqs[j] + more[:, n * sub : (n + 1) * sub]
                 if h == 0:
                     dk_s[at, :] = dk
                     dv_s[at, :] = dv
                 else:
                     out = (d_m2_ref, d_m1_ref, d_own_ref)[b]
-                    out[0, s0 : s0 + sub, :] = (dk_s[at, :] + dk).astype(out.dtype)
-                    out[1, s0 : s0 + sub, :] = (dv_s[at, :] + dv).astype(out.dtype)
+                    out[0, own, :] = (dk_s[at, :] + dk).astype(out.dtype)
+                    out[1, own, :] = (dv_s[at, :] + dv).astype(out.dtype)
+        dq_t = jnp.concatenate(dqs, axis=1)
         dq_low = dq_t.astype(bf16).astype(f32)
         dq_ref[rows, :] = unrotate_norm(dq_low, raw_ref[rows, :], qg_ref[...], cos, sin).astype(bf16)
 
 
-def finish_kernel(own_ref, r1_ref, r2_ref, raw_ref, kg_ref, cos_ref, sin_ref, out_ref):
+def finish_kernel(dq_ref, own_ref, r1_ref, r2_ref, raw_ref, kg_ref, cos_ref, sin_ref, out_ref):
     def total(i):
         t = own_ref[i] + r1_ref[i].astype(f32) + r2_ref[i].astype(f32)
         return t.T.astype(bf16).astype(f32)
 
-    out_ref[0:HD, :] = unrotate_norm(
+    out_ref[0 : 2 * HD, :] = dq_ref[...]
+    out_ref[2 * HD : 3 * HD, :] = unrotate_norm(
         total(0), raw_ref[2 * HD : 3 * HD, :], kg_ref[...], cos_ref[...], sin_ref[...]
     ).astype(bf16)
-    out_ref[HD : 2 * HD, :] = total(1).astype(bf16)
+    out_ref[3 * HD : 4 * HD, :] = total(1).astype(bf16)
 
 
 def shards(hidden_in, w_query, w_key, w_value, q_gain, k_gain, grad_out):
@@ -486,21 +496,19 @@
         pair_spec(5),
         alias={5: 0},
     ).reshape(NZ, NXL * blk, 2 * toks)
-    dq_other = core_swap(dq_raw)
-    dq_pair = jnp.concatenate([dq_raw, dq_other], axis=1)
-    r1, r2, x_pair, dq_pair = lax.optimization_barrier((r1, r2, x_pair, dq_pair))
-    dkv_raw = call(finish_kernel, sds((2 * HD, toks), bf16), 1.3)(
-        d_own, r1, r2, raw, kg, cos, sin
+    r1, r2, x_pair = lax.optimization_barrier((r1, r2, x_pair))
+    d_all = call(finish_kernel, sds((4 * HD, toks), bf16), 1.3)(
+        dq_raw, d_own, r1, r2, raw, kg, cos, sin
     )
-    dkv_other = core_swap(dkv_raw)
+    d_other = core_swap(d_all)
 
     def beside_tail(after):
-        here, there, _ = lax.optimization_barrier((dkv_raw, dkv_other, after))
-        d_pair = jnp.concatenate([dq_pair, jnp.concatenate([here, there], axis=1)])
+        here, there, _ = lax.optimization_barrier((d_all, d_other, after))
+        d_pair = jnp.concatenate([here, there], axis=1)
         g = lax.dot_general(x_pair, d_pair, (((2,), (1,)), ((), ())), preferred_element_type=f32)
         return g.astype(bf16)
 
-    grad_input, g = scatter_tp(w_own, dq_raw, dkv_raw, table, beside_tail)
+    grad_input, g = scatter_tp(w_own, d_all, table, beside_tail)
     grad_input = grad_input.T
     grad_w = across_x(along_z(g))
     return (grad_input, *grad_w)

time: 170 us -> 168 us (0.988)
  waiting for transfers between devices: 48 us -> 45.9 us
    ppermute x4, waiting for transfers between devices: 8.97 us -> 6.82 us  [from_behind(): return lax.ppermute(block, 'ctx', route)]
    unnamed x42 -> x40, local copies, waits for them, and re-layouts: 7.05 us -> 7.12 us
  transfers between devices with their start and end apart: 27 -> 26, of which waited for: 13 -> 13; matrix products, arithmetic and copies ran while one was open for 11% -> 11% of each run, Pallas kernels for 21% -> 21%
where the time goes in v2:
time: 168 us; the launch traced here: 167 us
  waiting for transfers between devices  45.9 us (27%)
  starting transfers between devices  39.6 us (24%)
  Pallas kernels  36 us (21%)
  between operations  14.5 us (9%)
  local copies, waits for them, and re-layouts  13.2 us (8%)
  matrix products  12.2 us (7%)
  other arithmetic  5.96 us (4%)
    pallas_call x5, Pallas kernels, with_table(): pl.pallas_call(kernel, out_shape=outs, grid_spec=pltpu.PrefetchScalarGrid...  25.4 us
    ppermute x12, waiting for transfers between devices, y_step(): return lax.ppermute(v, 'tp', tp_perm(0, d))  20.3 us
    ppermute x12, starting transfers between devices, y_step(): return lax.ppermute(v, 'tp', tp_perm(0, d))  17.3 us
    ppermute x4, starting transfers between devices, from_behind(): return lax.ppermute(block, 'ctx', route)  11.5 us
    pallas_call x8, Pallas kernels, run(): pl.pallas_call(kernel, out_shape=outs, in_specs=in_specs, out_specs=jax.t...  10.6 us
    ppermute x4, waiting for transfers between devices, x_swap(): return lax.ppermute(v, 'tp', tp_perm(1, 0))  10.2 us
    reduce_scatter x1, waiting for transfers between devices, along_z(): lax.psum_scatter(g, 'ctx', scatter_dimension=0, tiled=True, axis_index_gr...  8.47 us
    ppermute x4, starting transfers between devices, x_swap(): return lax.ppermute(v, 'tp', tp_perm(1, 0))  7.89 us
  transfers between devices with their start and end apart: 26, of which 13 were waited for; matrix products, arithmetic and copies ran while one was open for 11% of the time, Pallas kernels for 21%

profile of v2, /device:TPU:2, one launch (start us, length us, event | category | flops | bytes accessed | tf_op | source)
XLA Modules:
  0.0 167.2 jit_solution(17595177889671283615)
XLA Ops:
  7.2 2.2 %collective-permute-start.3 = (bf16[672,512]{1,0:T(8,128)(2,1)}, bf16[672,512]{1,0:T(8,128)(2,1)}, u32[]{:S(2)}, u32[]{:S(2)}) collective-permute-start(bf16[672,512]{1,0:T(8,128)(2,1)} %bitcast.90), channel_id=1, source_target_pairs={{0,4},{1,5},{2,6},{3,7},{4,0},{5,1},{6,2},{7,3},{8,12},{9,13},{10,... | collective-permute-start | bytes 2064392 | tf_op jit(solution)/shard_map/ppermute | solution.py:38
  9.4 3.0 %collective-permute-start.1 = (bf16[672,512]{1,0:T(8,128)(2,1)}, bf16[672,512]{1,0:T(8,128)(2,1)S(1)}, u32[]{:S(2)}, u32[]{:S(2)}) collective-permute-start(bf16[672,512]{1,0:T(8,128)(2,1)} %bitcast.91), channel_id=1, source_target_pairs={{0,3},{1,0},{2,1},{3,2},{4,7},{5,4},{6,5},{7,6},{8,11},{9,8},{10,9... | collective-permute-start | bytes 2064392 | tf_op jit(solution)/shard_map/ppermute | solution.py:34
  12.4 3.4 %pad_maximum_fusion = bf16[5376,512]{1,0:T(8,128)(2,1)S(1)} fusion(bf16[5376,128]{1,0:T(8,128)(2,1)} %param.10, bf16[5376,128]{1,0:T(8,128)(2,1)} %param.9, bf16[5376,256]{1,0:T(8,128)(2,1)} %param.8), kind=kLoop, calls=%fused_computation | loop fusion | flops 16515072 | bytes 11010048 | tf_op jit(solution)/shard_map/concatenate | solution.py:392
  15.8 2.4 %copy-done.8 = bf16[5376,512]{1,0:T(8,128)(2,1)} copy-done((bf16[5376,512]{1,0:T(8,128)(2,1)}, bf16[5376,512]{1,0:T(8,128)(2,1)S(1)}, u32[]{:S(2)}) %copy-start.8) | copy-done | bytes 5505048
  19.8 1.9 %fusion.14 = f32[512,512]{1,0:T(8,128)S(1)} fusion(bf16[512,672]{0,1:T(8,128)(2,1)} %param.7, bf16[8,672,512]{2,1,0:T(8,128)(2,1)} %bitcast.72, s32[]{:T(128)S(6)} %select_n.178), kind=kOutput, calls=%fused_computation.31 | convolution fusion | flops 352321536 | bytes 2424836 | tf_op jit(solution)/shard_map/dot_general | solution.py:401
  21.7 5.4 %collective-permute-done.1 = bf16[672,512]{1,0:T(8,128)(2,1)S(1)} collective-permute-done((bf16[672,512]{1,0:T(8,128)(2,1)}, bf16[672,512]{1,0:T(8,128)(2,1)S(1)}, u32[]{:S(2)}, u32[]{:S(2)}) %collective-permute-start.1) | collective-permute-done | bytes 688160 | tf_op jit(solution)/shard_map/ppermute | solution.py:34
  27.2 1.1 fusion.33
  28.3 2.1 %collective-permute-done = bf16[672,512]{1,0:T(8,128)(2,1)S(1)} collective-permute-done((bf16[672,512]{1,0:T(8,128)(2,1)}, bf16[672,512]{1,0:T(8,128)(2,1)S(1)}, u32[]{:S(2)}, u32[]{:S(2)}) %collective-permute-start) | collective-permute-done | bytes 688160 | tf_op jit(solution)/shard_map/ppermute | solution.py:34
  30.8 1.5 collective-permute-start.2
  32.3 3.1 %collective-permute-start.7 = (bf16[672,512]{1,0:T(8,128)(2,1)S(1)}, bf16[672,512]{1,0:T(8,128)(2,1)S(1)}, u32[]{:S(2)}, u32[]{:S(2)}) collective-permute-start(bf16[672,512]{1,0:T(8,128)(2,1)S(1)} %get-tuple-element.102), channel_id=1, source_target_pairs={{0,3},{1,0},{2,1},{3,2},{4,7},{5,4},{6,5},{7,6},{8,11},{9,8},{10,9... | collective-permute-start | bytes 2064392 | tf_op jit(solution)/shard_map/ppermute | solution.py:34
  35.4 1.5 pad_maximum_fusion.1.x_ref
  36.9 1.3 dynamic-slice_bitcast_fusion
  38.9 1.7 %fusion.10 = f32[512,512]{1,0:T(8,128)S(1)} fusion(bf16[672,512]{1,0:T(8,128)(2,1)} %collective-permute-done.3, bf16[8,672,512]{2,1,0:T(8,128)(2,1)S(1)} %bitcast.79, s32[]{:T(128)S(6)} %select_n.181), kind=kOutput, calls=%fused_computation.27 | convolution fusion | flops 352321536 | bytes 2424836 | tf_op jit(solution)/shard_map/dot_general | solution.py:401
  41.2 6.8 %collective-permute-done.2 = bf16[672,512]{1,0:T(8,128)(2,1)S(1)} collective-permute-done((bf16[672,512]{1,0:T(8,128)(2,1)S(1)}, bf16[672,512]{1,0:T(8,128)(2,1)S(1)}, u32[]{:S(2)}, u32[]{:S(2)}) %collective-permute-start.2) | collective-permute-done | bytes 688160 | tf_op jit(solution)/shard_map/ppermute | solution.py:38
  50.4 3.0 %collective-permute-start.5 = (bf16[336,512]{1,0:T(8,128)(2,1)S(1)}, bf16[336,512]{1,0:T(8,128)(2,1)S(1)}, u32[]{:S(2)}, u32[]{:S(2)}) collective-permute-start(bf16[336,512]{1,0:T(8,128)(2,1)S(1)} %get-tuple-element.48), channel_id=1, source_target_pairs={{0,3},{1,0},{2,1},{3,2},{4,7},{5,4},{6,5},{7,6},{8,11},{9,8},{10,9... | collective-permute-start | bytes 1032200 | tf_op jit(solution)/shard_map/ppermute | solution.py:34
  53.7 1.2 dynamic-slice_bitcast_fusion.1
  55.5 3.0 %collective-permute-done.4 = bf16[336,512]{1,0:T(8,128)(2,1)S(1)} collective-permute-done((bf16[336,512]{1,0:T(8,128)(2,1)S(1)}, bf16[336,512]{1,0:T(8,128)(2,1)S(1)}, u32[]{:S(2)}, u32[]{:S(2)}) %collective-permute-start.4) | collective-permute-done | bytes 344096 | tf_op jit(solution)/shard_map/ppermute | solution.py:34
  59.9 3.8 %collective-permute-start.9 = (bf16[256,512]{1,0:T(8,128)(2,1)S(1)}, bf16[256,512]{1,0:T(8,128)(2,1)S(1)}, u32[]{:S(2)}, u32[]{:S(2)}) collective-permute-start(bf16[256,512]{1,0:T(8,128)(2,1)S(1)} %get-tuple-element.53.own_ref), channel_id=1, source_target_pairs={{0,16},{8,24},{16,32},{24,40},{32,48},{40,56},{48,64},{56,72},{64,... | collective-permute-start | bytes 786440 | tf_op jit(solution)/shard_map/ppermute | solution.py:53
  63.7 2.1 %collective-permute-start.8 = (bf16[256,512]{1,0:T(8,128)(2,1)S(1)}, bf16[256,512]{1,0:T(8,128)(2,1)S(1)}, u32[]{:S(2)}, u32[]{:S(2)}) collective-permute-start(bf16[256,512]{1,0:T(8,128)(2,1)S(1)} %get-tuple-element.53.own_ref), channel_id=1, source_target_pairs={{0,8},{8,16},{16,24},{24,32},{32,40},{40,48},{48,56},{56,64},{64,7... | collective-permute-start | bytes 786440 | tf_op jit(solution)/shard_map/ppermute | solution.py:53
  65.9 1.9 %collective-permute-start.14 = (bf16[1,2,168,512]{3,2,1,0:T(8,128)(2,1)S(1)}, bf16[1,2,168,512]{3,2,1,0:T(8,128)(2,1)S(1)}, u32[]{:S(2)}, u32[]{:S(2)}) collective-permute-start(bf16[1,2,168,512]{3,2,1,0:T(8,128)(2,1)S(1)} %dynamic-slice_bitcast_fusion.3), channel_id=1, source_target_pairs={{0,8},{8,0},{16,24},{24,16},{32,40},{40,32},{48,56},{56,48},{64,72... | collective-permute-start | bytes 1032200 | tf_op jit(solution)/shard_map/ppermute | solution.py:42
  67.8 4.7 %shard_map.103.begun_ref = bf16[4,2,2,168,1024]{4,3,2,1,0:T(8,128)(2,1)} custom-call(s32[17]{0:T(128)} %stack.74.table_ref.own_ref, bf16[4,2,2,168,512]{4,3,2,1,0:T(8,128)(2,1)} %copy-done.10, bf16[4,2,168,512]{3,2,1,0:T(8,128)(2,1)} %collective-permute-done.10.o_ref), custom_call_target="tpu_custom_call" | custom-call | bytes 13600000 | tf_op jit(solution)/shard_map/pallas_call | solution.py:187
  72.5 2.9 %collective-permute-done.9.m2_ref = bf16[256,512]{1,0:T(8,128)(2,1)S(1)} collective-permute-done((bf16[256,512]{1,0:T(8,128)(2,1)S(1)}, bf16[256,512]{1,0:T(8,128)(2,1)S(1)}, u32[]{:S(2)}, u32[]{:S(2)}) %collective-permute-start.9) | collective-permute-done | bytes 262176 | tf_op jit(solution)/shard_map/ppermute | solution.py:53
  75.4 2.6 %collective-permute-done.8.m1_ref = bf16[256,512]{1,0:T(8,128)(2,1)S(1)} collective-permute-done((bf16[256,512]{1,0:T(8,128)(2,1)S(1)}, bf16[256,512]{1,0:T(8,128)(2,1)S(1)}, u32[]{:S(2)}, u32[]{:S(2)}) %collective-permute-start.8) | collective-permute-done | bytes 262176 | tf_op jit(solution)/shard_map/ppermute | solution.py:53
  78.0 5.0 %shard_map.104 = (bf16[256,512]{1,0:T(8,128)(2,1)S(1)}, f32[2,512,128]{2,1,0:T(8,128)S(1)}, bf16[2,512,128]{2,1,0:T(8,128)(2,1)S(1)}, bf16[2,512,128]{2,1,0:T(8,128)(2,1)S(1)}) custom-call(s32[1]{0:T(128)} %bitcast.10.ctx_ref, bf16[256,512]{1,0:T(8,128)(2,1)S(1)} %get-tuple-element.51.q_ref, f32[512,512]{1,0:T(8,128)S(1)} %get-tuple-element.52.raw_ref, ...), custom_call_target="tpu_custom_call" | custom-call | bytes 18700000 | tf_op jit(solution)/shard_map/pallas_call | solution.py:96
  83.0 1.9 %collective-permute-start.11 = (bf16[2,512,128]{2,1,0:T(8,128)(2,1)S(1)}, bf16[2,512,128]{2,1,0:T(8,128)(2,1)S(1)}, u32[]{:S(2)}, u32[]{:S(2)}) collective-permute-start(bf16[2,512,128]{2,1,0:T(8,128)(2,1)S(1)} %get-tuple-element.58), channel_id=1, source_target_pairs={{8,0},{16,8},{24,16},{32,24},{40,32},{48,40},{56,48},{64,56},{72,6... | collective-permute-start | bytes 786440 | tf_op jit(solution)/shard_map/ppermute | solution.py:53
  85.0 3.6 %collective-permute-start.12 = (bf16[2,512,128]{2,1,0:T(8,128)(2,1)S(1)}, bf16[2,512,128]{2,1,0:T(8,128)(2,1)S(1)}, u32[]{:S(2)}, u32[]{:S(2)}) collective-permute-start(bf16[2,512,128]{2,1,0:T(8,128)(2,1)S(1)} %get-tuple-element.59), channel_id=1, source_target_pairs={{16,0},{24,8},{32,16},{40,24},{48,32},{56,40},{64,48},{72,56},{80,... | collective-permute-start | bytes 786440 | tf_op jit(solution)/shard_map/ppermute | solution.py:53
  89.3 4.9 %shard_map.105 = bf16[4,2,2,168,1024]{4,3,2,1,0:T(8,128)(2,1)} custom-call(s32[17]{0:T(128)} %stack.74.table_ref.own_ref, bf16[3,2,2,168,512]{4,3,2,1,0:T(8,128)(2,1)} %copy-done.11, bf16[3,2,168,512]{3,2,1,0:T(8,128)(2,1)} %collective-permute-done.13.ob_ref, bf16[1,2,2,168,512]{4,3,2,1,0:T(8,128)(2,1)} %bitcast.69, ...), custom_call_target="tpu_custom_call", output_to_operand_aliasing={{}: (5, {})} | custom-call | bytes 13600000 | tf_op jit(solution)/shard_map/pallas_call | solution.py:187
  94.2 1.3 collective-permute-done.12.r2_ref
  96.6 3.5 %shard_map.108 = (bf16[336,512]{1,0:T(8,128)(2,1)}, bf16[336,512]{1,0:T(8,128)(2,1)}) custom-call(s32[17]{0:T(128)} %stack.74.table_ref.own_ref, bf16[8,672,512]{2,1,0:T(8,128)(2,1)} %bitcast.73, bf16[512,512]{1,0:T(8,128)(2,1)} %copy-done.1), custom_call_target="tpu_custom_call" | custom-call | bytes 6800000 | tf_op jit(solution)/shard_map/pallas_call | solution.py:187
  100.2 5.5 %convolution_convert_fusion = bf16[8,336,512]{2,1,0:T(8,128)(2,1)} fusion(bf16[8,336,1024]{2,1,0:T(8,128)(2,1)S(1)} %bitcast.84, bf16[512,512]{1,0:T(8,128)(2,1)S(1)} %collective-permute-done.15, bf16[512,512]{1,0:T(8,128)(2,1)} %copy-done.1), kind=kOutput, calls=%fused_computation.2 | convolution fusion | flops 2822045696 | bytes 9306112 | tf_op jit(solution)/shard_map/dot_general | solution.py:508
  106.7 1.5 collective-permute-start.20
  108.1 1.8 %collective-permute-start.19 = (bf16[336,512]{1,0:T(8,128)(2,1)S(1)}, bf16[336,512]{1,0:T(8,128)(2,1)S(1)}, u32[]{:S(2)}, u32[]{:S(2)}) collective-permute-start(bf16[336,512]{1,0:T(8,128)(2,1)S(1)} %copy-done.16), channel_id=1, source_target_pairs={{0,3},{1,0},{2,1},{3,2},{4,7},{5,4},{6,5},{7,6},{8,11},{9,8},{10,9... | collective-permute-start | bytes 1032200 | tf_op jit(solution)/shard_map/ppermute | solution.py:34
  109.9 5.6 %shard_map.109 = (bf16[672,512]{1,0:T(8,128)(2,1)}, bf16[672,512]{1,0:T(8,128)(2,1)}, bf16[672,512]{1,0:T(8,128)(2,1)}) custom-call(s32[17]{0:T(128)} %stack.74.table_ref.own_ref, bf16[8,672,512]{2,1,0:T(8,128)(2,1)} %bitcast.74, bf16[512,512]{1,0:T(8,128)(2,1)} %copy-done.1), custom_call_target="tpu_custom_call" | custom-call | bytes 15300000 | tf_op jit(solution)/shard_map/pallas_call | solution.py:187
  115.5 1.9 %collective-permute-start.16 = (bf16[672,512]{1,0:T(8,128)(2,1)}, bf16[672,512]{1,0:T(8,128)(2,1)S(1)}, u32[]{:S(2)}, u32[]{:S(2)}) collective-permute-start(bf16[672,512]{1,0:T(8,128)(2,1)} %get-tuple-element.73), channel_id=1, source_target_pairs={{0,3},{1,0},{2,1},{3,2},{4,7},{5,4},{6,5},{7,6},{8,11},{9,8},{10,9... | collective-permute-start | bytes 2064392 | tf_op jit(solution)/shard_map/ppermute | solution.py:34
  117.7 1.1 copy-done.5
  119.0 2.1 %collective-permute-start.21 = (bf16[672,512]{1,0:T(8,128)(2,1)S(1)}, bf16[672,512]{1,0:T(8,128)(2,1)S(1)}, u32[]{:S(2)}, u32[]{:S(2)}) collective-permute-start(bf16[672,512]{1,0:T(8,128)(2,1)S(1)} %shard_map.111), channel_id=1, source_target_pairs={{0,4},{1,5},{2,6},{3,7},{4,0},{5,1},{6,2},{7,3},{8,12},{9,13},{10,... | collective-permute-start | bytes 2064392 | tf_op jit(solution)/shard_map/ppermute | solution.py:38
  121.0 6.7 %shard_map.107 = (bf16[672,512]{1,0:T(8,128)(2,1)}, bf16[672,512]{1,0:T(8,128)(2,1)}, bf16[672,512]{1,0:T(8,128)(2,1)}, f32[672,512]{1,0:T(8,128)}) custom-call(s32[17]{0:T(128)} %stack.74.table_ref.own_ref, bf16[8,672,512]{2,1,0:T(8,128)(2,1)} %bitcast.75, bf16[512,512]{1,0:T(8,128)(2,1)} %copy-done.1), custom_call_target="tpu_custom_call" | custom-call | bytes 20400000 | tf_op jit(solution)/shard_map/pallas_call | solution.py:187
  127.7 4.7 %collective-permute-done.16.down_ref = bf16[672,512]{1,0:T(8,128)(2,1)S(1)} collective-permute-done((bf16[672,512]{1,0:T(8,128)(2,1)}, bf16[672,512]{1,0:T(8,128)(2,1)S(1)}, u32[]{:S(2)}, u32[]{:S(2)}) %collective-permute-start.16) | collective-permute-done | bytes 688160 | tf_op jit(solution)/shard_map/ppermute | solution.py:34
  132.4 2.6 %collective-permute-done.17.up_ref = bf16[672,512]{1,0:T(8,128)(2,1)S(1)} collective-permute-done((bf16[672,512]{1,0:T(8,128)(2,1)}, bf16[672,512]{1,0:T(8,128)(2,1)S(1)}, u32[]{:S(2)}, u32[]{:S(2)}) %collective-permute-start.17) | collective-permute-done | bytes 688160 | tf_op jit(solution)/shard_map/ppermute | solution.py:34
  135.0 1.1 copy-done.6
  136.3 2.1 %collective-permute-start.18 = (bf16[672,512]{1,0:T(8,128)(2,1)S(1)}, bf16[672,512]{1,0:T(8,128)(2,1)S(1)}, u32[]{:S(2)}, u32[]{:S(2)}) collective-permute-start(bf16[672,512]{1,0:T(8,128)(2,1)S(1)} %shard_map.110), channel_id=1, source_target_pairs={{0,4},{1,5},{2,6},{3,7},{4,0},{5,1},{6,2},{7,3},{8,12},{9,13},{10,... | collective-permute-start | bytes 2064392 | tf_op jit(solution)/shard_map/ppermute | solution.py:38
  138.4 1.2 shard_map.112
  139.6 1.5 collective-permute-start.22
  141.6 8.5 %reduce-scatter.2.cloned.1.call-done = bf16[1,336,512]{2,1,0:T(8,128)(2,1)} async-done(((bf16[8,336,512]{2,1,0:T(8,128)(2,1)}), bf16[1,336,512]{2,1,0:T(8,128)(2,1)}) %reduce-scatter.2.cloned.1.call-update) | async-done | bytes 344080 | tf_op jit(solution)/shard_map/reduce_scatter | solution.py:443
  150.1 1.0 dynamic-slice_bitcast_fusion.4
  151.7 3.4 %collective-permute-done.18.a_ref = bf16[672,512]{1,0:T(8,128)(2,1)S(1)} collective-permute-done((bf16[672,512]{1,0:T(8,128)(2,1)S(1)}, bf16[672,512]{1,0:T(8,128)(2,1)S(1)}, u32[]{:S(2)}, u32[]{:S(2)}) %collective-permute-start.18) | collective-permute-done | bytes 688160 | tf_op jit(solution)/shard_map/ppermute | solution.py:38
  155.1 2.3 %collective-permute-done.23.c_ref = bf16[672,512]{1,0:T(8,128)(2,1)} collective-permute-done((bf16[672,512]{1,0:T(8,128)(2,1)}, bf16[672,512]{1,0:T(8,128)(2,1)}, u32[]{:S(2)}, u32[]{:S(2)}) %collective-permute-start.23) | collective-permute-done | bytes 688160 | tf_op jit(solution)/shard_map/ppermute | solution.py:34
  157.4 2.2 %shard_map.113 = bf16[672,512]{1,0:T(8,128)(2,1)} custom-call(f32[672,512]{1,0:T(8,128)S(1)} %copy-done.2, bf16[672,512]{1,0:T(8,128)(2,1)S(1)} %collective-permute-done.18.a_ref, bf16[672,512]{1,0:T(8,128)(2,1)S(1)} %collective-permute-done.22.b_ref, bf16[672,512]{1,0:T(8,128)(2,1)} %collective-permute-done.23.c_ref), custom_call_target="tpu_custom_call" | custom-call | bytes 5100000 | tf_op jit(solution)/shard_map/pallas_call | solution.py:96
  (92 shorter events, 13.0 us)
Async XLA Ops:
  7.2 142.9 %reduce-scatter.2.cloned.1.call-start = ((), (), s32[]{:S(2)}) async-start(), calls=%async_computation.1 | async-start | bytes 3096576 | tf_op jit(solution)/shard_map/reduce_scatter | solution.py:443
  7.2 20.0 %collective-permute-start.3 = (bf16[672,512]{1,0:T(8,128)(2,1)}, bf16[672,512]{1,0:T(8,128)(2,1)}, u32[]{:S(2)}, u32[]{:S(2)}) collective-permute-start(bf16[672,512]{1,0:T(8,128)(2,1)} %bitcast.90), channel_id=1, source_target_pairs={{0,4},{1,5},{2,6},{3,7},{4,0},{5,1},{6,2},{7,3},{8,12},{9,13},{10,... | collective-permute-start | bytes 2064392 | tf_op jit(solution)/shard_map/ppermute | solution.py:38
  9.4 17.7 %collective-permute-start.1 = (bf16[672,512]{1,0:T(8,128)(2,1)}, bf16[672,512]{1,0:T(8,128)(2,1)S(1)}, u32[]{:S(2)}, u32[]{:S(2)}) collective-permute-start(bf16[672,512]{1,0:T(8,128)(2,1)} %bitcast.91), channel_id=1, source_target_pairs={{0,3},{1,0},{2,1},{3,2},{4,7},{5,4},{6,5},{7,6},{8,11},{9,8},{10,9... | collective-permute-start | bytes 2064392 | tf_op jit(solution)/shard_map/ppermute | solution.py:34
  12.4 18.0 %collective-permute-start = (bf16[672,512]{1,0:T(8,128)(2,1)}, bf16[672,512]{1,0:T(8,128)(2,1)S(1)}, u32[]{:S(2)}, u32[]{:S(2)}) collective-permute-start(bf16[672,512]{1,0:T(8,128)(2,1)} %bitcast.92), channel_id=1, source_target_pairs={{0,1},{1,2},{2,3},{3,0},{4,5},{5,6},{6,7},{7,4},{8,9},{9,10},{10,1... | collective-permute-start | bytes 2064392 | tf_op jit(solution)/shard_map/ppermute | solution.py:34
  15.8 2.4 %copy-start.8 = (bf16[5376,512]{1,0:T(8,128)(2,1)}, bf16[5376,512]{1,0:T(8,128)(2,1)S(1)}, u32[]{:S(2)}) copy-start(bf16[5376,512]{1,0:T(8,128)(2,1)S(1)} %pad_maximum_fusion) | copy-start | bytes 16515076
  28.3 7.1 %copy-start.12 = (bf16[512,672]{0,1:T(8,128)(2,1)S(1)}, bf16[512,672]{0,1:T(8,128)(2,1)}, u32[]{:S(2)}) copy-start(bf16[512,672]{0,1:T(8,128)(2,1)} %param.7) | copy-start | bytes 2064388
  30.5 7.7 %slice-start = ((s8[5505024]{0:T(1024)(128)(4,1)}), s8[4194304]{0:T(1024)(128)(4,1)S(1)}, s32[]{:S(2)}) async-start(s8[5505024]{0:T(1024)(128)(4,1)} %bitcast.76), calls=%async_computation.2 | async-start | bytes 8388608
  30.7 18.1 %collective-permute-start.6 = (bf16[672,512]{1,0:T(8,128)(2,1)S(1)}, bf16[672,512]{1,0:T(8,128)(2,1)S(1)}, u32[]{:S(2)}, u32[]{:S(2)}) collective-permute-start(bf16[672,512]{1,0:T(8,128)(2,1)S(1)} %get-tuple-element.100), channel_id=1, source_target_pairs={{0,1},{1,2},{2,3},{3,0},{4,5},{5,6},{6,7},{7,4},{8,9},{9,10},{10,1... | collective-permute-start | bytes 2064392 | tf_op jit(solution)/shard_map/ppermute | solution.py:34
  30.8 17.3 %collective-permute-start.2 = (bf16[672,512]{1,0:T(8,128)(2,1)S(1)}, bf16[672,512]{1,0:T(8,128)(2,1)S(1)}, u32[]{:S(2)}, u32[]{:S(2)}) collective-permute-start(bf16[672,512]{1,0:T(8,128)(2,1)S(1)} %get-tuple-element.101), channel_id=1, source_target_pairs={{0,4},{1,5},{2,6},{3,7},{4,0},{5,1},{6,2},{7,3},{8,12},{9,13},{10,... | collective-permute-start | bytes 2064392 | tf_op jit(solution)/shard_map/ppermute | solution.py:38
  32.3 15.8 %collective-permute-start.7 = (bf16[672,512]{1,0:T(8,128)(2,1)S(1)}, bf16[672,512]{1,0:T(8,128)(2,1)S(1)}, u32[]{:S(2)}, u32[]{:S(2)}) collective-permute-start(bf16[672,512]{1,0:T(8,128)(2,1)S(1)} %get-tuple-element.102), channel_id=1, source_target_pairs={{0,3},{1,0},{2,1},{3,2},{4,7},{5,4},{6,5},{7,6},{8,11},{9,8},{10,9... | collective-permute-start | bytes 2064392 | tf_op jit(solution)/shard_map/ppermute | solution.py:34
  35.4 2.8 %slice-start.1 = ((s8[5505024]{0:T(1024)(128)(4,1)}), s8[1310720]{0:T(1024)(128)(4,1)S(1)}, s32[]{:S(2)}) async-start(s8[5505024]{0:T(1024)(128)(4,1)} %bitcast.76), calls=%async_computation.3 | async-start | bytes 2621440
  36.9 2.0 %copy-start.10 = (bf16[4,2,2,168,512]{4,3,2,1,0:T(8,128)(2,1)}, bf16[4,2,2,168,512]{4,3,2,1,0:T(8,128)(2,1)S(1)}, u32[]{:S(2)}) copy-start(bf16[4,2,2,168,512]{4,3,2,1,0:T(8,128)(2,1)S(1)} %pad_maximum_fusion.1.x_ref) | copy-start | bytes 8257540
  38.2 29.6 %collective-permute-start.10 = (bf16[4,2,168,512]{3,2,1,0:T(8,128)(2,1)}, bf16[4,2,168,512]{3,2,1,0:T(8,128)(2,1)}, u32[]{:S(2)}, u32[]{:S(2)}) collective-permute-start(bf16[4,2,168,512]{3,2,1,0:T(8,128)(2,1)} %dynamic-slice_bitcast_fusion), channel_id=1, source_target_pairs={{0,8},{8,0},{16,24},{24,16},{32,40},{40,32},{48,56},{56,48},{64,72... | collective-permute-start | bytes 4128776 | tf_op jit(solution)/shard_map/ppermute | solution.py:42
  49.6 8.9 %collective-permute-start.4 = (bf16[336,512]{1,0:T(8,128)(2,1)S(1)}, bf16[336,512]{1,0:T(8,128)(2,1)S(1)}, u32[]{:S(2)}, u32[]{:S(2)}) collective-permute-start(bf16[336,512]{1,0:T(8,128)(2,1)S(1)} %get-tuple-element.47), channel_id=1, source_target_pairs={{0,1},{1,2},{2,3},{3,0},{4,5},{5,6},{6,7},{7,4},{8,9},{9,10},{10,1... | collective-permute-start | bytes 1032200 | tf_op jit(solution)/shard_map/ppermute | solution.py:34
  50.4 8.1 %collective-permute-start.5 = (bf16[336,512]{1,0:T(8,128)(2,1)S(1)}, bf16[336,512]{1,0:T(8,128)(2,1)S(1)}, u32[]{:S(2)}, u32[]{:S(2)}) collective-permute-start(bf16[336,512]{1,0:T(8,128)(2,1)S(1)} %get-tuple-element.48), channel_id=1, source_target_pairs={{0,3},{1,0},{2,1},{3,2},{4,7},{5,4},{6,5},{7,6},{8,11},{9,8},{10,9... | collective-permute-start | bytes 1032200 | tf_op jit(solution)/shard_map/ppermute | solution.py:34
  53.6 1.8 %copy-start.11 = (bf16[3,2,2,168,512]{4,3,2,1,0:T(8,128)(2,1)}, bf16[3,2,2,168,512]{4,3,2,1,0:T(8,128)(2,1)S(1)}, u32[]{:S(2)}) copy-start(bf16[3,2,2,168,512]{4,3,2,1,0:T(8,128)(2,1)S(1)} %pad_maximum_fusion.2.xb_ref) | copy-start | bytes 6193156
  54.9 4.0 %copy-start.14 = (f32[128]{0:T(128)S(1)}, f32[128]{0:T(128)}, u32[]{:S(2)}) copy-start(f32[128]{0:T(128)} %param.11) | copy-start | bytes 1540
  54.9 4.1 %copy-start.15 = (f32[128]{0:T(128)S(1)}, f32[128]{0:T(128)}, u32[]{:S(2)}) copy-start(f32[128]{0:T(128)} %param.12) | copy-start | bytes 1540
  58.6 14.0 %copy-start = (bf16[672,512]{1,0:T(8,128)(2,1)}, bf16[672,512]{1,0:T(8,128)(2,1)S(1)}, u32[]{:S(2)}) copy-start(bf16[672,512]{1,0:T(8,128)(2,1)S(1)} %pad_maximum_fusion.6.last_ref) | copy-start | bytes 2064388
  58.6 30.1 %collective-permute-start.13 = (bf16[3,2,168,512]{3,2,1,0:T(8,128)(2,1)}, bf16[3,2,168,512]{3,2,1,0:T(8,128)(2,1)}, u32[]{:S(2)}, u32[]{:S(2)}) collective-permute-start(bf16[3,2,168,512]{3,2,1,0:T(8,128)(2,1)} %dynamic-slice_bitcast_fusion.1), channel_id=1, source_target_pairs={{0,8},{8,0},{16,24},{24,16},{32,40},{40,32},{48,56},{56,48},{64,72... | collective-permute-start | bytes 3096584 | tf_op jit(solution)/shard_map/ppermute | solution.py:42
  59.9 15.5 %collective-permute-start.9 = (bf16[256,512]{1,0:T(8,128)(2,1)S(1)}, bf16[256,512]{1,0:T(8,128)(2,1)S(1)}, u32[]{:S(2)}, u32[]{:S(2)}) collective-permute-start(bf16[256,512]{1,0:T(8,128)(2,1)S(1)} %get-tuple-element.53.own_ref), channel_id=1, source_target_pairs={{0,16},{8,24},{16,32},{24,40},{32,48},{40,56},{48,64},{56,72},{64,... | collective-permute-start | bytes 786440 | tf_op jit(solution)/shard_map/ppermute | solution.py:53
  63.7 14.3 %collective-permute-start.8 = (bf16[256,512]{1,0:T(8,128)(2,1)S(1)}, bf16[256,512]{1,0:T(8,128)(2,1)S(1)}, u32[]{:S(2)}, u32[]{:S(2)}) collective-permute-start(bf16[256,512]{1,0:T(8,128)(2,1)S(1)} %get-tuple-element.53.own_ref), channel_id=1, source_target_pairs={{0,8},{8,16},{16,24},{24,32},{32,40},{40,48},{48,56},{56,64},{64,7... | collective-permute-start | bytes 786440 | tf_op jit(solution)/shard_map/ppermute | solution.py:53
  65.9 12.1 %copy-start.7 = (bf16[512,256]{1,0:T(8,128)(2,1)S(1)}, bf16[512,256]{1,0:T(8,128)(2,1)}, u32[]{:S(2)}) copy-start(bf16[512,256]{1,0:T(8,128)(2,1)} %go_ref.1) | copy-start | bytes 786436
  65.9 22.7 %collective-permute-start.14 = (bf16[1,2,168,512]{3,2,1,0:T(8,128)(2,1)S(1)}, bf16[1,2,168,512]{3,2,1,0:T(8,128)(2,1)S(1)}, u32[]{:S(2)}, u32[]{:S(2)}) collective-permute-start(bf16[1,2,168,512]{3,2,1,0:T(8,128)(2,1)S(1)} %dynamic-slice_bitcast_fusion.3), channel_id=1, source_target_pairs={{0,8},{8,0},{16,24},{24,16},{32,40},{40,32},{48,56},{56,48},{64,72... | collective-permute-start | bytes 1032200 | tf_op jit(solution)/shard_map/ppermute | solution.py:42
  83.0 11.2 %collective-permute-start.11 = (bf16[2,512,128]{2,1,0:T(8,128)(2,1)S(1)}, bf16[2,512,128]{2,1,0:T(8,128)(2,1)S(1)}, u32[]{:S(2)}, u32[]{:S(2)}) collective-permute-start(bf16[2,512,128]{2,1,0:T(8,128)(2,1)S(1)} %get-tuple-element.58), channel_id=1, source_target_pairs={{8,0},{16,8},{24,16},{32,24},{40,32},{48,40},{56,48},{64,56},{72,6... | collective-permute-start | bytes 786440 | tf_op jit(solution)/shard_map/ppermute | solution.py:53
  85.0 10.6 %collective-permute-start.12 = (bf16[2,512,128]{2,1,0:T(8,128)(2,1)S(1)}, bf16[2,512,128]{2,1,0:T(8,128)(2,1)S(1)}, u32[]{:S(2)}, u32[]{:S(2)}) collective-permute-start(bf16[2,512,128]{2,1,0:T(8,128)(2,1)S(1)} %get-tuple-element.59), channel_id=1, source_target_pairs={{16,0},{24,8},{32,16},{40,24},{48,32},{56,40},{64,48},{72,56},{80,... | collective-permute-start | bytes 786440 | tf_op jit(solution)/shard_map/ppermute | solution.py:53
  88.6 0.7 copy-start.13
  95.8 0.8 copy-start.1
  95.8 4.3 %copy-start.9 = (bf16[4,2,2,168,1024]{4,3,2,1,0:T(8,128)(2,1)S(1)}, bf16[4,2,2,168,1024]{4,3,2,1,0:T(8,128)(2,1)}, u32[]{:S(2)}) copy-start(bf16[4,2,2,168,1024]{4,3,2,1,0:T(8,128)(2,1)} %shard_map.105) | copy-start | bytes 16515076
  95.9 4.3 %collective-permute-start.15 = (bf16[512,512]{1,0:T(8,128)(2,1)S(1)}, bf16[512,512]{1,0:T(8,128)(2,1)S(1)}, u32[]{:S(2)}, u32[]{:S(2)}) collective-permute-start(bf16[512,512]{1,0:T(8,128)(2,1)S(1)} %shard_map.106.d_ref), channel_id=1, source_target_pairs={{0,8},{8,0},{16,24},{24,16},{32,40},{40,32},{48,56},{56,48},{64,72... | collective-permute-start | bytes 1572872 | tf_op jit(solution)/shard_map/ppermute | solution.py:42
  105.7 1.0 copy-start.17
  105.7 2.4 %copy-start.16 = (bf16[336,512]{1,0:T(8,128)(2,1)S(1)}, bf16[336,512]{1,0:T(8,128)(2,1)}, u32[]{:S(2)}) copy-start(bf16[336,512]{1,0:T(8,128)(2,1)} %get-tuple-element.69) | copy-start | bytes 1032196
  106.7 11.0 %collective-permute-start.20 = (bf16[336,512]{1,0:T(8,128)(2,1)S(1)}, bf16[336,512]{1,0:T(8,128)(2,1)S(1)}, u32[]{:S(2)}, u32[]{:S(2)}) collective-permute-start(bf16[336,512]{1,0:T(8,128)(2,1)S(1)} %copy-done.17), channel_id=1, source_target_pairs={{0,1},{1,2},{2,3},{3,0},{4,5},{5,6},{6,7},{7,4},{8,9},{9,10},{10,1... | collective-permute-start | bytes 1032200 | tf_op jit(solution)/shard_map/ppermute | solution.py:34
  108.1 9.6 %collective-permute-start.19 = (bf16[336,512]{1,0:T(8,128)(2,1)S(1)}, bf16[336,512]{1,0:T(8,128)(2,1)S(1)}, u32[]{:S(2)}, u32[]{:S(2)}) collective-permute-start(bf16[336,512]{1,0:T(8,128)(2,1)S(1)} %copy-done.16), channel_id=1, source_target_pairs={{0,3},{1,0},{2,1},{3,2},{4,7},{5,4},{6,5},{7,6},{8,11},{9,8},{10,9... | collective-permute-start | bytes 1032200 | tf_op jit(solution)/shard_map/ppermute | solution.py:34
  115.5 16.9 %collective-permute-start.16 = (bf16[672,512]{1,0:T(8,128)(2,1)}, bf16[672,512]{1,0:T(8,128)(2,1)S(1)}, u32[]{:S(2)}, u32[]{:S(2)}) collective-permute-start(bf16[672,512]{1,0:T(8,128)(2,1)} %get-tuple-element.73), channel_id=1, source_target_pairs={{0,3},{1,0},{2,1},{3,2},{4,7},{5,4},{6,5},{7,6},{8,11},{9,8},{10,9... | collective-permute-start | bytes 2064392 | tf_op jit(solution)/shard_map/ppermute | solution.py:34
  117.3 17.6 %collective-permute-start.17 = (bf16[672,512]{1,0:T(8,128)(2,1)}, bf16[672,512]{1,0:T(8,128)(2,1)S(1)}, u32[]{:S(2)}, u32[]{:S(2)}) collective-permute-start(bf16[672,512]{1,0:T(8,128)(2,1)} %get-tuple-element.74), channel_id=1, source_target_pairs={{0,1},{1,2},{2,3},{3,0},{4,5},{5,6},{6,7},{7,4},{8,9},{9,10},{10,1... | collective-permute-start | bytes 2064392 | tf_op jit(solution)/shard_map/ppermute | solution.py:34
  117.7 1.1 copy-start.5
  119.0 19.4 %collective-permute-start.21 = (bf16[672,512]{1,0:T(8,128)(2,1)S(1)}, bf16[672,512]{1,0:T(8,128)(2,1)S(1)}, u32[]{:S(2)}, u32[]{:S(2)}) collective-permute-start(bf16[672,512]{1,0:T(8,128)(2,1)S(1)} %shard_map.111), channel_id=1, source_target_pairs={{0,4},{1,5},{2,6},{3,7},{4,0},{5,1},{6,2},{7,3},{8,12},{9,13},{10,... | collective-permute-start | bytes 2064392 | tf_op jit(solution)/shard_map/ppermute | solution.py:38
  127.7 10.6 %copy-start.3 = (bf16[672,512]{1,0:T(8,128)(2,1)S(1)}, bf16[672,512]{1,0:T(8,128)(2,1)}, u32[]{:S(2)}) copy-start(bf16[672,512]{1,0:T(8,128)(2,1)} %get-tuple-element.81.below_ref) | copy-start | bytes 2064388
  127.7 10.6 %copy-start.4 = (bf16[672,512]{1,0:T(8,128)(2,1)S(1)}, bf16[672,512]{1,0:T(8,128)(2,1)}, u32[]{:S(2)}) copy-start(bf16[672,512]{1,0:T(8,128)(2,1)} %get-tuple-element.82.above_ref) | copy-start | bytes 2064388
  135.0 1.1 copy-start.6
  136.2 21.2 %copy-start.2 = (f32[672,512]{1,0:T(8,128)S(1)}, f32[672,512]{1,0:T(8,128)}, u32[]{:S(2)}) copy-start(f32[672,512]{1,0:T(8,128)} %get-tuple-element.67.mine_ref) | copy-start | bytes 4128772
  136.3 18.8 %collective-permute-start.18 = (bf16[672,512]{1,0:T(8,128)(2,1)S(1)}, bf16[672,512]{1,0:T(8,128)(2,1)S(1)}, u32[]{:S(2)}, u32[]{:S(2)}) collective-permute-start(bf16[672,512]{1,0:T(8,128)(2,1)S(1)} %shard_map.110), channel_id=1, source_target_pairs={{0,4},{1,5},{2,6},{3,7},{4,0},{5,1},{6,2},{7,3},{8,12},{9,13},{10,... | collective-permute-start | bytes 2064392 | tf_op jit(solution)/shard_map/ppermute | solution.py:38
  139.6 15.5 %collective-permute-start.22 = (bf16[672,512]{1,0:T(8,128)(2,1)}, bf16[672,512]{1,0:T(8,128)(2,1)S(1)}, u32[]{:S(2)}, u32[]{:S(2)}) collective-permute-start(bf16[672,512]{1,0:T(8,128)(2,1)} %get-tuple-element.85), channel_id=1, source_target_pairs={{0,3},{1,0},{2,1},{3,2},{4,7},{5,4},{6,5},{7,6},{8,11},{9,8},{10,9... | collective-permute-start | bytes 2064392 | tf_op jit(solution)/shard_map/ppermute | solution.py:34
  141.1 16.3 %collective-permute-start.23 = (bf16[672,512]{1,0:T(8,128)(2,1)}, bf16[672,512]{1,0:T(8,128)(2,1)}, u32[]{:S(2)}, u32[]{:S(2)}) collective-permute-start(bf16[672,512]{1,0:T(8,128)(2,1)} %get-tuple-element.86), channel_id=1, source_target_pairs={{0,1},{1,2},{2,3},{3,0},{4,5},{5,6},{6,7},{7,4},{8,9},{9,10},{10,1... | collective-permute-start | bytes 2064392 | tf_op jit(solution)/shard_map/ppermute | solution.py:34
  151.1 8.5 %collective-permute-start.24 = (bf16[168,512]{1,0:T(8,128)(2,1)S(1)}, bf16[168,512]{1,0:T(8,128)(2,1)S(1)}, u32[]{:S(2)}, u32[]{:S(2)}) collective-permute-start(bf16[168,512]{1,0:T(8,128)(2,1)S(1)} %get-tuple-element.98), channel_id=1, source_target_pairs={{0,128},{8,136},{16,144},{24,152},{32,160},{40,168},{48,176},{56,1... | collective-permute-start | bytes 516104 | tf_op jit(solution)/shard_map/ppermute | solution.py:47
Sparse Core Ops, SparseCore 0:
  105.8 44.2 reduce-scatter.1

commit v3 on v2

--- a/solution.py
+++ b/solution.py
@@ -111,8 +111,8 @@
     return slice(0, half), slice(half, 2 * half)
 
 
-def add_pair(keep_ref, got_ref, q_ref, k_ref, v_ref):
-    total = keep_ref[...].astype(f32) + got_ref[...].astype(f32)
+def add_pair(g_ref, got_ref, q_ref, k_ref, v_ref):
+    total = g_ref[0].astype(f32) + got_ref[...].astype(f32)
     q_ref[...] = total[:, : 2 * HD]
     k_ref[...] = total[:, 2 * HD : 3 * HD]
     v_ref[...] = total[:, 3 * HD :]
@@ -180,7 +180,7 @@
 
 def add_last(mine_ref, a_ref, b_ref, c_ref, out_ref):
     got = a_ref[...].astype(f32) + b_ref[...].astype(f32) + c_ref[...].astype(f32)
-    out_ref[...] = (mine_ref[...] + got).astype(bf16)
+    out_ref[...] = (mine_ref[...].astype(f32) + got).astype(bf16)
 
 
 def with_table(kernel, us, grid, table, specs, args, outs, out_specs, scratch=(), alias={}):
@@ -229,8 +229,7 @@
     side, down, up = terms(second_terms, 4.5, 1, 3, [full] * 3, extra)
     down, up = y_step(down, -1), y_step(up, 1)
     side = x_swap(call(add_side, full, 0.8)(side, top, bottom))
-    mine = sds((feats, toks), f32)
-    across, below, above, mine = terms(third_terms, 6.0, 4, 4, [full, full, full, mine])
+    across, below, above, mine = terms(third_terms, 6.0, 4, 4, [full] * 4)
     down, up, across, below, above = lax.optimization_barrier((down, up, across, below, above))
     across = x_swap(call(add_across, full, 0.8)(across, down, up))
     below, above = call(add_near, (full, full), 1.2)(below, above, side, down, up)
@@ -392,7 +391,7 @@
     w_cat = jnp.concatenate([w_query, w_key, w_value], axis=1)
     w_own = w_cat.reshape(n_tp, feats, w_cat.shape[1])
 
-    table = jnp.stack([core, *[owner(rel) for rel in RELS + SENT]]).astype(jnp.int32)
+    table = jnp.stack([core, *[owner(rel) for rel in RELS + SENT], j // NZ]).astype(jnp.int32)
     w_last = lax.dynamic_index_in_dim(w_own, owner(RELS[7]), 0, keepdims=False).T
 
     def project(total, parts, rels):
@@ -423,7 +422,6 @@
         most, w_last, last, qg, kg, cos, sin
     )
     rings = [[(a * NZ + z) * NC + c for z in range(NZ)] for a in range(NXL) for c in range(NC)]
-    xl = j // NZ
 
     def x_specs(at):
         return [
@@ -432,9 +430,10 @@
         ]
 
     def pair_spec(first):
+        half = 1 + len(RELS + SENT)
         return pl.BlockSpec(
             (1, 2, 1, blk, 2 * toks),
-            lambda i, t: (t[first + i] % NY, 0, t[first + i] // NY, 0, 0),
+            lambda i, t: (t[first + i] % NY, 0, (t[first + i] // NY + t[half]) % NXL, 0, 0),
         )
 
     pair_shape = sds((NY, 2, NXH, blk, 2 * toks), bf16)
@@ -446,10 +445,8 @@
 
     def across_x(g):
         g = g.reshape(NXL, blk, -1)
-        keep = lax.dynamic_index_in_dim(g, xl, 0, keepdims=False)
-        send = lax.dynamic_index_in_dim(g, 1 - xl, 0, keepdims=False)
         outs = [sds((blk, w), f32) for w in (2 * HD, HD, HD)]
-        return call(add_pair, outs, 0.7)(keep, xlo_swap(send))
+        return call(add_pair, outs, 0.7)(g, xlo_swap(g[1]))
 
     kv1 = from_behind(kv_t, 1)
     kv2 = from_behind(kv_t, 2)

time: 168 us -> 167 us (level)
    unnamed x40 -> x42, local copies, waits for them, and re-layouts: 7.12 us -> 7.13 us
  transfers between devices with their start and end apart: 26 -> 26, of which waited for: 13 -> 13; matrix products, arithmetic and copies ran while one was open for 11% -> 11% of each run, Pallas kernels for 21% -> 20%
where the time goes in v3:
time: 167 us; the launch traced here: 166 us
  waiting for transfers between devices  46 us (28%)
  starting transfers between devices  39.6 us (24%)
  Pallas kernels  34.7 us (21%)
  between operations  14.5 us (9%)
  local copies, waits for them, and re-layouts  13.2 us (8%)
  matrix products  12.2 us (7%)
  other arithmetic  5.96 us (4%)
    pallas_call x5, Pallas kernels, with_table(): pl.pallas_call(kernel, out_shape=outs, grid_spec=pltpu.PrefetchScalarGrid...  25.2 us
    ppermute x12, waiting for transfers between devices, y_step(): return lax.ppermute(v, 'tp', tp_perm(0, d))  20.4 us
    ppermute x12, starting transfers between devices, y_step(): return lax.ppermute(v, 'tp', tp_perm(0, d))  17.3 us
    ppermute x4, starting transfers between devices, from_behind(): return lax.ppermute(block, 'ctx', route)  11.5 us
    ppermute x4, waiting for transfers between devices, x_swap(): return lax.ppermute(v, 'tp', tp_perm(1, 0))  10.2 us
    pallas_call x8, Pallas kernels, run(): pl.pallas_call(kernel, out_shape=outs, in_specs=in_specs, out_specs=jax.t...  9.52 us
    reduce_scatter x1, waiting for transfers between devices, along_z(): lax.psum_scatter(g, 'ctx', scatter_dimension=0, tiled=True, axis_index_gr...  8.49 us
    ppermute x4, starting transfers between devices, x_swap(): return lax.ppermute(v, 'tp', tp_perm(1, 0))  7.89 us
  transfers between devices with their start and end apart: 26, of which 13 were waited for; matrix products, arithmetic and copies ran while one was open for 11% of the time, Pallas kernels for 20%

profile of v3, /device:TPU:2, one launch (start us, length us, event | category | flops | bytes accessed | tf_op | source)
XLA Modules:
  0.0 166.1 jit_solution(14855964580677780323)
XLA Ops:
  7.2 2.2 %collective-permute-start.3 = (bf16[672,512]{1,0:T(8,128)(2,1)}, bf16[672,512]{1,0:T(8,128)(2,1)}, u32[]{:S(2)}, u32[]{:S(2)}) collective-permute-start(bf16[672,512]{1,0:T(8,128)(2,1)} %bitcast.91), channel_id=1, source_target_pairs={{0,4},{1,5},{2,6},{3,7},{4,0},{5,1},{6,2},{7,3},{8,12},{9,13},{10,... | collective-permute-start | bytes 2064392 | tf_op jit(solution)/shard_map/ppermute | solution.py:38
  9.4 3.0 %collective-permute-start.1 = (bf16[672,512]{1,0:T(8,128)(2,1)}, bf16[672,512]{1,0:T(8,128)(2,1)S(1)}, u32[]{:S(2)}, u32[]{:S(2)}) collective-permute-start(bf16[672,512]{1,0:T(8,128)(2,1)} %bitcast.92), channel_id=1, source_target_pairs={{0,3},{1,0},{2,1},{3,2},{4,7},{5,4},{6,5},{7,6},{8,11},{9,8},{10,9... | collective-permute-start | bytes 2064392 | tf_op jit(solution)/shard_map/ppermute | solution.py:34
  12.4 3.4 %pad_maximum_fusion = bf16[5376,512]{1,0:T(8,128)(2,1)S(1)} fusion(bf16[5376,128]{1,0:T(8,128)(2,1)} %param.10, bf16[5376,128]{1,0:T(8,128)(2,1)} %param.9, bf16[5376,256]{1,0:T(8,128)(2,1)} %param.8), kind=kLoop, calls=%fused_computation | loop fusion | flops 16515072 | bytes 11010048 | tf_op jit(solution)/shard_map/concatenate | solution.py:391
  15.8 2.4 %copy-done.9 = bf16[5376,512]{1,0:T(8,128)(2,1)} copy-done((bf16[5376,512]{1,0:T(8,128)(2,1)}, bf16[5376,512]{1,0:T(8,128)(2,1)S(1)}, u32[]{:S(2)}) %copy-start.9) | copy-done | bytes 5505048
  19.8 1.9 %fusion.14 = f32[512,512]{1,0:T(8,128)S(1)} fusion(bf16[512,672]{0,1:T(8,128)(2,1)} %param.7, bf16[8,672,512]{2,1,0:T(8,128)(2,1)} %bitcast.72, s32[]{:T(128)S(6)} %select_n.173), kind=kOutput, calls=%fused_computation.31 | convolution fusion | flops 352321536 | bytes 2424836 | tf_op jit(solution)/shard_map/dot_general | solution.py:400
  21.7 5.4 %collective-permute-done.1 = bf16[672,512]{1,0:T(8,128)(2,1)S(1)} collective-permute-done((bf16[672,512]{1,0:T(8,128)(2,1)}, bf16[672,512]{1,0:T(8,128)(2,1)S(1)}, u32[]{:S(2)}, u32[]{:S(2)}) %collective-permute-start.1) | collective-permute-done | bytes 688160 | tf_op jit(solution)/shard_map/ppermute | solution.py:34
  27.2 1.1 fusion.33
  28.3 2.1 %collective-permute-done = bf16[672,512]{1,0:T(8,128)(2,1)S(1)} collective-permute-done((bf16[672,512]{1,0:T(8,128)(2,1)}, bf16[672,512]{1,0:T(8,128)(2,1)S(1)}, u32[]{:S(2)}, u32[]{:S(2)}) %collective-permute-start) | collective-permute-done | bytes 688160 | tf_op jit(solution)/shard_map/ppermute | solution.py:34
  30.8 1.5 collective-permute-start.2
  32.3 3.1 %collective-permute-start.7 = (bf16[672,512]{1,0:T(8,128)(2,1)S(1)}, bf16[672,512]{1,0:T(8,128)(2,1)S(1)}, u32[]{:S(2)}, u32[]{:S(2)}) collective-permute-start(bf16[672,512]{1,0:T(8,128)(2,1)S(1)} %get-tuple-element.100), channel_id=1, source_target_pairs={{0,3},{1,0},{2,1},{3,2},{4,7},{5,4},{6,5},{7,6},{8,11},{9,8},{10,9... | collective-permute-start | bytes 2064392 | tf_op jit(solution)/shard_map/ppermute | solution.py:34
  35.4 1.5 pad_maximum_fusion.1.x_ref
  36.9 1.3 dynamic-slice_bitcast_fusion
  38.9 1.7 %fusion.10 = f32[512,512]{1,0:T(8,128)S(1)} fusion(bf16[672,512]{1,0:T(8,128)(2,1)} %collective-permute-done.3, bf16[8,672,512]{2,1,0:T(8,128)(2,1)S(1)} %bitcast.79, s32[]{:T(128)S(6)} %select_n.176), kind=kOutput, calls=%fused_computation.27 | convolution fusion | flops 352321536 | bytes 2424836 | tf_op jit(solution)/shard_map/dot_general | solution.py:400
  41.2 6.8 %collective-permute-done.2 = bf16[672,512]{1,0:T(8,128)(2,1)S(1)} collective-permute-done((bf16[672,512]{1,0:T(8,128)(2,1)S(1)}, bf16[672,512]{1,0:T(8,128)(2,1)S(1)}, u32[]{:S(2)}, u32[]{:S(2)}) %collective-permute-start.2) | collective-permute-done | bytes 688160 | tf_op jit(solution)/shard_map/ppermute | solution.py:38
  50.4 3.0 %collective-permute-start.5 = (bf16[336,512]{1,0:T(8,128)(2,1)S(1)}, bf16[336,512]{1,0:T(8,128)(2,1)S(1)}, u32[]{:S(2)}, u32[]{:S(2)}) collective-permute-start(bf16[336,512]{1,0:T(8,128)(2,1)S(1)} %get-tuple-element.48), channel_id=1, source_target_pairs={{0,3},{1,0},{2,1},{3,2},{4,7},{5,4},{6,5},{7,6},{8,11},{9,8},{10,9... | collective-permute-start | bytes 1032200 | tf_op jit(solution)/shard_map/ppermute | solution.py:34
  53.7 1.2 dynamic-slice_bitcast_fusion.1
  55.5 3.0 %collective-permute-done.4 = bf16[336,512]{1,0:T(8,128)(2,1)S(1)} collective-permute-done((bf16[336,512]{1,0:T(8,128)(2,1)S(1)}, bf16[336,512]{1,0:T(8,128)(2,1)S(1)}, u32[]{:S(2)}, u32[]{:S(2)}) %collective-permute-start.4) | collective-permute-done | bytes 344096 | tf_op jit(solution)/shard_map/ppermute | solution.py:34
  59.9 3.8 %collective-permute-start.9 = (bf16[256,512]{1,0:T(8,128)(2,1)S(1)}, bf16[256,512]{1,0:T(8,128)(2,1)S(1)}, u32[]{:S(2)}, u32[]{:S(2)}) collective-permute-start(bf16[256,512]{1,0:T(8,128)(2,1)S(1)} %get-tuple-element.53.own_ref), channel_id=1, source_target_pairs={{0,16},{8,24},{16,32},{24,40},{32,48},{40,56},{48,64},{56,72},{64,... | collective-permute-start | bytes 786440 | tf_op jit(solution)/shard_map/ppermute | solution.py:53
  63.7 2.1 %collective-permute-start.8 = (bf16[256,512]{1,0:T(8,128)(2,1)S(1)}, bf16[256,512]{1,0:T(8,128)(2,1)S(1)}, u32[]{:S(2)}, u32[]{:S(2)}) collective-permute-start(bf16[256,512]{1,0:T(8,128)(2,1)S(1)} %get-tuple-element.53.own_ref), channel_id=1, source_target_pairs={{0,8},{8,16},{16,24},{24,32},{32,40},{40,48},{48,56},{56,64},{64,7... | collective-permute-start | bytes 786440 | tf_op jit(solution)/shard_map/ppermute | solution.py:53
  65.9 1.9 %collective-permute-start.14 = (bf16[1,2,168,512]{3,2,1,0:T(8,128)(2,1)S(1)}, bf16[1,2,168,512]{3,2,1,0:T(8,128)(2,1)S(1)}, u32[]{:S(2)}, u32[]{:S(2)}) collective-permute-start(bf16[1,2,168,512]{3,2,1,0:T(8,128)(2,1)S(1)} %dynamic-slice_bitcast_fusion.3), channel_id=1, source_target_pairs={{0,8},{8,0},{16,24},{24,16},{32,40},{40,32},{48,56},{56,48},{64,72... | collective-permute-start | bytes 1032200 | tf_op jit(solution)/shard_map/ppermute | solution.py:42
  67.8 4.7 %shard_map.103.begun_ref = bf16[4,2,2,168,1024]{4,3,2,1,0:T(8,128)(2,1)} custom-call(s32[18]{0:T(128)} %stack.78.table_ref.own_ref, bf16[4,2,2,168,512]{4,3,2,1,0:T(8,128)(2,1)} %copy-done.11, bf16[4,2,168,512]{3,2,1,0:T(8,128)(2,1)} %collective-permute-done.10.o_ref), custom_call_target="tpu_custom_call" | custom-call | bytes 13600000 | tf_op jit(solution)/shard_map/pallas_call | solution.py:187
  72.5 2.9 %collective-permute-done.9.m2_ref = bf16[256,512]{1,0:T(8,128)(2,1)S(1)} collective-permute-done((bf16[256,512]{1,0:T(8,128)(2,1)S(1)}, bf16[256,512]{1,0:T(8,128)(2,1)S(1)}, u32[]{:S(2)}, u32[]{:S(2)}) %collective-permute-start.9) | collective-permute-done | bytes 262176 | tf_op jit(solution)/shard_map/ppermute | solution.py:53
  75.4 2.6 %collective-permute-done.8.m1_ref = bf16[256,512]{1,0:T(8,128)(2,1)S(1)} collective-permute-done((bf16[256,512]{1,0:T(8,128)(2,1)S(1)}, bf16[256,512]{1,0:T(8,128)(2,1)S(1)}, u32[]{:S(2)}, u32[]{:S(2)}) %collective-permute-start.8) | collective-permute-done | bytes 262176 | tf_op jit(solution)/shard_map/ppermute | solution.py:53
  78.0 5.0 %shard_map.104 = (bf16[256,512]{1,0:T(8,128)(2,1)S(1)}, f32[2,512,128]{2,1,0:T(8,128)S(1)}, bf16[2,512,128]{2,1,0:T(8,128)(2,1)S(1)}, bf16[2,512,128]{2,1,0:T(8,128)(2,1)S(1)}) custom-call(s32[1]{0:T(128)} %bitcast.11.ctx_ref, bf16[256,512]{1,0:T(8,128)(2,1)S(1)} %get-tuple-element.51.q_ref, f32[512,512]{1,0:T(8,128)S(1)} %get-tuple-element.52.raw_ref, ...), custom_call_target="tpu_custom_call" | custom-call | bytes 18700000 | tf_op jit(solution)/shard_map/pallas_call | solution.py:96
  83.0 1.9 %collective-permute-start.11 = (bf16[2,512,128]{2,1,0:T(8,128)(2,1)S(1)}, bf16[2,512,128]{2,1,0:T(8,128)(2,1)S(1)}, u32[]{:S(2)}, u32[]{:S(2)}) collective-permute-start(bf16[2,512,128]{2,1,0:T(8,128)(2,1)S(1)} %get-tuple-element.58), channel_id=1, source_target_pairs={{8,0},{16,8},{24,16},{32,24},{40,32},{48,40},{56,48},{64,56},{72,6... | collective-permute-start | bytes 786440 | tf_op jit(solution)/shard_map/ppermute | solution.py:53
  85.0 3.6 %collective-permute-start.12 = (bf16[2,512,128]{2,1,0:T(8,128)(2,1)S(1)}, bf16[2,512,128]{2,1,0:T(8,128)(2,1)S(1)}, u32[]{:S(2)}, u32[]{:S(2)}) collective-permute-start(bf16[2,512,128]{2,1,0:T(8,128)(2,1)S(1)} %get-tuple-element.59), channel_id=1, source_target_pairs={{16,0},{24,8},{32,16},{40,24},{48,32},{56,40},{64,48},{72,56},{80,... | collective-permute-start | bytes 786440 | tf_op jit(solution)/shard_map/ppermute | solution.py:53
  89.3 4.9 %shard_map.105 = bf16[4,2,2,168,1024]{4,3,2,1,0:T(8,128)(2,1)} custom-call(s32[18]{0:T(128)} %stack.78.table_ref.own_ref, bf16[3,2,2,168,512]{4,3,2,1,0:T(8,128)(2,1)} %copy-done.12, bf16[3,2,168,512]{3,2,1,0:T(8,128)(2,1)} %collective-permute-done.13.ob_ref, bf16[1,2,2,168,512]{4,3,2,1,0:T(8,128)(2,1)} %bitcast.68, ...), custom_call_target="tpu_custom_call", output_to_operand_aliasing={{}: (5, {})} | custom-call | bytes 13600000 | tf_op jit(solution)/shard_map/pallas_call | solution.py:187
  94.2 1.3 collective-permute-done.12.r2_ref
  96.7 3.5 %shard_map.108 = (bf16[336,512]{1,0:T(8,128)(2,1)}, bf16[336,512]{1,0:T(8,128)(2,1)}) custom-call(s32[18]{0:T(128)} %stack.78.table_ref.own_ref, bf16[8,672,512]{2,1,0:T(8,128)(2,1)} %bitcast.73, bf16[512,512]{1,0:T(8,128)(2,1)} %copy-done.1), custom_call_target="tpu_custom_call" | custom-call | bytes 6800000 | tf_op jit(solution)/shard_map/pallas_call | solution.py:187
  100.2 5.5 %convolution_convert_fusion = bf16[8,336,512]{2,1,0:T(8,128)(2,1)} fusion(bf16[8,336,1024]{2,1,0:T(8,128)(2,1)S(1)} %bitcast.84, bf16[512,512]{1,0:T(8,128)(2,1)S(1)} %collective-permute-done.15, bf16[512,512]{1,0:T(8,128)(2,1)} %copy-done.1), kind=kOutput, calls=%fused_computation.2 | convolution fusion | flops 2822045696 | bytes 9306112 | tf_op jit(solution)/shard_map/dot_general | solution.py:505
  106.7 1.5 collective-permute-start.20
  108.1 1.8 %collective-permute-start.19 = (bf16[336,512]{1,0:T(8,128)(2,1)S(1)}, bf16[336,512]{1,0:T(8,128)(2,1)S(1)}, u32[]{:S(2)}, u32[]{:S(2)}) collective-permute-start(bf16[336,512]{1,0:T(8,128)(2,1)S(1)} %copy-done.17), channel_id=1, source_target_pairs={{0,3},{1,0},{2,1},{3,2},{4,7},{5,4},{6,5},{7,6},{8,11},{9,8},{10,9... | collective-permute-start | bytes 1032200 | tf_op jit(solution)/shard_map/ppermute | solution.py:34
  109.9 5.5 %shard_map.109 = (bf16[672,512]{1,0:T(8,128)(2,1)}, bf16[672,512]{1,0:T(8,128)(2,1)}, bf16[672,512]{1,0:T(8,128)(2,1)}) custom-call(s32[18]{0:T(128)} %stack.78.table_ref.own_ref, bf16[8,672,512]{2,1,0:T(8,128)(2,1)} %bitcast.74, bf16[512,512]{1,0:T(8,128)(2,1)} %copy-done.1), custom_call_target="tpu_custom_call" | custom-call | bytes 15300000 | tf_op jit(solution)/shard_map/pallas_call | solution.py:187
  115.4 1.9 %collective-permute-start.16 = (bf16[672,512]{1,0:T(8,128)(2,1)}, bf16[672,512]{1,0:T(8,128)(2,1)S(1)}, u32[]{:S(2)}, u32[]{:S(2)}) collective-permute-start(bf16[672,512]{1,0:T(8,128)(2,1)} %get-tuple-element.73), channel_id=1, source_target_pairs={{0,3},{1,0},{2,1},{3,2},{4,7},{5,4},{6,5},{7,6},{8,11},{9,8},{10,9... | collective-permute-start | bytes 2064392 | tf_op jit(solution)/shard_map/ppermute | solution.py:34
  117.7 1.1 copy-done.6
  119.0 2.1 %collective-permute-start.21 = (bf16[672,512]{1,0:T(8,128)(2,1)S(1)}, bf16[672,512]{1,0:T(8,128)(2,1)S(1)}, u32[]{:S(2)}, u32[]{:S(2)}) collective-permute-start(bf16[672,512]{1,0:T(8,128)(2,1)S(1)} %shard_map.111), channel_id=1, source_target_pairs={{0,4},{1,5},{2,6},{3,7},{4,0},{5,1},{6,2},{7,3},{8,12},{9,13},{10,... | collective-permute-start | bytes 2064392 | tf_op jit(solution)/shard_map/ppermute | solution.py:38
  121.0 6.5 %shard_map.107 = (bf16[672,512]{1,0:T(8,128)(2,1)}, bf16[672,512]{1,0:T(8,128)(2,1)}, bf16[672,512]{1,0:T(8,128)(2,1)}, bf16[672,512]{1,0:T(8,128)(2,1)}) custom-call(s32[18]{0:T(128)} %stack.78.table_ref.own_ref, bf16[8,672,512]{2,1,0:T(8,128)(2,1)} %bitcast.75, bf16[512,512]{1,0:T(8,128)(2,1)} %copy-done.1), custom_call_target="tpu_custom_call" | custom-call | bytes 20400000 | tf_op jit(solution)/shard_map/pallas_call | solution.py:187
  127.5 4.9 %collective-permute-done.16.down_ref = bf16[672,512]{1,0:T(8,128)(2,1)S(1)} collective-permute-done((bf16[672,512]{1,0:T(8,128)(2,1)}, bf16[672,512]{1,0:T(8,128)(2,1)S(1)}, u32[]{:S(2)}, u32[]{:S(2)}) %collective-permute-start.16) | collective-permute-done | bytes 688160 | tf_op jit(solution)/shard_map/ppermute | solution.py:34
  132.4 2.6 %collective-permute-done.17.up_ref = bf16[672,512]{1,0:T(8,128)(2,1)S(1)} collective-permute-done((bf16[672,512]{1,0:T(8,128)(2,1)}, bf16[672,512]{1,0:T(8,128)(2,1)S(1)}, u32[]{:S(2)}, u32[]{:S(2)}) %collective-permute-start.17) | collective-permute-done | bytes 688160 | tf_op jit(solution)/shard_map/ppermute | solution.py:34
  135.0 1.1 copy-done.7
  136.2 2.1 %collective-permute-start.18 = (bf16[672,512]{1,0:T(8,128)(2,1)S(1)}, bf16[672,512]{1,0:T(8,128)(2,1)S(1)}, u32[]{:S(2)}, u32[]{:S(2)}) collective-permute-start(bf16[672,512]{1,0:T(8,128)(2,1)S(1)} %shard_map.110), channel_id=1, source_target_pairs={{0,4},{1,5},{2,6},{3,7},{4,0},{5,1},{6,2},{7,3},{8,12},{9,13},{10,... | collective-permute-start | bytes 2064392 | tf_op jit(solution)/shard_map/ppermute | solution.py:38
  138.3 1.2 shard_map.112
  139.6 1.5 collective-permute-start.22
  141.6 8.5 %reduce-scatter.2.cloned.1.call-done = bf16[1,336,512]{2,1,0:T(8,128)(2,1)} async-done(((bf16[8,336,512]{2,1,0:T(8,128)(2,1)}), bf16[1,336,512]{2,1,0:T(8,128)(2,1)}) %reduce-scatter.2.cloned.1.call-update) | async-done | bytes 344080 | tf_op jit(solution)/shard_map/reduce_scatter | solution.py:442
  150.1 1.0 slice_bitcast_fusion
  151.7 3.4 %collective-permute-done.18.a_ref = bf16[672,512]{1,0:T(8,128)(2,1)S(1)} collective-permute-done((bf16[672,512]{1,0:T(8,128)(2,1)S(1)}, bf16[672,512]{1,0:T(8,128)(2,1)S(1)}, u32[]{:S(2)}, u32[]{:S(2)}) %collective-permute-start.18) | collective-permute-done | bytes 688160 | tf_op jit(solution)/shard_map/ppermute | solution.py:38
  155.1 2.2 %collective-permute-done.23.c_ref = bf16[672,512]{1,0:T(8,128)(2,1)S(1)} collective-permute-done((bf16[672,512]{1,0:T(8,128)(2,1)}, bf16[672,512]{1,0:T(8,128)(2,1)S(1)}, u32[]{:S(2)}, u32[]{:S(2)}) %collective-permute-start.23) | collective-permute-done | bytes 688160 | tf_op jit(solution)/shard_map/ppermute | solution.py:34
  157.3 1.2 shard_map.113
  (94 shorter events, 13.1 us)
Async XLA Ops:
  7.2 142.9 %reduce-scatter.2.cloned.1.call-start = ((), (), s32[]{:S(2)}) async-start(), calls=%async_computation.1 | async-start | bytes 3096576 | tf_op jit(solution)/shard_map/reduce_scatter | solution.py:442
  7.2 20.0 %collective-permute-start.3 = (bf16[672,512]{1,0:T(8,128)(2,1)}, bf16[672,512]{1,0:T(8,128)(2,1)}, u32[]{:S(2)}, u32[]{:S(2)}) collective-permute-start(bf16[672,512]{1,0:T(8,128)(2,1)} %bitcast.91), channel_id=1, source_target_pairs={{0,4},{1,5},{2,6},{3,7},{4,0},{5,1},{6,2},{7,3},{8,12},{9,13},{10,... | collective-permute-start | bytes 2064392 | tf_op jit(solution)/shard_map/ppermute | solution.py:38
  9.4 17.7 %collective-permute-start.1 = (bf16[672,512]{1,0:T(8,128)(2,1)}, bf16[672,512]{1,0:T(8,128)(2,1)S(1)}, u32[]{:S(2)}, u32[]{:S(2)}) collective-permute-start(bf16[672,512]{1,0:T(8,128)(2,1)} %bitcast.92), channel_id=1, source_target_pairs={{0,3},{1,0},{2,1},{3,2},{4,7},{5,4},{6,5},{7,6},{8,11},{9,8},{10,9... | collective-permute-start | bytes 2064392 | tf_op jit(solution)/shard_map/ppermute | solution.py:34
  12.4 18.0 %collective-permute-start = (bf16[672,512]{1,0:T(8,128)(2,1)}, bf16[672,512]{1,0:T(8,128)(2,1)S(1)}, u32[]{:S(2)}, u32[]{:S(2)}) collective-permute-start(bf16[672,512]{1,0:T(8,128)(2,1)} %bitcast.93), channel_id=1, source_target_pairs={{0,1},{1,2},{2,3},{3,0},{4,5},{5,6},{6,7},{7,4},{8,9},{9,10},{10,1... | collective-permute-start | bytes 2064392 | tf_op jit(solution)/shard_map/ppermute | solution.py:34
  15.8 2.4 %copy-start.9 = (bf16[5376,512]{1,0:T(8,128)(2,1)}, bf16[5376,512]{1,0:T(8,128)(2,1)S(1)}, u32[]{:S(2)}) copy-start(bf16[5376,512]{1,0:T(8,128)(2,1)S(1)} %pad_maximum_fusion) | copy-start | bytes 16515076
  28.3 7.1 %copy-start.13 = (bf16[512,672]{0,1:T(8,128)(2,1)S(1)}, bf16[512,672]{0,1:T(8,128)(2,1)}, u32[]{:S(2)}) copy-start(bf16[512,672]{0,1:T(8,128)(2,1)} %param.7) | copy-start | bytes 2064388
  30.5 7.7 %slice-start = ((s8[5505024]{0:T(1024)(128)(4,1)}), s8[4194304]{0:T(1024)(128)(4,1)S(1)}, s32[]{:S(2)}) async-start(s8[5505024]{0:T(1024)(128)(4,1)} %bitcast.76), calls=%async_computation.2 | async-start | bytes 8388608
  30.7 18.1 %collective-permute-start.6 = (bf16[672,512]{1,0:T(8,128)(2,1)S(1)}, bf16[672,512]{1,0:T(8,128)(2,1)S(1)}, u32[]{:S(2)}, u32[]{:S(2)}) collective-permute-start(bf16[672,512]{1,0:T(8,128)(2,1)S(1)} %get-tuple-element.98), channel_id=1, source_target_pairs={{0,1},{1,2},{2,3},{3,0},{4,5},{5,6},{6,7},{7,4},{8,9},{9,10},{10,1... | collective-permute-start | bytes 2064392 | tf_op jit(solution)/shard_map/ppermute | solution.py:34
  30.8 17.3 %collective-permute-start.2 = (bf16[672,512]{1,0:T(8,128)(2,1)S(1)}, bf16[672,512]{1,0:T(8,128)(2,1)S(1)}, u32[]{:S(2)}, u32[]{:S(2)}) collective-permute-start(bf16[672,512]{1,0:T(8,128)(2,1)S(1)} %get-tuple-element.99), channel_id=1, source_target_pairs={{0,4},{1,5},{2,6},{3,7},{4,0},{5,1},{6,2},{7,3},{8,12},{9,13},{10,... | collective-permute-start | bytes 2064392 | tf_op jit(solution)/shard_map/ppermute | solution.py:38
  32.3 15.8 %collective-permute-start.7 = (bf16[672,512]{1,0:T(8,128)(2,1)S(1)}, bf16[672,512]{1,0:T(8,128)(2,1)S(1)}, u32[]{:S(2)}, u32[]{:S(2)}) collective-permute-start(bf16[672,512]{1,0:T(8,128)(2,1)S(1)} %get-tuple-element.100), channel_id=1, source_target_pairs={{0,3},{1,0},{2,1},{3,2},{4,7},{5,4},{6,5},{7,6},{8,11},{9,8},{10,9... | collective-permute-start | bytes 2064392 | tf_op jit(solution)/shard_map/ppermute | solution.py:34
  35.4 2.8 %slice-start.1 = ((s8[5505024]{0:T(1024)(128)(4,1)}), s8[1310720]{0:T(1024)(128)(4,1)S(1)}, s32[]{:S(2)}) async-start(s8[5505024]{0:T(1024)(128)(4,1)} %bitcast.76), calls=%async_computation.3 | async-start | bytes 2621440
  36.9 2.0 %copy-start.11 = (bf16[4,2,2,168,512]{4,3,2,1,0:T(8,128)(2,1)}, bf16[4,2,2,168,512]{4,3,2,1,0:T(8,128)(2,1)S(1)}, u32[]{:S(2)}) copy-start(bf16[4,2,2,168,512]{4,3,2,1,0:T(8,128)(2,1)S(1)} %pad_maximum_fusion.1.x_ref) | copy-start | bytes 8257540
  38.2 29.6 %collective-permute-start.10 = (bf16[4,2,168,512]{3,2,1,0:T(8,128)(2,1)}, bf16[4,2,168,512]{3,2,1,0:T(8,128)(2,1)}, u32[]{:S(2)}, u32[]{:S(2)}) collective-permute-start(bf16[4,2,168,512]{3,2,1,0:T(8,128)(2,1)} %dynamic-slice_bitcast_fusion), channel_id=1, source_target_pairs={{0,8},{8,0},{16,24},{24,16},{32,40},{40,32},{48,56},{56,48},{64,72... | collective-permute-start | bytes 4128776 | tf_op jit(solution)/shard_map/ppermute | solution.py:42
  49.6 8.9 %collective-permute-start.4 = (bf16[336,512]{1,0:T(8,128)(2,1)S(1)}, bf16[336,512]{1,0:T(8,128)(2,1)S(1)}, u32[]{:S(2)}, u32[]{:S(2)}) collective-permute-start(bf16[336,512]{1,0:T(8,128)(2,1)S(1)} %get-tuple-element.47), channel_id=1, source_target_pairs={{0,1},{1,2},{2,3},{3,0},{4,5},{5,6},{6,7},{7,4},{8,9},{9,10},{10,1... | collective-permute-start | bytes 1032200 | tf_op jit(solution)/shard_map/ppermute | solution.py:34
  50.4 8.1 %collective-permute-start.5 = (bf16[336,512]{1,0:T(8,128)(2,1)S(1)}, bf16[336,512]{1,0:T(8,128)(2,1)S(1)}, u32[]{:S(2)}, u32[]{:S(2)}) collective-permute-start(bf16[336,512]{1,0:T(8,128)(2,1)S(1)} %get-tuple-element.48), channel_id=1, source_target_pairs={{0,3},{1,0},{2,1},{3,2},{4,7},{5,4},{6,5},{7,6},{8,11},{9,8},{10,9... | collective-permute-start | bytes 1032200 | tf_op jit(solution)/shard_map/ppermute | solution.py:34
  53.6 1.8 %copy-start.12 = (bf16[3,2,2,168,512]{4,3,2,1,0:T(8,128)(2,1)}, bf16[3,2,2,168,512]{4,3,2,1,0:T(8,128)(2,1)S(1)}, u32[]{:S(2)}) copy-start(bf16[3,2,2,168,512]{4,3,2,1,0:T(8,128)(2,1)S(1)} %pad_maximum_fusion.2.xb_ref) | copy-start | bytes 6193156
  54.9 4.0 %copy-start.15 = (f32[128]{0:T(128)S(1)}, f32[128]{0:T(128)}, u32[]{:S(2)}) copy-start(f32[128]{0:T(128)} %param.11) | copy-start | bytes 1540
  54.9 4.1 %copy-start.16 = (f32[128]{0:T(128)S(1)}, f32[128]{0:T(128)}, u32[]{:S(2)}) copy-start(f32[128]{0:T(128)} %param.12) | copy-start | bytes 1540
  58.6 14.0 %copy-start = (bf16[672,512]{1,0:T(8,128)(2,1)}, bf16[672,512]{1,0:T(8,128)(2,1)S(1)}, u32[]{:S(2)}) copy-start(bf16[672,512]{1,0:T(8,128)(2,1)S(1)} %pad_maximum_fusion.6.last_ref) | copy-start | bytes 2064388
  58.6 30.1 %collective-permute-start.13 = (bf16[3,2,168,512]{3,2,1,0:T(8,128)(2,1)}, bf16[3,2,168,512]{3,2,1,0:T(8,128)(2,1)}, u32[]{:S(2)}, u32[]{:S(2)}) collective-permute-start(bf16[3,2,168,512]{3,2,1,0:T(8,128)(2,1)} %dynamic-slice_bitcast_fusion.1), channel_id=1, source_target_pairs={{0,8},{8,0},{16,24},{24,16},{32,40},{40,32},{48,56},{56,48},{64,72... | collective-permute-start | bytes 3096584 | tf_op jit(solution)/shard_map/ppermute | solution.py:42
  59.9 15.5 %collective-permute-start.9 = (bf16[256,512]{1,0:T(8,128)(2,1)S(1)}, bf16[256,512]{1,0:T(8,128)(2,1)S(1)}, u32[]{:S(2)}, u32[]{:S(2)}) collective-permute-start(bf16[256,512]{1,0:T(8,128)(2,1)S(1)} %get-tuple-element.53.own_ref), channel_id=1, source_target_pairs={{0,16},{8,24},{16,32},{24,40},{32,48},{40,56},{48,64},{56,72},{64,... | collective-permute-start | bytes 786440 | tf_op jit(solution)/shard_map/ppermute | solution.py:53
  63.7 14.3 %collective-permute-start.8 = (bf16[256,512]{1,0:T(8,128)(2,1)S(1)}, bf16[256,512]{1,0:T(8,128)(2,1)S(1)}, u32[]{:S(2)}, u32[]{:S(2)}) collective-permute-start(bf16[256,512]{1,0:T(8,128)(2,1)S(1)} %get-tuple-element.53.own_ref), channel_id=1, source_target_pairs={{0,8},{8,16},{16,24},{24,32},{32,40},{40,48},{48,56},{56,64},{64,7... | collective-permute-start | bytes 786440 | tf_op jit(solution)/shard_map/ppermute | solution.py:53
  65.9 12.1 %copy-start.8 = (bf16[512,256]{1,0:T(8,128)(2,1)S(1)}, bf16[512,256]{1,0:T(8,128)(2,1)}, u32[]{:S(2)}) copy-start(bf16[512,256]{1,0:T(8,128)(2,1)} %go_ref.1) | copy-start | bytes 786436
  65.9 22.7 %collective-permute-start.14 = (bf16[1,2,168,512]{3,2,1,0:T(8,128)(2,1)S(1)}, bf16[1,2,168,512]{3,2,1,0:T(8,128)(2,1)S(1)}, u32[]{:S(2)}, u32[]{:S(2)}) collective-permute-start(bf16[1,2,168,512]{3,2,1,0:T(8,128)(2,1)S(1)} %dynamic-slice_bitcast_fusion.3), channel_id=1, source_target_pairs={{0,8},{8,0},{16,24},{24,16},{32,40},{40,32},{48,56},{56,48},{64,72... | collective-permute-start | bytes 1032200 | tf_op jit(solution)/shard_map/ppermute | solution.py:42
  83.0 11.2 %collective-permute-start.11 = (bf16[2,512,128]{2,1,0:T(8,128)(2,1)S(1)}, bf16[2,512,128]{2,1,0:T(8,128)(2,1)S(1)}, u32[]{:S(2)}, u32[]{:S(2)}) collective-permute-start(bf16[2,512,128]{2,1,0:T(8,128)(2,1)S(1)} %get-tuple-element.58), channel_id=1, source_target_pairs={{8,0},{16,8},{24,16},{32,24},{40,32},{48,40},{56,48},{64,56},{72,6... | collective-permute-start | bytes 786440 | tf_op jit(solution)/shard_map/ppermute | solution.py:53
  85.0 10.6 %collective-permute-start.12 = (bf16[2,512,128]{2,1,0:T(8,128)(2,1)S(1)}, bf16[2,512,128]{2,1,0:T(8,128)(2,1)S(1)}, u32[]{:S(2)}, u32[]{:S(2)}) collective-permute-start(bf16[2,512,128]{2,1,0:T(8,128)(2,1)S(1)} %get-tuple-element.59), channel_id=1, source_target_pairs={{16,0},{24,8},{32,16},{40,24},{48,32},{56,40},{64,48},{72,56},{80,... | collective-permute-start | bytes 786440 | tf_op jit(solution)/shard_map/ppermute | solution.py:53
  88.6 0.7 copy-start.14
  95.8 0.8 copy-start.1
  95.8 4.3 %copy-start.10 = (bf16[4,2,2,168,1024]{4,3,2,1,0:T(8,128)(2,1)S(1)}, bf16[4,2,2,168,1024]{4,3,2,1,0:T(8,128)(2,1)}, u32[]{:S(2)}) copy-start(bf16[4,2,2,168,1024]{4,3,2,1,0:T(8,128)(2,1)} %shard_map.105) | copy-start | bytes 16515076
  95.9 4.3 %collective-permute-start.15 = (bf16[512,512]{1,0:T(8,128)(2,1)S(1)}, bf16[512,512]{1,0:T(8,128)(2,1)S(1)}, u32[]{:S(2)}, u32[]{:S(2)}) collective-permute-start(bf16[512,512]{1,0:T(8,128)(2,1)S(1)} %shard_map.106.d_ref), channel_id=1, source_target_pairs={{0,8},{8,0},{16,24},{24,16},{32,40},{40,32},{48,56},{56,48},{64,72... | collective-permute-start | bytes 1572872 | tf_op jit(solution)/shard_map/ppermute | solution.py:42
  105.7 1.0 copy-start.18
  105.7 2.4 %copy-start.17 = (bf16[336,512]{1,0:T(8,128)(2,1)S(1)}, bf16[336,512]{1,0:T(8,128)(2,1)}, u32[]{:S(2)}) copy-start(bf16[336,512]{1,0:T(8,128)(2,1)} %get-tuple-element.69) | copy-start | bytes 1032196
  106.7 11.0 %collective-permute-start.20 = (bf16[336,512]{1,0:T(8,128)(2,1)S(1)}, bf16[336,512]{1,0:T(8,128)(2,1)S(1)}, u32[]{:S(2)}, u32[]{:S(2)}) collective-permute-start(bf16[336,512]{1,0:T(8,128)(2,1)S(1)} %copy-done.18), channel_id=1, source_target_pairs={{0,1},{1,2},{2,3},{3,0},{4,5},{5,6},{6,7},{7,4},{8,9},{9,10},{10,1... | collective-permute-start | bytes 1032200 | tf_op jit(solution)/shard_map/ppermute | solution.py:34
  108.1 9.6 %collective-permute-start.19 = (bf16[336,512]{1,0:T(8,128)(2,1)S(1)}, bf16[336,512]{1,0:T(8,128)(2,1)S(1)}, u32[]{:S(2)}, u32[]{:S(2)}) collective-permute-start(bf16[336,512]{1,0:T(8,128)(2,1)S(1)} %copy-done.17), channel_id=1, source_target_pairs={{0,3},{1,0},{2,1},{3,2},{4,7},{5,4},{6,5},{7,6},{8,11},{9,8},{10,9... | collective-permute-start | bytes 1032200 | tf_op jit(solution)/shard_map/ppermute | solution.py:34
  115.4 16.9 %collective-permute-start.16 = (bf16[672,512]{1,0:T(8,128)(2,1)}, bf16[672,512]{1,0:T(8,128)(2,1)S(1)}, u32[]{:S(2)}, u32[]{:S(2)}) collective-permute-start(bf16[672,512]{1,0:T(8,128)(2,1)} %get-tuple-element.73), channel_id=1, source_target_pairs={{0,3},{1,0},{2,1},{3,2},{4,7},{5,4},{6,5},{7,6},{8,11},{9,8},{10,9... | collective-permute-start | bytes 2064392 | tf_op jit(solution)/shard_map/ppermute | solution.py:34
  117.3 17.6 %collective-permute-start.17 = (bf16[672,512]{1,0:T(8,128)(2,1)}, bf16[672,512]{1,0:T(8,128)(2,1)S(1)}, u32[]{:S(2)}, u32[]{:S(2)}) collective-permute-start(bf16[672,512]{1,0:T(8,128)(2,1)} %get-tuple-element.74), channel_id=1, source_target_pairs={{0,1},{1,2},{2,3},{3,0},{4,5},{5,6},{6,7},{7,4},{8,9},{9,10},{10,1... | collective-permute-start | bytes 2064392 | tf_op jit(solution)/shard_map/ppermute | solution.py:34
  117.7 1.1 copy-start.6
  119.0 19.4 %collective-permute-start.21 = (bf16[672,512]{1,0:T(8,128)(2,1)S(1)}, bf16[672,512]{1,0:T(8,128)(2,1)S(1)}, u32[]{:S(2)}, u32[]{:S(2)}) collective-permute-start(bf16[672,512]{1,0:T(8,128)(2,1)S(1)} %shard_map.111), channel_id=1, source_target_pairs={{0,4},{1,5},{2,6},{3,7},{4,0},{5,1},{6,2},{7,3},{8,12},{9,13},{10,... | collective-permute-start | bytes 2064392 | tf_op jit(solution)/shard_map/ppermute | solution.py:38
  127.5 10.8 %copy-start.4 = (bf16[672,512]{1,0:T(8,128)(2,1)S(1)}, bf16[672,512]{1,0:T(8,128)(2,1)}, u32[]{:S(2)}) copy-start(bf16[672,512]{1,0:T(8,128)(2,1)} %get-tuple-element.81.below_ref) | copy-start | bytes 2064388
  127.5 10.8 %copy-start.5 = (bf16[672,512]{1,0:T(8,128)(2,1)S(1)}, bf16[672,512]{1,0:T(8,128)(2,1)}, u32[]{:S(2)}) copy-start(bf16[672,512]{1,0:T(8,128)(2,1)} %get-tuple-element.82.above_ref) | copy-start | bytes 2064388
  135.0 1.1 copy-start.7
  136.2 21.0 %copy-start.3 = (bf16[672,512]{1,0:T(8,128)(2,1)S(1)}, bf16[672,512]{1,0:T(8,128)(2,1)}, u32[]{:S(2)}) copy-start(bf16[672,512]{1,0:T(8,128)(2,1)} %get-tuple-element.67.mine_ref) | copy-start | bytes 2064388
  136.2 18.8 %collective-permute-start.18 = (bf16[672,512]{1,0:T(8,128)(2,1)S(1)}, bf16[672,512]{1,0:T(8,128)(2,1)S(1)}, u32[]{:S(2)}, u32[]{:S(2)}) collective-permute-start(bf16[672,512]{1,0:T(8,128)(2,1)S(1)} %shard_map.110), channel_id=1, source_target_pairs={{0,4},{1,5},{2,6},{3,7},{4,0},{5,1},{6,2},{7,3},{8,12},{9,13},{10,... | collective-permute-start | bytes 2064392 | tf_op jit(solution)/shard_map/ppermute | solution.py:38
  139.6 15.5 %collective-permute-start.22 = (bf16[672,512]{1,0:T(8,128)(2,1)}, bf16[672,512]{1,0:T(8,128)(2,1)S(1)}, u32[]{:S(2)}, u32[]{:S(2)}) collective-permute-start(bf16[672,512]{1,0:T(8,128)(2,1)} %get-tuple-element.85), channel_id=1, source_target_pairs={{0,3},{1,0},{2,1},{3,2},{4,7},{5,4},{6,5},{7,6},{8,11},{9,8},{10,9... | collective-permute-start | bytes 2064392 | tf_op jit(solution)/shard_map/ppermute | solution.py:34
  141.1 16.2 %collective-permute-start.23 = (bf16[672,512]{1,0:T(8,128)(2,1)}, bf16[672,512]{1,0:T(8,128)(2,1)S(1)}, u32[]{:S(2)}, u32[]{:S(2)}) collective-permute-start(bf16[672,512]{1,0:T(8,128)(2,1)} %get-tuple-element.86), channel_id=1, source_target_pairs={{0,1},{1,2},{2,3},{3,0},{4,5},{5,6},{6,7},{7,4},{8,9},{9,10},{10,1... | collective-permute-start | bytes 2064392 | tf_op jit(solution)/shard_map/ppermute | solution.py:34
  150.1 8.4 %copy-start.2 = (bf16[1,336,512]{2,1,0:T(8,128)(2,1)S(1)}, bf16[1,336,512]{2,1,0:T(8,128)(2,1)}, u32[]{:S(2)}) copy-start(bf16[1,336,512]{2,1,0:T(8,128)(2,1)} %reduce-scatter.2.cloned.1.call-done) | copy-start | bytes 1032196
  151.1 7.4 %collective-permute-start.24 = (bf16[168,512]{1,0:T(8,128)(2,1)S(1)}, bf16[168,512]{1,0:T(8,128)(2,1)S(1)}, u32[]{:S(2)}, u32[]{:S(2)}) collective-permute-start(bf16[168,512]{1,0:T(8,128)(2,1)S(1)} %slice_bitcast_fusion), channel_id=1, source_target_pairs={{0,128},{8,136},{16,144},{24,152},{32,160},{40,168},{48,176},{56,1... | collective-permute-start | bytes 516104 | tf_op jit(solution)/shard_map/ppermute | solution.py:47
Sparse Core Ops, SparseCore 0:
  105.8 44.2 reduce-scatter.1

commit v4 on v3

--- a/solution.py
+++ b/solution.py
@@ -120,9 +120,11 @@
 
 def first_terms(own_ref, w_ref, d_ref, top_ref, bottom_ref):
     t = jnp.dot(w_ref[0], d_ref[...], preferred_element_type=f32).astype(bf16)
-    lo, hi = halves(w_ref)
-    top_ref[...] = t[lo]
-    bottom_ref[...] = t[hi]
+    for n, ref in enumerate((top_ref, bottom_ref)):
+
+        @pl.when(pl.program_id(0) == n)
+        def _(ref=ref):
+            ref[...] = t
 
 
 def second_terms(own_ref, w_ref, d_ref, side_ref, down_ref, up_ref):
@@ -223,7 +225,21 @@
             [whole(o) for o in outs],
         )
 
-    top, bottom = terms(first_terms, 2.0, 0, 1, [part, part])
+    whole = lambda v: pl.BlockSpec(v.shape, lambda i, t: (0,) * len(v.shape))
+    to_far = 1 + len(RELS)
+    top, bottom = with_table(
+        first_terms,
+        2.0,
+        (2,),
+        table,
+        [
+            pl.BlockSpec((1, feats // 2, cols), lambda i, t: (t[to_far], i, 0)),
+            whole(d_all),
+        ],
+        (w_own, d_all),
+        [part, part],
+        [whole(part), whole(part)],
+    )
     extra = beside(top)
     top, bottom = y_step(top, -1), y_step(bottom, 1)
     side, down, up = terms(second_terms, 4.5, 1, 3, [full] * 3, extra)

time: 167 us -> 167 us (level)
  no operation moved by 1% of the time
where the time goes in v4:
time: 167 us; the launch traced here: 166 us
  waiting for transfers between devices  45.9 us (27%)
  starting transfers between devices  39.7 us (24%)
  Pallas kernels  34.9 us (21%)
  between operations  14.5 us (9%)
  local copies, waits for them, and re-layouts  13.2 us (8%)
  matrix products  12.2 us (7%)
  other arithmetic  5.96 us (4%)
    pallas_call x5, Pallas kernels, with_table(): pl.pallas_call(kernel, out_shape=outs, grid_spec=pltpu.PrefetchScalarGrid...  25.4 us
    ppermute x12, waiting for transfers between devices, y_step(): return lax.ppermute(v, 'tp', tp_perm(0, d))  20.4 us
    ppermute x12, starting transfers between devices, y_step(): return lax.ppermute(v, 'tp', tp_perm(0, d))  17.3 us
    ppermute x4, starting transfers between devices, from_behind(): return lax.ppermute(block, 'ctx', route)  11.5 us
    ppermute x4, waiting for transfers between devices, x_swap(): return lax.ppermute(v, 'tp', tp_perm(1, 0))  10.1 us
    pallas_call x8, Pallas kernels, run(): pl.pallas_call(kernel, out_shape=outs, in_specs=in_specs, out_specs=jax.t...  9.52 us
    reduce_scatter x1, waiting for transfers between devices, along_z(): lax.psum_scatter(g, 'ctx', scatter_dimension=0, tiled=True, axis_index_gr...  8.47 us
    ppermute x4, starting transfers between devices, x_swap(): return lax.ppermute(v, 'tp', tp_perm(1, 0))  7.88 us
  transfers between devices with their start and end apart: 26, of which 13 were waited for; matrix products, arithmetic and copies ran while one was open for 11% of the time, Pallas kernels for 20%

profile of v4, /device:TPU:2, one launch (start us, length us, event | category | flops | bytes accessed | tf_op | source)
XLA Modules:
  0.0 166.3 jit_solution(5779168431447043533)
XLA Ops:
  7.2 2.2 %collective-permute-start.3 = (bf16[672,512]{1,0:T(8,128)(2,1)}, bf16[672,512]{1,0:T(8,128)(2,1)}, u32[]{:S(2)}, u32[]{:S(2)}) collective-permute-start(bf16[672,512]{1,0:T(8,128)(2,1)} %bitcast.91), channel_id=1, source_target_pairs={{0,4},{1,5},{2,6},{3,7},{4,0},{5,1},{6,2},{7,3},{8,12},{9,13},{10,... | collective-permute-start | bytes 2064392 | tf_op jit(solution)/shard_map/ppermute | solution.py:38
  9.4 3.0 %collective-permute-start.1 = (bf16[672,512]{1,0:T(8,128)(2,1)}, bf16[672,512]{1,0:T(8,128)(2,1)S(1)}, u32[]{:S(2)}, u32[]{:S(2)}) collective-permute-start(bf16[672,512]{1,0:T(8,128)(2,1)} %bitcast.92), channel_id=1, source_target_pairs={{0,3},{1,0},{2,1},{3,2},{4,7},{5,4},{6,5},{7,6},{8,11},{9,8},{10,9... | collective-permute-start | bytes 2064392 | tf_op jit(solution)/shard_map/ppermute | solution.py:34
  12.4 3.4 %pad_maximum_fusion = bf16[5376,512]{1,0:T(8,128)(2,1)S(1)} fusion(bf16[5376,128]{1,0:T(8,128)(2,1)} %param.10, bf16[5376,128]{1,0:T(8,128)(2,1)} %param.9, bf16[5376,256]{1,0:T(8,128)(2,1)} %param.8), kind=kLoop, calls=%fused_computation | loop fusion | flops 16515072 | bytes 11010048 | tf_op jit(solution)/shard_map/concatenate | solution.py:407
  15.8 2.4 %copy-done.9 = bf16[5376,512]{1,0:T(8,128)(2,1)} copy-done((bf16[5376,512]{1,0:T(8,128)(2,1)}, bf16[5376,512]{1,0:T(8,128)(2,1)S(1)}, u32[]{:S(2)}) %copy-start.9) | copy-done | bytes 5505048
  19.8 1.9 %fusion.14 = f32[512,512]{1,0:T(8,128)S(1)} fusion(bf16[512,672]{0,1:T(8,128)(2,1)} %param.7, bf16[8,672,512]{2,1,0:T(8,128)(2,1)} %bitcast.72, s32[]{:T(128)S(6)} %select_n.173), kind=kOutput, calls=%fused_computation.31 | convolution fusion | flops 352321536 | bytes 2424836 | tf_op jit(solution)/shard_map/dot_general | solution.py:416
  21.7 5.4 %collective-permute-done.1 = bf16[672,512]{1,0:T(8,128)(2,1)S(1)} collective-permute-done((bf16[672,512]{1,0:T(8,128)(2,1)}, bf16[672,512]{1,0:T(8,128)(2,1)S(1)}, u32[]{:S(2)}, u32[]{:S(2)}) %collective-permute-start.1) | collective-permute-done | bytes 688160 | tf_op jit(solution)/shard_map/ppermute | solution.py:34
  27.2 1.1 fusion.33
  28.3 2.1 %collective-permute-done = bf16[672,512]{1,0:T(8,128)(2,1)S(1)} collective-permute-done((bf16[672,512]{1,0:T(8,128)(2,1)}, bf16[672,512]{1,0:T(8,128)(2,1)S(1)}, u32[]{:S(2)}, u32[]{:S(2)}) %collective-permute-start) | collective-permute-done | bytes 688160 | tf_op jit(solution)/shard_map/ppermute | solution.py:34
  30.8 1.5 collective-permute-start.2
  32.3 3.1 %collective-permute-start.7 = (bf16[672,512]{1,0:T(8,128)(2,1)S(1)}, bf16[672,512]{1,0:T(8,128)(2,1)S(1)}, u32[]{:S(2)}, u32[]{:S(2)}) collective-permute-start(bf16[672,512]{1,0:T(8,128)(2,1)S(1)} %get-tuple-element.100), channel_id=1, source_target_pairs={{0,3},{1,0},{2,1},{3,2},{4,7},{5,4},{6,5},{7,6},{8,11},{9,8},{10,9... | collective-permute-start | bytes 2064392 | tf_op jit(solution)/shard_map/ppermute | solution.py:34
  35.4 1.5 pad_maximum_fusion.1.x_ref
  36.9 1.3 dynamic-slice_bitcast_fusion
  38.9 1.7 %fusion.10 = f32[512,512]{1,0:T(8,128)S(1)} fusion(bf16[672,512]{1,0:T(8,128)(2,1)} %collective-permute-done.3, bf16[8,672,512]{2,1,0:T(8,128)(2,1)S(1)} %bitcast.79, s32[]{:T(128)S(6)} %select_n.176), kind=kOutput, calls=%fused_computation.27 | convolution fusion | flops 352321536 | bytes 2424836 | tf_op jit(solution)/shard_map/dot_general | solution.py:416
  41.2 6.8 %collective-permute-done.2 = bf16[672,512]{1,0:T(8,128)(2,1)S(1)} collective-permute-done((bf16[672,512]{1,0:T(8,128)(2,1)S(1)}, bf16[672,512]{1,0:T(8,128)(2,1)S(1)}, u32[]{:S(2)}, u32[]{:S(2)}) %collective-permute-start.2) | collective-permute-done | bytes 688160 | tf_op jit(solution)/shard_map/ppermute | solution.py:38
  50.4 3.0 %collective-permute-start.5 = (bf16[336,512]{1,0:T(8,128)(2,1)S(1)}, bf16[336,512]{1,0:T(8,128)(2,1)S(1)}, u32[]{:S(2)}, u32[]{:S(2)}) collective-permute-start(bf16[336,512]{1,0:T(8,128)(2,1)S(1)} %get-tuple-element.48), channel_id=1, source_target_pairs={{0,3},{1,0},{2,1},{3,2},{4,7},{5,4},{6,5},{7,6},{8,11},{9,8},{10,9... | collective-permute-start | bytes 1032200 | tf_op jit(solution)/shard_map/ppermute | solution.py:34
  53.7 1.2 dynamic-slice_bitcast_fusion.1
  55.5 3.0 %collective-permute-done.4 = bf16[336,512]{1,0:T(8,128)(2,1)S(1)} collective-permute-done((bf16[336,512]{1,0:T(8,128)(2,1)S(1)}, bf16[336,512]{1,0:T(8,128)(2,1)S(1)}, u32[]{:S(2)}, u32[]{:S(2)}) %collective-permute-start.4) | collective-permute-done | bytes 344096 | tf_op jit(solution)/shard_map/ppermute | solution.py:34
  59.9 3.8 %collective-permute-start.9 = (bf16[256,512]{1,0:T(8,128)(2,1)S(1)}, bf16[256,512]{1,0:T(8,128)(2,1)S(1)}, u32[]{:S(2)}, u32[]{:S(2)}) collective-permute-start(bf16[256,512]{1,0:T(8,128)(2,1)S(1)} %get-tuple-element.53.own_ref), channel_id=1, source_target_pairs={{0,16},{8,24},{16,32},{24,40},{32,48},{40,56},{48,64},{56,72},{64,... | collective-permute-start | bytes 786440 | tf_op jit(solution)/shard_map/ppermute | solution.py:53
  63.7 2.1 %collective-permute-start.8 = (bf16[256,512]{1,0:T(8,128)(2,1)S(1)}, bf16[256,512]{1,0:T(8,128)(2,1)S(1)}, u32[]{:S(2)}, u32[]{:S(2)}) collective-permute-start(bf16[256,512]{1,0:T(8,128)(2,1)S(1)} %get-tuple-element.53.own_ref), channel_id=1, source_target_pairs={{0,8},{8,16},{16,24},{24,32},{32,40},{40,48},{48,56},{56,64},{64,7... | collective-permute-start | bytes 786440 | tf_op jit(solution)/shard_map/ppermute | solution.py:53
  65.9 1.9 %collective-permute-start.14 = (bf16[1,2,168,512]{3,2,1,0:T(8,128)(2,1)S(1)}, bf16[1,2,168,512]{3,2,1,0:T(8,128)(2,1)S(1)}, u32[]{:S(2)}, u32[]{:S(2)}) collective-permute-start(bf16[1,2,168,512]{3,2,1,0:T(8,128)(2,1)S(1)} %dynamic-slice_bitcast_fusion.3), channel_id=1, source_target_pairs={{0,8},{8,0},{16,24},{24,16},{32,40},{40,32},{48,56},{56,48},{64,72... | collective-permute-start | bytes 1032200 | tf_op jit(solution)/shard_map/ppermute | solution.py:42
  67.8 4.7 %shard_map.103.begun_ref = bf16[4,2,2,168,1024]{4,3,2,1,0:T(8,128)(2,1)} custom-call(s32[18]{0:T(128)} %stack.78.table_ref.own_ref, bf16[4,2,2,168,512]{4,3,2,1,0:T(8,128)(2,1)} %copy-done.11, bf16[4,2,168,512]{3,2,1,0:T(8,128)(2,1)} %collective-permute-done.10.o_ref), custom_call_target="tpu_custom_call" | custom-call | bytes 13600000 | tf_op jit(solution)/shard_map/pallas_call | solution.py:189
  72.5 2.9 %collective-permute-done.9.m2_ref = bf16[256,512]{1,0:T(8,128)(2,1)S(1)} collective-permute-done((bf16[256,512]{1,0:T(8,128)(2,1)S(1)}, bf16[256,512]{1,0:T(8,128)(2,1)S(1)}, u32[]{:S(2)}, u32[]{:S(2)}) %collective-permute-start.9) | collective-permute-done | bytes 262176 | tf_op jit(solution)/shard_map/ppermute | solution.py:53
  75.4 2.6 %collective-permute-done.8.m1_ref = bf16[256,512]{1,0:T(8,128)(2,1)S(1)} collective-permute-done((bf16[256,512]{1,0:T(8,128)(2,1)S(1)}, bf16[256,512]{1,0:T(8,128)(2,1)S(1)}, u32[]{:S(2)}, u32[]{:S(2)}) %collective-permute-start.8) | collective-permute-done | bytes 262176 | tf_op jit(solution)/shard_map/ppermute | solution.py:53
  78.0 5.0 %shard_map.104 = (bf16[256,512]{1,0:T(8,128)(2,1)S(1)}, f32[2,512,128]{2,1,0:T(8,128)S(1)}, bf16[2,512,128]{2,1,0:T(8,128)(2,1)S(1)}, bf16[2,512,128]{2,1,0:T(8,128)(2,1)S(1)}) custom-call(s32[1]{0:T(128)} %bitcast.11.ctx_ref, bf16[256,512]{1,0:T(8,128)(2,1)S(1)} %get-tuple-element.51.q_ref, f32[512,512]{1,0:T(8,128)S(1)} %get-tuple-element.52.raw_ref, ...), custom_call_target="tpu_custom_call" | custom-call | bytes 18700000 | tf_op jit(solution)/shard_map/pallas_call | solution.py:96
  83.0 1.9 %collective-permute-start.11 = (bf16[2,512,128]{2,1,0:T(8,128)(2,1)S(1)}, bf16[2,512,128]{2,1,0:T(8,128)(2,1)S(1)}, u32[]{:S(2)}, u32[]{:S(2)}) collective-permute-start(bf16[2,512,128]{2,1,0:T(8,128)(2,1)S(1)} %get-tuple-element.58), channel_id=1, source_target_pairs={{8,0},{16,8},{24,16},{32,24},{40,32},{48,40},{56,48},{64,56},{72,6... | collective-permute-start | bytes 786440 | tf_op jit(solution)/shard_map/ppermute | solution.py:53
  85.0 3.6 %collective-permute-start.12 = (bf16[2,512,128]{2,1,0:T(8,128)(2,1)S(1)}, bf16[2,512,128]{2,1,0:T(8,128)(2,1)S(1)}, u32[]{:S(2)}, u32[]{:S(2)}) collective-permute-start(bf16[2,512,128]{2,1,0:T(8,128)(2,1)S(1)} %get-tuple-element.59), channel_id=1, source_target_pairs={{16,0},{24,8},{32,16},{40,24},{48,32},{56,40},{64,48},{72,56},{80,... | collective-permute-start | bytes 786440 | tf_op jit(solution)/shard_map/ppermute | solution.py:53
  89.3 4.9 %shard_map.105 = bf16[4,2,2,168,1024]{4,3,2,1,0:T(8,128)(2,1)} custom-call(s32[18]{0:T(128)} %stack.78.table_ref.own_ref, bf16[3,2,2,168,512]{4,3,2,1,0:T(8,128)(2,1)} %copy-done.12, bf16[3,2,168,512]{3,2,1,0:T(8,128)(2,1)} %collective-permute-done.13.ob_ref, bf16[1,2,2,168,512]{4,3,2,1,0:T(8,128)(2,1)} %bitcast.68, ...), custom_call_target="tpu_custom_call", output_to_operand_aliasing={{}: (5, {})} | custom-call | bytes 13600000 | tf_op jit(solution)/shard_map/pallas_call | solution.py:189
  94.2 1.3 collective-permute-done.12.r2_ref
  96.7 3.8 %shard_map.108 = (bf16[336,512]{1,0:T(8,128)(2,1)}, bf16[336,512]{1,0:T(8,128)(2,1)}) custom-call(s32[18]{0:T(128)} %stack.78.table_ref.own_ref, bf16[8,672,512]{2,1,0:T(8,128)(2,1)} %bitcast.73, bf16[512,512]{1,0:T(8,128)(2,1)} %copy-done.1), custom_call_target="tpu_custom_call" | custom-call | bytes 6800000 | tf_op jit(solution)/shard_map/pallas_call | solution.py:189
  100.4 5.5 %convolution_convert_fusion = bf16[8,336,512]{2,1,0:T(8,128)(2,1)} fusion(bf16[8,336,1024]{2,1,0:T(8,128)(2,1)S(1)} %bitcast.84, bf16[512,512]{1,0:T(8,128)(2,1)S(1)} %collective-permute-done.15, bf16[512,512]{1,0:T(8,128)(2,1)} %copy-done.1), kind=kOutput, calls=%fused_computation.2 | convolution fusion | flops 2822045696 | bytes 9306112 | tf_op jit(solution)/shard_map/dot_general | solution.py:521
  106.9 1.5 collective-permute-start.20
  108.3 1.8 %collective-permute-start.19 = (bf16[336,512]{1,0:T(8,128)(2,1)S(1)}, bf16[336,512]{1,0:T(8,128)(2,1)S(1)}, u32[]{:S(2)}, u32[]{:S(2)}) collective-permute-start(bf16[336,512]{1,0:T(8,128)(2,1)S(1)} %copy-done.17), channel_id=1, source_target_pairs={{0,3},{1,0},{2,1},{3,2},{4,7},{5,4},{6,5},{7,6},{8,11},{9,8},{10,9... | collective-permute-start | bytes 1032200 | tf_op jit(solution)/shard_map/ppermute | solution.py:34
  110.1 5.5 %shard_map.109 = (bf16[672,512]{1,0:T(8,128)(2,1)}, bf16[672,512]{1,0:T(8,128)(2,1)}, bf16[672,512]{1,0:T(8,128)(2,1)}) custom-call(s32[18]{0:T(128)} %stack.78.table_ref.own_ref, bf16[8,672,512]{2,1,0:T(8,128)(2,1)} %bitcast.74, bf16[512,512]{1,0:T(8,128)(2,1)} %copy-done.1), custom_call_target="tpu_custom_call" | custom-call | bytes 15300000 | tf_op jit(solution)/shard_map/pallas_call | solution.py:189
  115.7 1.9 %collective-permute-start.16 = (bf16[672,512]{1,0:T(8,128)(2,1)}, bf16[672,512]{1,0:T(8,128)(2,1)S(1)}, u32[]{:S(2)}, u32[]{:S(2)}) collective-permute-start(bf16[672,512]{1,0:T(8,128)(2,1)} %get-tuple-element.73), channel_id=1, source_target_pairs={{0,3},{1,0},{2,1},{3,2},{4,7},{5,4},{6,5},{7,6},{8,11},{9,8},{10,9... | collective-permute-start | bytes 2064392 | tf_op jit(solution)/shard_map/ppermute | solution.py:34
  117.9 1.1 copy-done.6
  119.2 2.1 %collective-permute-start.21 = (bf16[672,512]{1,0:T(8,128)(2,1)S(1)}, bf16[672,512]{1,0:T(8,128)(2,1)S(1)}, u32[]{:S(2)}, u32[]{:S(2)}) collective-permute-start(bf16[672,512]{1,0:T(8,128)(2,1)S(1)} %shard_map.111), channel_id=1, source_target_pairs={{0,4},{1,5},{2,6},{3,7},{4,0},{5,1},{6,2},{7,3},{8,12},{9,13},{10,... | collective-permute-start | bytes 2064392 | tf_op jit(solution)/shard_map/ppermute | solution.py:38
  121.3 6.5 %shard_map.107 = (bf16[672,512]{1,0:T(8,128)(2,1)}, bf16[672,512]{1,0:T(8,128)(2,1)}, bf16[672,512]{1,0:T(8,128)(2,1)}, bf16[672,512]{1,0:T(8,128)(2,1)}) custom-call(s32[18]{0:T(128)} %stack.78.table_ref.own_ref, bf16[8,672,512]{2,1,0:T(8,128)(2,1)} %bitcast.75, bf16[512,512]{1,0:T(8,128)(2,1)} %copy-done.1), custom_call_target="tpu_custom_call" | custom-call | bytes 20400000 | tf_op jit(solution)/shard_map/pallas_call | solution.py:189
  127.7 4.9 %collective-permute-done.16.down_ref = bf16[672,512]{1,0:T(8,128)(2,1)S(1)} collective-permute-done((bf16[672,512]{1,0:T(8,128)(2,1)}, bf16[672,512]{1,0:T(8,128)(2,1)S(1)}, u32[]{:S(2)}, u32[]{:S(2)}) %collective-permute-start.16) | collective-permute-done | bytes 688160 | tf_op jit(solution)/shard_map/ppermute | solution.py:34
  132.6 2.6 %collective-permute-done.17.up_ref = bf16[672,512]{1,0:T(8,128)(2,1)S(1)} collective-permute-done((bf16[672,512]{1,0:T(8,128)(2,1)}, bf16[672,512]{1,0:T(8,128)(2,1)S(1)}, u32[]{:S(2)}, u32[]{:S(2)}) %collective-permute-start.17) | collective-permute-done | bytes 688160 | tf_op jit(solution)/shard_map/ppermute | solution.py:34
  135.2 1.1 copy-done.7
  136.5 2.1 %collective-permute-start.18 = (bf16[672,512]{1,0:T(8,128)(2,1)S(1)}, bf16[672,512]{1,0:T(8,128)(2,1)S(1)}, u32[]{:S(2)}, u32[]{:S(2)}) collective-permute-start(bf16[672,512]{1,0:T(8,128)(2,1)S(1)} %shard_map.110), channel_id=1, source_target_pairs={{0,4},{1,5},{2,6},{3,7},{4,0},{5,1},{6,2},{7,3},{8,12},{9,13},{10,... | collective-permute-start | bytes 2064392 | tf_op jit(solution)/shard_map/ppermute | solution.py:38
  138.6 1.2 shard_map.112
  139.8 1.5 collective-permute-start.22
  141.8 8.5 %reduce-scatter.2.cloned.1.call-done = bf16[1,336,512]{2,1,0:T(8,128)(2,1)} async-done(((bf16[8,336,512]{2,1,0:T(8,128)(2,1)}), bf16[1,336,512]{2,1,0:T(8,128)(2,1)}) %reduce-scatter.2.cloned.1.call-update) | async-done | bytes 344080 | tf_op jit(solution)/shard_map/reduce_scatter | solution.py:458
  150.3 1.0 slice_bitcast_fusion
  152.0 3.3 %collective-permute-done.18.a_ref = bf16[672,512]{1,0:T(8,128)(2,1)S(1)} collective-permute-done((bf16[672,512]{1,0:T(8,128)(2,1)S(1)}, bf16[672,512]{1,0:T(8,128)(2,1)S(1)}, u32[]{:S(2)}, u32[]{:S(2)}) %collective-permute-start.18) | collective-permute-done | bytes 688160 | tf_op jit(solution)/shard_map/ppermute | solution.py:38
  155.3 2.2 %collective-permute-done.23.c_ref = bf16[672,512]{1,0:T(8,128)(2,1)S(1)} collective-permute-done((bf16[672,512]{1,0:T(8,128)(2,1)}, bf16[672,512]{1,0:T(8,128)(2,1)S(1)}, u32[]{:S(2)}, u32[]{:S(2)}) %collective-permute-start.23) | collective-permute-done | bytes 688160 | tf_op jit(solution)/shard_map/ppermute | solution.py:34
  157.5 1.2 shard_map.113
  (94 shorter events, 13.2 us)
Async XLA Ops:
  7.2 143.1 %reduce-scatter.2.cloned.1.call-start = ((), (), s32[]{:S(2)}) async-start(), calls=%async_computation.1 | async-start | bytes 3096576 | tf_op jit(solution)/shard_map/reduce_scatter | solution.py:458
  7.2 20.0 %collective-permute-start.3 = (bf16[672,512]{1,0:T(8,128)(2,1)}, bf16[672,512]{1,0:T(8,128)(2,1)}, u32[]{:S(2)}, u32[]{:S(2)}) collective-permute-start(bf16[672,512]{1,0:T(8,128)(2,1)} %bitcast.91), channel_id=1, source_target_pairs={{0,4},{1,5},{2,6},{3,7},{4,0},{5,1},{6,2},{7,3},{8,12},{9,13},{10,... | collective-permute-start | bytes 2064392 | tf_op jit(solution)/shard_map/ppermute | solution.py:38
  9.4 17.7 %collective-permute-start.1 = (bf16[672,512]{1,0:T(8,128)(2,1)}, bf16[672,512]{1,0:T(8,128)(2,1)S(1)}, u32[]{:S(2)}, u32[]{:S(2)}) collective-permute-start(bf16[672,512]{1,0:T(8,128)(2,1)} %bitcast.92), channel_id=1, source_target_pairs={{0,3},{1,0},{2,1},{3,2},{4,7},{5,4},{6,5},{7,6},{8,11},{9,8},{10,9... | collective-permute-start | bytes 2064392 | tf_op jit(solution)/shard_map/ppermute | solution.py:34
  12.4 18.0 %collective-permute-start = (bf16[672,512]{1,0:T(8,128)(2,1)}, bf16[672,512]{1,0:T(8,128)(2,1)S(1)}, u32[]{:S(2)}, u32[]{:S(2)}) collective-permute-start(bf16[672,512]{1,0:T(8,128)(2,1)} %bitcast.93), channel_id=1, source_target_pairs={{0,1},{1,2},{2,3},{3,0},{4,5},{5,6},{6,7},{7,4},{8,9},{9,10},{10,1... | collective-permute-start | bytes 2064392 | tf_op jit(solution)/shard_map/ppermute | solution.py:34
  15.8 2.4 %copy-start.9 = (bf16[5376,512]{1,0:T(8,128)(2,1)}, bf16[5376,512]{1,0:T(8,128)(2,1)S(1)}, u32[]{:S(2)}) copy-start(bf16[5376,512]{1,0:T(8,128)(2,1)S(1)} %pad_maximum_fusion) | copy-start | bytes 16515076
  28.3 7.1 %copy-start.13 = (bf16[512,672]{0,1:T(8,128)(2,1)S(1)}, bf16[512,672]{0,1:T(8,128)(2,1)}, u32[]{:S(2)}) copy-start(bf16[512,672]{0,1:T(8,128)(2,1)} %param.7) | copy-start | bytes 2064388
  30.5 7.7 %slice-start = ((s8[5505024]{0:T(1024)(128)(4,1)}), s8[4194304]{0:T(1024)(128)(4,1)S(1)}, s32[]{:S(2)}) async-start(s8[5505024]{0:T(1024)(128)(4,1)} %bitcast.76), calls=%async_computation.2 | async-start | bytes 8388608
  30.7 18.1 %collective-permute-start.6 = (bf16[672,512]{1,0:T(8,128)(2,1)S(1)}, bf16[672,512]{1,0:T(8,128)(2,1)S(1)}, u32[]{:S(2)}, u32[]{:S(2)}) collective-permute-start(bf16[672,512]{1,0:T(8,128)(2,1)S(1)} %get-tuple-element.98), channel_id=1, source_target_pairs={{0,1},{1,2},{2,3},{3,0},{4,5},{5,6},{6,7},{7,4},{8,9},{9,10},{10,1... | collective-permute-start | bytes 2064392 | tf_op jit(solution)/shard_map/ppermute | solution.py:34
  30.8 17.3 %collective-permute-start.2 = (bf16[672,512]{1,0:T(8,128)(2,1)S(1)}, bf16[672,512]{1,0:T(8,128)(2,1)S(1)}, u32[]{:S(2)}, u32[]{:S(2)}) collective-permute-start(bf16[672,512]{1,0:T(8,128)(2,1)S(1)} %get-tuple-element.99), channel_id=1, source_target_pairs={{0,4},{1,5},{2,6},{3,7},{4,0},{5,1},{6,2},{7,3},{8,12},{9,13},{10,... | collective-permute-start | bytes 2064392 | tf_op jit(solution)/shard_map/ppermute | solution.py:38
  32.3 15.8 %collective-permute-start.7 = (bf16[672,512]{1,0:T(8,128)(2,1)S(1)}, bf16[672,512]{1,0:T(8,128)(2,1)S(1)}, u32[]{:S(2)}, u32[]{:S(2)}) collective-permute-start(bf16[672,512]{1,0:T(8,128)(2,1)S(1)} %get-tuple-element.100), channel_id=1, source_target_pairs={{0,3},{1,0},{2,1},{3,2},{4,7},{5,4},{6,5},{7,6},{8,11},{9,8},{10,9... | collective-permute-start | bytes 2064392 | tf_op jit(solution)/shard_map/ppermute | solution.py:34
  35.4 2.8 %slice-start.1 = ((s8[5505024]{0:T(1024)(128)(4,1)}), s8[1310720]{0:T(1024)(128)(4,1)S(1)}, s32[]{:S(2)}) async-start(s8[5505024]{0:T(1024)(128)(4,1)} %bitcast.76), calls=%async_computation.3 | async-start | bytes 2621440
  36.9 2.0 %copy-start.11 = (bf16[4,2,2,168,512]{4,3,2,1,0:T(8,128)(2,1)}, bf16[4,2,2,168,512]{4,3,2,1,0:T(8,128)(2,1)S(1)}, u32[]{:S(2)}) copy-start(bf16[4,2,2,168,512]{4,3,2,1,0:T(8,128)(2,1)S(1)} %pad_maximum_fusion.1.x_ref) | copy-start | bytes 8257540
  38.2 29.6 %collective-permute-start.10 = (bf16[4,2,168,512]{3,2,1,0:T(8,128)(2,1)}, bf16[4,2,168,512]{3,2,1,0:T(8,128)(2,1)}, u32[]{:S(2)}, u32[]{:S(2)}) collective-permute-start(bf16[4,2,168,512]{3,2,1,0:T(8,128)(2,1)} %dynamic-slice_bitcast_fusion), channel_id=1, source_target_pairs={{0,8},{8,0},{16,24},{24,16},{32,40},{40,32},{48,56},{56,48},{64,72... | collective-permute-start | bytes 4128776 | tf_op jit(solution)/shard_map/ppermute | solution.py:42
  49.6 8.9 %collective-permute-start.4 = (bf16[336,512]{1,0:T(8,128)(2,1)S(1)}, bf16[336,512]{1,0:T(8,128)(2,1)S(1)}, u32[]{:S(2)}, u32[]{:S(2)}) collective-permute-start(bf16[336,512]{1,0:T(8,128)(2,1)S(1)} %get-tuple-element.47), channel_id=1, source_target_pairs={{0,1},{1,2},{2,3},{3,0},{4,5},{5,6},{6,7},{7,4},{8,9},{9,10},{10,1... | collective-permute-start | bytes 1032200 | tf_op jit(solution)/shard_map/ppermute | solution.py:34
  50.4 8.1 %collective-permute-start.5 = (bf16[336,512]{1,0:T(8,128)(2,1)S(1)}, bf16[336,512]{1,0:T(8,128)(2,1)S(1)}, u32[]{:S(2)}, u32[]{:S(2)}) collective-permute-start(bf16[336,512]{1,0:T(8,128)(2,1)S(1)} %get-tuple-element.48), channel_id=1, source_target_pairs={{0,3},{1,0},{2,1},{3,2},{4,7},{5,4},{6,5},{7,6},{8,11},{9,8},{10,9... | collective-permute-start | bytes 1032200 | tf_op jit(solution)/shard_map/ppermute | solution.py:34
  53.6 1.8 %copy-start.12 = (bf16[3,2,2,168,512]{4,3,2,1,0:T(8,128)(2,1)}, bf16[3,2,2,168,512]{4,3,2,1,0:T(8,128)(2,1)S(1)}, u32[]{:S(2)}) copy-start(bf16[3,2,2,168,512]{4,3,2,1,0:T(8,128)(2,1)S(1)} %pad_maximum_fusion.2.xb_ref) | copy-start | bytes 6193156
  54.9 4.0 %copy-start.15 = (f32[128]{0:T(128)S(1)}, f32[128]{0:T(128)}, u32[]{:S(2)}) copy-start(f32[128]{0:T(128)} %param.11) | copy-start | bytes 1540
  54.9 4.1 %copy-start.16 = (f32[128]{0:T(128)S(1)}, f32[128]{0:T(128)}, u32[]{:S(2)}) copy-start(f32[128]{0:T(128)} %param.12) | copy-start | bytes 1540
  58.6 14.0 %copy-start = (bf16[672,512]{1,0:T(8,128)(2,1)}, bf16[672,512]{1,0:T(8,128)(2,1)S(1)}, u32[]{:S(2)}) copy-start(bf16[672,512]{1,0:T(8,128)(2,1)S(1)} %pad_maximum_fusion.6.last_ref) | copy-start | bytes 2064388
  58.6 30.1 %collective-permute-start.13 = (bf16[3,2,168,512]{3,2,1,0:T(8,128)(2,1)}, bf16[3,2,168,512]{3,2,1,0:T(8,128)(2,1)}, u32[]{:S(2)}, u32[]{:S(2)}) collective-permute-start(bf16[3,2,168,512]{3,2,1,0:T(8,128)(2,1)} %dynamic-slice_bitcast_fusion.1), channel_id=1, source_target_pairs={{0,8},{8,0},{16,24},{24,16},{32,40},{40,32},{48,56},{56,48},{64,72... | collective-permute-start | bytes 3096584 | tf_op jit(solution)/shard_map/ppermute | solution.py:42
  59.9 15.5 %collective-permute-start.9 = (bf16[256,512]{1,0:T(8,128)(2,1)S(1)}, bf16[256,512]{1,0:T(8,128)(2,1)S(1)}, u32[]{:S(2)}, u32[]{:S(2)}) collective-permute-start(bf16[256,512]{1,0:T(8,128)(2,1)S(1)} %get-tuple-element.53.own_ref), channel_id=1, source_target_pairs={{0,16},{8,24},{16,32},{24,40},{32,48},{40,56},{48,64},{56,72},{64,... | collective-permute-start | bytes 786440 | tf_op jit(solution)/shard_map/ppermute | solution.py:53
  63.7 14.3 %collective-permute-start.8 = (bf16[256,512]{1,0:T(8,128)(2,1)S(1)}, bf16[256,512]{1,0:T(8,128)(2,1)S(1)}, u32[]{:S(2)}, u32[]{:S(2)}) collective-permute-start(bf16[256,512]{1,0:T(8,128)(2,1)S(1)} %get-tuple-element.53.own_ref), channel_id=1, source_target_pairs={{0,8},{8,16},{16,24},{24,32},{32,40},{40,48},{48,56},{56,64},{64,7... | collective-permute-start | bytes 786440 | tf_op jit(solution)/shard_map/ppermute | solution.py:53
  65.9 12.1 %copy-start.8 = (bf16[512,256]{1,0:T(8,128)(2,1)S(1)}, bf16[512,256]{1,0:T(8,128)(2,1)}, u32[]{:S(2)}) copy-start(bf16[512,256]{1,0:T(8,128)(2,1)} %go_ref.1) | copy-start | bytes 786436
  65.9 22.7 %collective-permute-start.14 = (bf16[1,2,168,512]{3,2,1,0:T(8,128)(2,1)S(1)}, bf16[1,2,168,512]{3,2,1,0:T(8,128)(2,1)S(1)}, u32[]{:S(2)}, u32[]{:S(2)}) collective-permute-start(bf16[1,2,168,512]{3,2,1,0:T(8,128)(2,1)S(1)} %dynamic-slice_bitcast_fusion.3), channel_id=1, source_target_pairs={{0,8},{8,0},{16,24},{24,16},{32,40},{40,32},{48,56},{56,48},{64,72... | collective-permute-start | bytes 1032200 | tf_op jit(solution)/shard_map/ppermute | solution.py:42
  83.0 11.2 %collective-permute-start.11 = (bf16[2,512,128]{2,1,0:T(8,128)(2,1)S(1)}, bf16[2,512,128]{2,1,0:T(8,128)(2,1)S(1)}, u32[]{:S(2)}, u32[]{:S(2)}) collective-permute-start(bf16[2,512,128]{2,1,0:T(8,128)(2,1)S(1)} %get-tuple-element.58), channel_id=1, source_target_pairs={{8,0},{16,8},{24,16},{32,24},{40,32},{48,40},{56,48},{64,56},{72,6... | collective-permute-start | bytes 786440 | tf_op jit(solution)/shard_map/ppermute | solution.py:53
  85.0 10.6 %collective-permute-start.12 = (bf16[2,512,128]{2,1,0:T(8,128)(2,1)S(1)}, bf16[2,512,128]{2,1,0:T(8,128)(2,1)S(1)}, u32[]{:S(2)}, u32[]{:S(2)}) collective-permute-start(bf16[2,512,128]{2,1,0:T(8,128)(2,1)S(1)} %get-tuple-element.59), channel_id=1, source_target_pairs={{16,0},{24,8},{32,16},{40,24},{48,32},{56,40},{64,48},{72,56},{80,... | collective-permute-start | bytes 786440 | tf_op jit(solution)/shard_map/ppermute | solution.py:53
  88.6 0.7 copy-start.14
  95.8 0.8 copy-start.1
  95.8 4.6 %copy-start.10 = (bf16[4,2,2,168,1024]{4,3,2,1,0:T(8,128)(2,1)S(1)}, bf16[4,2,2,168,1024]{4,3,2,1,0:T(8,128)(2,1)}, u32[]{:S(2)}) copy-start(bf16[4,2,2,168,1024]{4,3,2,1,0:T(8,128)(2,1)} %shard_map.105) | copy-start | bytes 16515076
  95.9 4.6 %collective-permute-start.15 = (bf16[512,512]{1,0:T(8,128)(2,1)S(1)}, bf16[512,512]{1,0:T(8,128)(2,1)S(1)}, u32[]{:S(2)}, u32[]{:S(2)}) collective-permute-start(bf16[512,512]{1,0:T(8,128)(2,1)S(1)} %shard_map.106.d_ref), channel_id=1, source_target_pairs={{0,8},{8,0},{16,24},{24,16},{32,40},{40,32},{48,56},{56,48},{64,72... | collective-permute-start | bytes 1572872 | tf_op jit(solution)/shard_map/ppermute | solution.py:42
  105.9 1.0 copy-start.18
  105.9 2.4 %copy-start.17 = (bf16[336,512]{1,0:T(8,128)(2,1)S(1)}, bf16[336,512]{1,0:T(8,128)(2,1)}, u32[]{:S(2)}) copy-start(bf16[336,512]{1,0:T(8,128)(2,1)} %get-tuple-element.69) | copy-start | bytes 1032196
  106.9 11.0 %collective-permute-start.20 = (bf16[336,512]{1,0:T(8,128)(2,1)S(1)}, bf16[336,512]{1,0:T(8,128)(2,1)S(1)}, u32[]{:S(2)}, u32[]{:S(2)}) collective-permute-start(bf16[336,512]{1,0:T(8,128)(2,1)S(1)} %copy-done.18), channel_id=1, source_target_pairs={{0,1},{1,2},{2,3},{3,0},{4,5},{5,6},{6,7},{7,4},{8,9},{9,10},{10,1... | collective-permute-start | bytes 1032200 | tf_op jit(solution)/shard_map/ppermute | solution.py:34
  108.3 9.6 %collective-permute-start.19 = (bf16[336,512]{1,0:T(8,128)(2,1)S(1)}, bf16[336,512]{1,0:T(8,128)(2,1)S(1)}, u32[]{:S(2)}, u32[]{:S(2)}) collective-permute-start(bf16[336,512]{1,0:T(8,128)(2,1)S(1)} %copy-done.17), channel_id=1, source_target_pairs={{0,3},{1,0},{2,1},{3,2},{4,7},{5,4},{6,5},{7,6},{8,11},{9,8},{10,9... | collective-permute-start | bytes 1032200 | tf_op jit(solution)/shard_map/ppermute | solution.py:34
  115.7 16.9 %collective-permute-start.16 = (bf16[672,512]{1,0:T(8,128)(2,1)}, bf16[672,512]{1,0:T(8,128)(2,1)S(1)}, u32[]{:S(2)}, u32[]{:S(2)}) collective-permute-start(bf16[672,512]{1,0:T(8,128)(2,1)} %get-tuple-element.73), channel_id=1, source_target_pairs={{0,3},{1,0},{2,1},{3,2},{4,7},{5,4},{6,5},{7,6},{8,11},{9,8},{10,9... | collective-permute-start | bytes 2064392 | tf_op jit(solution)/shard_map/ppermute | solution.py:34
  117.6 17.6 %collective-permute-start.17 = (bf16[672,512]{1,0:T(8,128)(2,1)}, bf16[672,512]{1,0:T(8,128)(2,1)S(1)}, u32[]{:S(2)}, u32[]{:S(2)}) collective-permute-start(bf16[672,512]{1,0:T(8,128)(2,1)} %get-tuple-element.74), channel_id=1, source_target_pairs={{0,1},{1,2},{2,3},{3,0},{4,5},{5,6},{6,7},{7,4},{8,9},{9,10},{10,1... | collective-permute-start | bytes 2064392 | tf_op jit(solution)/shard_map/ppermute | solution.py:34
  117.9 1.1 copy-start.6
  119.2 19.4 %collective-permute-start.21 = (bf16[672,512]{1,0:T(8,128)(2,1)S(1)}, bf16[672,512]{1,0:T(8,128)(2,1)S(1)}, u32[]{:S(2)}, u32[]{:S(2)}) collective-permute-start(bf16[672,512]{1,0:T(8,128)(2,1)S(1)} %shard_map.111), channel_id=1, source_target_pairs={{0,4},{1,5},{2,6},{3,7},{4,0},{5,1},{6,2},{7,3},{8,12},{9,13},{10,... | collective-permute-start | bytes 2064392 | tf_op jit(solution)/shard_map/ppermute | solution.py:38
  127.7 10.8 %copy-start.4 = (bf16[672,512]{1,0:T(8,128)(2,1)S(1)}, bf16[672,512]{1,0:T(8,128)(2,1)}, u32[]{:S(2)}) copy-start(bf16[672,512]{1,0:T(8,128)(2,1)} %get-tuple-element.81.below_ref) | copy-start | bytes 2064388
  127.7 10.8 %copy-start.5 = (bf16[672,512]{1,0:T(8,128)(2,1)S(1)}, bf16[672,512]{1,0:T(8,128)(2,1)}, u32[]{:S(2)}) copy-start(bf16[672,512]{1,0:T(8,128)(2,1)} %get-tuple-element.82.above_ref) | copy-start | bytes 2064388
  135.2 1.1 copy-start.7
  136.5 21.0 %copy-start.3 = (bf16[672,512]{1,0:T(8,128)(2,1)S(1)}, bf16[672,512]{1,0:T(8,128)(2,1)}, u32[]{:S(2)}) copy-start(bf16[672,512]{1,0:T(8,128)(2,1)} %get-tuple-element.67.mine_ref) | copy-start | bytes 2064388
  136.5 18.8 %collective-permute-start.18 = (bf16[672,512]{1,0:T(8,128)(2,1)S(1)}, bf16[672,512]{1,0:T(8,128)(2,1)S(1)}, u32[]{:S(2)}, u32[]{:S(2)}) collective-permute-start(bf16[672,512]{1,0:T(8,128)(2,1)S(1)} %shard_map.110), channel_id=1, source_target_pairs={{0,4},{1,5},{2,6},{3,7},{4,0},{5,1},{6,2},{7,3},{8,12},{9,13},{10,... | collective-permute-start | bytes 2064392 | tf_op jit(solution)/shard_map/ppermute | solution.py:38
  139.8 15.5 %collective-permute-start.22 = (bf16[672,512]{1,0:T(8,128)(2,1)}, bf16[672,512]{1,0:T(8,128)(2,1)S(1)}, u32[]{:S(2)}, u32[]{:S(2)}) collective-permute-start(bf16[672,512]{1,0:T(8,128)(2,1)} %get-tuple-element.85), channel_id=1, source_target_pairs={{0,3},{1,0},{2,1},{3,2},{4,7},{5,4},{6,5},{7,6},{8,11},{9,8},{10,9... | collective-permute-start | bytes 2064392 | tf_op jit(solution)/shard_map/ppermute | solution.py:34
  141.3 16.2 %collective-permute-start.23 = (bf16[672,512]{1,0:T(8,128)(2,1)}, bf16[672,512]{1,0:T(8,128)(2,1)S(1)}, u32[]{:S(2)}, u32[]{:S(2)}) collective-permute-start(bf16[672,512]{1,0:T(8,128)(2,1)} %get-tuple-element.86), channel_id=1, source_target_pairs={{0,1},{1,2},{2,3},{3,0},{4,5},{5,6},{6,7},{7,4},{8,9},{9,10},{10,1... | collective-permute-start | bytes 2064392 | tf_op jit(solution)/shard_map/ppermute | solution.py:34
  150.3 8.4 %copy-start.2 = (bf16[1,336,512]{2,1,0:T(8,128)(2,1)S(1)}, bf16[1,336,512]{2,1,0:T(8,128)(2,1)}, u32[]{:S(2)}) copy-start(bf16[1,336,512]{2,1,0:T(8,128)(2,1)} %reduce-scatter.2.cloned.1.call-done) | copy-start | bytes 1032196
  151.3 7.4 %collective-permute-start.24 = (bf16[168,512]{1,0:T(8,128)(2,1)S(1)}, bf16[168,512]{1,0:T(8,128)(2,1)S(1)}, u32[]{:S(2)}, u32[]{:S(2)}) collective-permute-start(bf16[168,512]{1,0:T(8,128)(2,1)S(1)} %slice_bitcast_fusion), channel_id=1, source_target_pairs={{0,128},{8,136},{16,144},{24,152},{32,160},{40,168},{48,176},{56,1... | collective-permute-start | bytes 516104 | tf_op jit(solution)/shard_map/ppermute | solution.py:47
Sparse Core Ops, SparseCore 0:
  106.1 44.1 reduce-scatter.1
